TPU v7x, 32 devices: a whole 2x2x4 slice. The times are simulated.
32 devices in a mesh: section: 2 (over core), ctx: 4 (over y, x), fsdp: 4 (over z).
Axes of the slice: x: 2, y: 2, z: 4, core: 2. Of those that a mesh axis runs over, the one named last changes fastest.
Arguments:
- inputs: bfloat16 [2, 4, 1024, 896], P(None, 'fsdp', 'ctx'), may hold values from -6 to 6
- attend_gain: bfloat16 [2, 896], P('section', 'fsdp'), may hold values from 0.5 to 1.5
- projections: bfloat16 [2, 896, 1152], P('section', 'fsdp'), may hold values from -0.1875 to 0.1875
- biases: bfloat16 [2, 1152], P('section', 'fsdp'), may hold values from -3 to 3
- output_weight: bfloat16 [2, 896, 896], P('section', 'fsdp'), may hold values from -6 to 6
- mixer_gain: bfloat16 [2, 896], P('section', 'fsdp'), may hold values from 0.5 to 1.5
- expand_weight: bfloat16 [2, 896, 9728], P('section', 'fsdp'), may hold values from -0.1875 to 0.1875
- down_weight: bfloat16 [2, 4864, 896], P('section', 'fsdp'), may hold values from -0.078125 to 0.078125
- positions: int32 [2, 4, 1024], P(None, 'fsdp'), may hold values from 0 to 1023, as said below
- cotangent: bfloat16 [2, 4, 1024, 896], P(None, 'fsdp', 'ctx'), may hold values from -6 to 6
Outputs:
- activations: bfloat16 [2, 2, 4, 1024, 896], P('section', None, 'fsdp', 'ctx')
- input_grads: float32 [2, 2, 4, 1024, 896], P('section', None, 'fsdp', 'ctx')
- grad_attend: float32 [2, 896], P('section', 'fsdp')
- grad_projections: float32 [2, 896, 1152], P('section', 'fsdp')
- grad_biases: float32 [2, 1024], P('section', 'fsdp')
- grad_value_bias: float32 [2, 128], P('section', 'fsdp')
- grad_output: float32 [2, 896, 896], P('section', 'fsdp')
- grad_mixer: float32 [2, 896], P('section', 'fsdp')
- grad_expand: float32 [2, 896, 9728], P('section', 'fsdp')
- grad_down: float32 [2, 4864, 896], P('section', 'fsdp')
Inputs may be any that keep to these rules, and one draw needn't show every extreme that they name: For each sequence, positions is a permutation of 0 to 1023 made of runs of 128 consecutive numbers, each run starting at a multiple of 128 and stored in an aligned group of 128 rows.
All inputs are finite; a program needn't handle non-finite values.
Results may differ from a plain program's by a relative error of at most 0.017.
Values may be sent and summed in bfloat16 or wider, within the bound.
A program may use at most 384 MiB of HBM per device.

v0:
```python
import jax
import jax.numpy as jnp
from jax import lax
from jax.sharding import PartitionSpec as P

HEAD_DIM = 64


epsilon = 1e-06
theta_base = 1000000.0
masked_value = -1e30


def from_behind(block, axis, distance):
    devices = range(lax.axis_size(axis))
    route = [(i - distance, i) for i in devices if i - distance in devices]
    return lax.ppermute(block, axis, route)


def normalize_rows(values, gain_row):
    norm_scale = lax.rsqrt(jnp.mean(values * values, axis=-1, keepdims=True) + epsilon)
    return (values * norm_scale * gain_row, norm_scale)


def norm_back(upstream, values, norm_scale, gain_row):
    scaled = upstream * gain_row
    gain_grad = jnp.sum(upstream * values * norm_scale, axis=0)
    scale_cubed = norm_scale * norm_scale * norm_scale
    values_grad = norm_scale * scaled - values * scale_cubed * jnp.mean(
        scaled * values, axis=-1, keepdims=True
    )
    return (values_grad, gain_grad)


def tables(positions_row):
    half_dim = HEAD_DIM // 2
    frequency = theta_base ** (-(jnp.arange(half_dim, dtype=jnp.float32) * 2.0) / HEAD_DIM)
    angles = positions_row.astype(jnp.float32)[:, None] * frequency[None, :]
    angles = jnp.concatenate([angles, angles], axis=-1)
    return (jnp.cos(angles)[:, None, :], jnp.sin(angles)[:, None, :])


def turned(values):
    half_dim = values.shape[-1] // 2
    return jnp.concatenate([-values[..., half_dim:], values[..., :half_dim]], axis=-1)


def rotate(values, cosine, sine):
    return values * cosine + turned(values) * sine


def unrotate(grads, cosine, sine):
    return grads * cosine - turned(grads * sine)


def fetch_layer(first_gain, project, offset, out_weight, second_gain, expand, shrink):
    gathered = (
        lax.all_gather(first_gain, "fsdp", axis=1, tiled=True),
        lax.all_gather(project, "fsdp", axis=1, tiled=True),
        lax.all_gather(offset, "fsdp", axis=1, tiled=True),
        lax.all_gather(out_weight, "fsdp", axis=1, tiled=True),
        lax.all_gather(second_gain, "fsdp", axis=1, tiled=True),
        lax.all_gather(expand, "fsdp", axis=1, tiled=True),
        lax.all_gather(shrink, "fsdp", axis=1, tiled=True),
    )
    return tuple((piece[0] for piece in gathered))


def reorder(gradient, ctx_count, fsdp_count):
    part_rows = gradient.shape[0] // (ctx_count * fsdp_count)
    shaped = gradient.reshape((fsdp_count, ctx_count, part_rows) + gradient.shape[1:])
    return jnp.swapaxes(shaped, 0, 1).reshape(gradient.shape)


def head_scores(queries, every_kv, head_index, group_size, key_positions, query_positions):
    grouped = queries[:, head_index * group_size : (head_index + 1) * group_size, :]
    key_block = every_kv[:, head_index * HEAD_DIM : (head_index + 1) * HEAD_DIM]
    scores = jnp.einsum(
        "qgd,kd->gqk", grouped, key_block, preferred_element_type=jnp.float32
    ) * HEAD_DIM ** (-0.5)
    allowed = key_positions[None, None, :] <= query_positions[None, :, None]
    return (jnp.where(allowed, scores, masked_value), grouped, key_block)


def forward(current, hidden, cosine, sine, key_positions, query_positions):
    first_gain, project, offset, out_weight, second_gain, expand, shrink = current
    row_count, model_width = hidden.shape
    pair_width = (project.shape[1] - model_width) // 2
    head_count = model_width // HEAD_DIM
    kv_count = pair_width // HEAD_DIM
    group_size = head_count // kv_count
    hidden_units = expand.shape[1] // 2
    normed, first_scale = normalize_rows(hidden, first_gain.astype(jnp.float32))
    normed = normed.astype(jnp.bfloat16)
    combined = jnp.dot(normed, project, preferred_element_type=jnp.float32) + offset.astype(
        jnp.float32
    )
    queries = rotate(
        combined[:, :model_width].reshape(row_count, head_count, HEAD_DIM), cosine, sine
    ).astype(jnp.bfloat16)
    key_rows = rotate(
        combined[:, model_width : model_width + pair_width].reshape(row_count, kv_count, HEAD_DIM),
        cosine,
        sine,
    )
    local_kv = jnp.concatenate(
        [key_rows.reshape(row_count, pair_width), combined[:, model_width + pair_width :]], axis=1
    ).astype(jnp.bfloat16)
    every_kv = lax.all_gather(local_kv, "ctx", axis=0, tiled=True)
    contexts = []
    row_maxes = []
    row_totals = []
    for head_index in range(kv_count):
        masked, grouped, key_block = head_scores(
            queries, every_kv, head_index, group_size, key_positions, query_positions
        )
        row_max = jnp.max(masked, axis=-1, keepdims=True)
        exponent = jnp.exp(masked - row_max)
        row_total = jnp.sum(exponent, axis=-1, keepdims=True)
        attention_low = (exponent / row_total).astype(jnp.bfloat16)
        value_block = every_kv[
            :, pair_width + head_index * HEAD_DIM : pair_width + (head_index + 1) * HEAD_DIM
        ]
        contexts.append(
            jnp.einsum(
                "gqk,kd->qgd", attention_low, value_block, preferred_element_type=jnp.float32
            )
        )
        row_maxes.append(row_max)
        row_totals.append(row_total)
    context = jnp.concatenate(contexts, axis=1).reshape(row_count, model_width).astype(jnp.bfloat16)
    middle = hidden + jnp.dot(context, out_weight, preferred_element_type=jnp.float32)
    second_normed, second_scale = normalize_rows(middle, second_gain.astype(jnp.float32))
    second_normed = second_normed.astype(jnp.bfloat16)
    widened = jnp.dot(second_normed, expand, preferred_element_type=jnp.float32)
    activated = (jax.nn.silu(widened[:, :hidden_units]) * widened[:, hidden_units:]).astype(
        jnp.bfloat16
    )
    output = middle + jnp.dot(activated, shrink, preferred_element_type=jnp.float32)
    stored = (
        hidden,
        first_scale,
        normed,
        queries,
        every_kv,
        jnp.stack(row_maxes),
        jnp.stack(row_totals),
        context,
        middle,
        second_scale,
        second_normed,
        widened,
        activated,
    )
    return (output, stored)


def backward(current, stored, grad_out, key_positions, query_positions, cosine, sine):
    first_gain, project, offset, out_weight, second_gain, expand, shrink = current
    (
        hidden,
        first_scale,
        normed,
        queries,
        every_kv,
        row_maxes,
        row_totals,
        context,
        middle,
        second_scale,
        second_normed,
        widened,
        activated,
    ) = stored
    row_count, model_width = hidden.shape
    pair_width = every_kv.shape[1] // 2
    head_count = model_width // HEAD_DIM
    kv_count = pair_width // HEAD_DIM
    group_size = head_count // kv_count
    hidden_units = expand.shape[1] // 2
    upstream = grad_out.astype(jnp.float32)
    down_grad = jnp.einsum("rf,rd->fd", activated, grad_out, preferred_element_type=jnp.float32)
    spread_grad = jnp.einsum("rd,fd->rf", grad_out, shrink, preferred_element_type=jnp.float32)
    gate_part = widened[:, :hidden_units]
    up_part = widened[:, hidden_units:]
    sigmoid_gate = jax.nn.sigmoid(gate_part)
    gate_grad = spread_grad * up_part * sigmoid_gate * (1.0 + gate_part * (1.0 - sigmoid_gate))
    up_grad = spread_grad * (gate_part * sigmoid_gate)
    widened_grad = jnp.concatenate([gate_grad, up_grad], axis=1).astype(jnp.bfloat16)
    expand_grad = jnp.einsum(
        "rd,rf->df", second_normed, widened_grad, preferred_element_type=jnp.float32
    )
    second_normed_grad = jnp.einsum(
        "rf,df->rd", widened_grad, expand, preferred_element_type=jnp.float32
    )
    middle_part, second_grad = norm_back(
        second_normed_grad, middle, second_scale, second_gain.astype(jnp.float32)
    )
    middle_grad = upstream + middle_part
    middle_low = middle_grad.astype(jnp.bfloat16)
    output_grad = jnp.einsum("rd,re->de", context, middle_low, preferred_element_type=jnp.float32)
    context_grad = jnp.einsum(
        "re,de->rd", middle_low, out_weight, preferred_element_type=jnp.float32
    )
    context_grad = context_grad.astype(jnp.bfloat16).reshape(row_count, head_count, HEAD_DIM)
    query_grads = []
    key_grads = []
    value_grads = []
    for head_index in range(kv_count):
        masked, grouped, key_block = head_scores(
            queries, every_kv, head_index, group_size, key_positions, query_positions
        )
        attention_full = jnp.exp(masked - row_maxes[head_index]) / row_totals[head_index]
        attention_low = attention_full.astype(jnp.bfloat16)
        value_block = every_kv[
            :, pair_width + head_index * HEAD_DIM : pair_width + (head_index + 1) * HEAD_DIM
        ]
        context_block = context_grad[:, head_index * group_size : (head_index + 1) * group_size, :]
        probs_grad = jnp.einsum(
            "qgd,kd->gqk", context_block, value_block, preferred_element_type=jnp.float32
        )
        row_delta = jnp.sum(attention_full * probs_grad, axis=-1, keepdims=True)
        scores_grad = (attention_full * (probs_grad - row_delta)).astype(jnp.bfloat16)
        query_grads.append(
            jnp.einsum("gqk,kd->qgd", scores_grad, key_block, preferred_element_type=jnp.float32)
            * HEAD_DIM ** (-0.5)
        )
        key_grads.append(
            jnp.einsum("gqk,qgd->kd", scores_grad, grouped, preferred_element_type=jnp.float32)
            * HEAD_DIM ** (-0.5)
        )
        value_grads.append(
            jnp.einsum(
                "gqk,qgd->kd", attention_low, context_block, preferred_element_type=jnp.float32
            )
        )
    every_grad = jnp.concatenate(key_grads + value_grads, axis=1)
    own_grad = lax.psum_scatter(
        every_grad.astype(jnp.bfloat16), "ctx", scatter_dimension=0, tiled=True
    ).astype(jnp.float32)
    query_turned = unrotate(jnp.concatenate(query_grads, axis=1), cosine, sine).reshape(
        row_count, model_width
    )
    key_turned = unrotate(
        own_grad[:, :pair_width].reshape(row_count, kv_count, HEAD_DIM), cosine, sine
    ).reshape(row_count, pair_width)
    combined_grad = jnp.concatenate(
        [query_turned, key_turned, own_grad[:, pair_width:]], axis=1
    ).astype(jnp.bfloat16)
    project_grad = jnp.einsum(
        "rd,rf->df", normed, combined_grad, preferred_element_type=jnp.float32
    )
    offset_grad = jnp.sum(combined_grad.astype(jnp.float32), axis=0)
    normed_grad = jnp.einsum(
        "rf,df->rd", combined_grad, project, preferred_element_type=jnp.float32
    )
    hidden_part, first_grad = norm_back(
        normed_grad, hidden, first_scale, first_gain.astype(jnp.float32)
    )
    return (
        middle_grad + hidden_part,
        (first_grad, project_grad, offset_grad, output_grad, second_grad, expand_grad, down_grad),
    )


def per_device(
    inputs,
    attend_gain,
    projections,
    biases,
    output_weight,
    mixer_gain,
    expand_weight,
    down_weight,
    positions,
    cotangent,
):
    micro_count = inputs.shape[0]
    row_count = inputs.shape[2]
    model_width = inputs.shape[3]
    is_first = lax.axis_index("section") == 0
    offset_rows = lax.axis_index("ctx") * row_count
    ctx_count = lax.axis_size("ctx")
    fsdp_count = lax.axis_size("fsdp")
    incoming = jnp.zeros((row_count, model_width), jnp.bfloat16)
    stashed = []
    sent_list = []
    for moment in range(micro_count + 1):
        early_index = min(moment, micro_count - 1)
        late_index = max(moment - 1, 0)
        key_positions = jnp.where(is_first, positions[early_index, 0], positions[late_index, 0])
        query_positions = lax.dynamic_slice_in_dim(key_positions, offset_rows, row_count)
        cosine, sine = tables(query_positions)
        source = jnp.where(
            is_first, inputs[early_index, 0].astype(jnp.float32), incoming.astype(jnp.float32)
        )
        current = fetch_layer(
            attend_gain, projections, biases, output_weight, mixer_gain, expand_weight, down_weight
        )
        output, stored = forward(current, source, cosine, sine, key_positions, query_positions)
        sent = output.astype(jnp.bfloat16)
        sent_list.append(sent)
        stashed.append((stored, key_positions, query_positions, cosine, sine))
        if moment < micro_count:
            incoming = from_behind(sent, "section", 1)
    activations = jnp.stack(
        [
            jnp.where(is_first, sent_list[batch_index], sent_list[batch_index + 1])
            for batch_index in range(micro_count)
        ]
    )[None, :, None]
    grad_in = jnp.zeros((row_count, model_width), jnp.bfloat16)
    record = []
    totals = None
    pending = None
    for reverse in range(micro_count + 1):
        stored, key_positions, query_positions, cosine, sine = stashed[micro_count - reverse]
        if reverse < micro_count:
            upstream = cotangent[micro_count - 1 - reverse, 0]
        else:
            upstream = jnp.zeros_like(grad_in)
        grad_out = jnp.where(is_first, grad_in, upstream)
        current = fetch_layer(
            attend_gain, projections, biases, output_weight, mixer_gain, expand_weight, down_weight
        )
        hidden_grad, grads = backward(
            current, stored, grad_out, key_positions, query_positions, cosine, sine
        )
        if pending is None:
            pending = tuple(grads)
        else:
            pending = tuple((former + latter for former, latter in zip(pending, grads)))
        flush = reverse == micro_count
        if flush:
            (
                first_grad,
                project_grad,
                offset_grad,
                output_grad,
                second_grad,
                expand_grad,
                down_grad,
            ) = pending
            value_width = (offset_grad.shape[0] - model_width) // 2
            leading_offset = offset_grad[: model_width + value_width]
            value_offset = offset_grad[model_width + value_width :]
            portion = (
                lax.psum_scatter(
                    reorder(first_grad, ctx_count, fsdp_count),
                    ("ctx", "fsdp"),
                    scatter_dimension=0,
                    tiled=True,
                ),
                lax.psum_scatter(
                    reorder(project_grad, ctx_count, fsdp_count),
                    ("ctx", "fsdp"),
                    scatter_dimension=0,
                    tiled=True,
                ),
                lax.psum_scatter(
                    reorder(leading_offset, ctx_count, fsdp_count),
                    ("ctx", "fsdp"),
                    scatter_dimension=0,
                    tiled=True,
                ),
                lax.psum_scatter(
                    reorder(value_offset, ctx_count, fsdp_count),
                    ("ctx", "fsdp"),
                    scatter_dimension=0,
                    tiled=True,
                ),
                lax.psum_scatter(
                    reorder(output_grad, ctx_count, fsdp_count),
                    ("ctx", "fsdp"),
                    scatter_dimension=0,
                    tiled=True,
                ),
                lax.psum_scatter(
                    reorder(second_grad, ctx_count, fsdp_count),
                    ("ctx", "fsdp"),
                    scatter_dimension=0,
                    tiled=True,
                ),
                lax.psum_scatter(
                    reorder(expand_grad, ctx_count, fsdp_count),
                    ("ctx", "fsdp"),
                    scatter_dimension=0,
                    tiled=True,
                ),
                lax.psum_scatter(
                    reorder(down_grad, ctx_count, fsdp_count),
                    ("ctx", "fsdp"),
                    scatter_dimension=0,
                    tiled=True,
                ),
            )
            totals = tuple(portion)
            pending = None
        lowered = hidden_grad.astype(jnp.bfloat16)
        record.append(jnp.where(is_first, hidden_grad, lowered.astype(jnp.float32)))
        if reverse < micro_count:
            grad_in = from_behind(lowered, "section", -1)
    finished = (
        lax.all_gather(totals[0].astype(jnp.bfloat16), "ctx", axis=0, tiled=True).astype(
            jnp.float32
        ),
        lax.all_gather(totals[1].astype(jnp.bfloat16), "ctx", axis=0, tiled=True).astype(
            jnp.float32
        ),
        lax.all_gather(totals[2].astype(jnp.bfloat16), "ctx", axis=0, tiled=True).astype(
            jnp.float32
        ),
        lax.all_gather(totals[3].astype(jnp.bfloat16), "ctx", axis=0, tiled=True).astype(
            jnp.float32
        ),
        lax.all_gather(totals[4].astype(jnp.bfloat16), "ctx", axis=0, tiled=True).astype(
            jnp.float32
        ),
        lax.all_gather(totals[5].astype(jnp.bfloat16), "ctx", axis=0, tiled=True).astype(
            jnp.float32
        ),
        lax.all_gather(totals[6].astype(jnp.bfloat16), "ctx", axis=0, tiled=True).astype(
            jnp.float32
        ),
        lax.all_gather(totals[7].astype(jnp.bfloat16), "ctx", axis=0, tiled=True).astype(
            jnp.float32
        ),
    )
    input_grads = jnp.stack(
        [
            jnp.where(
                is_first, record[micro_count - batch_index], record[micro_count - 1 - batch_index]
            )
            for batch_index in range(micro_count)
        ]
    )[None, :, None]
    return (
        activations,
        input_grads,
        finished[0][None],
        finished[1][None],
        finished[2][None],
        finished[3][None],
        finished[4][None],
        finished[5][None],
        finished[6][None],
        finished[7][None],
    )


def solution(mesh):
    return jax.shard_map(
        per_device,
        mesh=mesh,
        in_specs=(
            P(None, "fsdp", "ctx", None),
            P("section", "fsdp"),
            P("section", "fsdp", None),
            P("section", "fsdp"),
            P("section", "fsdp", None),
            P("section", "fsdp"),
            P("section", "fsdp", None),
            P("section", "fsdp", None),
            P(None, "fsdp", None),
            P(None, "fsdp", "ctx", None),
        ),
        out_specs=(
            P("section", None, "fsdp", "ctx", None),
            P("section", None, "fsdp", "ctx", None),
            P("section", "fsdp"),
            P("section", "fsdp", None),
            P("section", "fsdp"),
            P("section", "fsdp"),
            P("section", "fsdp", None),
            P("section", "fsdp"),
            P("section", "fsdp", None),
            P("section", "fsdp", None),
        ),
        check_vma=False,
    )
```

profile of v0, /device:TPU:0, one launch (start us, length us, event | category | flops | bytes accessed | tf_op | source)
XLA Modules:
  0.0 2415.5 jit_solution(15032962237107220014)
XLA Ops:
  12.8 13.8 all-reduce.14
  30.6 27.3 %all-gather.7.cloned.1.call-done = bf16[1,896,1152]{2,1,0:T(8,128)(2,1)} async-done(((bf16[1,224,1152]{2,1,0:T(8,128)(2,1)}), bf16[1,896,1152]{2,1,0:T(8,128)(2,1)}) %all-gather.7.cloned.1.call-update) | async-done | bytes 2064400 | tf_op jit(solution)/shard_map/all_gather | solution.py:59
  63.0 10.0 all_gather.39
  98.5 296.7 %all-gather.11.cloned.1.call-done = bf16[1,896,9728]{2,1,0:T(8,128)(2,1)} async-done(((bf16[1,224,9728]{2,1,0:T(8,128)(2,1)}), bf16[1,896,9728]{2,1,0:T(8,128)(2,1)}) %all-gather.11.cloned.1.call-update) | async-done | bytes 17432592 | tf_op jit(solution)/shard_map/all_gather | solution.py:63
  395.2 9.3 fusion.16
  411.3 139.4 %all-gather.13.cloned.1.call-done = bf16[1,4864,896]{2,1,0:T(8,128)(2,1)} async-done(((bf16[1,1216,896]{2,1,0:T(8,128)(2,1)}), bf16[1,4864,896]{2,1,0:T(8,128)(2,1)}) %all-gather.13.cloned.1.call-update) | async-done | bytes 8716304 | tf_op jit(solution)/shard_map/all_gather | solution.py:64
  566.7 10.6 all_gather.44
  601.2 8.4 fusion.14
  631.9 11.2 all_gather.45
  680.7 11.9 multiply_convert_fusion.5
  692.6 12.7 multiply_reduce_fusion.2
  750.2 17.0 reduce-scatter.13.cloned.1.call-done
  776.2 19.4 fusion.272
  795.8 10.5 multiply_convert_fusion.3
  806.3 12.4 multiply_reduce_fusion.1
  863.8 20.5 reduce-scatter.15.cloned.1.call-done
  901.5 10.4 multiply_convert_fusion.1
  911.9 12.6 multiply_reduce_fusion
  962.0 20.5 add_add_fusion.1
  982.5 11.8 copy.327
  995.5 19.0 fusion.76
  1014.5 18.2 fusion.75
  1032.7 37.2 %add_add_fusion = f32[896,9728]{1,0:T(8,128)} fusion(f32[896,9728]{1,0:T(8,128)} %fusion.76, f32[896,9728]{1,0:T(8,128)} %fusion.75, bf16[256,4864]{1,0:T(8,128)(2,1)} %get-tuple-element.80, bf16[256,4864]{1,0:T(8,128)(2,1)} %get-tuple-element.79, f32[256,896]{1,0:T(8,128)S(1)} %copy-done.11, f32[896]{0:T(1024)S(1)} %mul.1145, f32[256]{0:T(256)S(1)} %copy-done.106), kind=kOutput, calls=%fused_computation.6 | convolution fusion | flops 4490821632 | bytes 110498304 | tf_op jit(solution)/shard_map/rd,rf->df/dot_general | solution.py:190
  1070.0 23.3 copy.326
  1116.0 242.7 %reduce-scatter.21.cloned.1.call-done = f32[304,896]{1,0:T(8,128)} async-done(((f32[4864,896]{1,0:T(8,128)}), f32[304,896]{1,0:T(8,128)}) %reduce-scatter.21.cloned.1.call-update) | async-done | bytes 1089552 | tf_op jit(solution)/shard_map/reduce_scatter | solution.py:390
  1360.9 715.2 %reduce-scatter.19.cloned.1.call-done = f32[56,9728]{1,0:T(8,128)} async-done(((f32[896,9728]{1,0:T(8,128)}), f32[56,9728]{1,0:T(8,128)}) %reduce-scatter.19.cloned.1.call-update) | async-done | bytes 2179088 | tf_op jit(solution)/shard_map/reduce_scatter | solution.py:384
  2098.6 75.8 %all-reduce.13 = (bf16[896]{0:T(1024)(128)(2,1)S(1)}, bf16[1024]{0:T(1024)(128)(2,1)S(1)}, bf16[128]{0:T(256)(128)(2,1)S(1)}, bf16[896]{0:T(1024)(128)(2,1)S(1)}) all-reduce(f32[896]{0:T(1024)S(1)} %reshape.632, f32[1024]{0:T(1024)S(1)} %reshape.636, ...), channel_id=5, replica_groups=mesh['section'=2,'ctx'=4,'fsdp'=4] {'ctx','fsdp'}, use_global_device_ids=true, to_apply=%region_36.37.clone | all-reduce | flops 2944 | bytes 17664
  2190.4 10.2 all_gather.100
  2201.6 106.4 %reduce-scatter.23.cloned.1.call-done = f32[56,1152]{1,0:T(8,128)} async-done(((f32[896,1152]{1,0:T(8,128)}), f32[56,1152]{1,0:T(8,128)}) %reduce-scatter.23.cloned.1.call-update) | async-done | bytes 258064
  2308.9 11.6 all_gather.47
  2321.5 23.6 all-gather.17.cloned.1.call-done
  2349.1 52.7 %all-gather.15.cloned.1.call-done = bf16[224,9728]{1,0:T(8,128)(2,1)} async-done(((bf16[56,9728]{1,0:T(8,128)(2,1)}), bf16[224,9728]{1,0:T(8,128)(2,1)}) %all-gather.15.cloned.1.call-update) | async-done | bytes 4358160 | tf_op jit(solution)/shard_map/all_gather | solution.py:422
  (650 shorter events, 370.9 us)
Async XLA Ops:
  7.2 50.6 %all-gather.7.cloned.1.call-start = ((), (), s32[]{:S(2)}) async-start(), calls=%async_computation.7 | async-start | bytes 2580480 | tf_op jit(solution)/shard_map/all_gather | solution.py:59
  8.0 87.7 %all-gather.9.cloned.1.call-start = ((), (), s32[]{:S(2)}) async-start(), calls=%async_computation.8 | async-start | bytes 2007040 | tf_op jit(solution)/shard_map/all_gather | solution.py:61
  8.7 386.5 %all-gather.11.cloned.1.call-start = ((), (), s32[]{:S(2)}) async-start(), calls=%async_computation.9 | async-start | bytes 21790720 | tf_op jit(solution)/shard_map/all_gather | solution.py:63
  9.5 541.2 %all-gather.13.cloned.1.call-start = ((), (), s32[]{:S(2)}) async-start(), calls=%async_computation.10 | async-start | bytes 10895360 | tf_op jit(solution)/shard_map/all_gather | solution.py:64
  10.0 757.2 %reduce-scatter.13.cloned.1.call-start = ((), (), s32[]{:S(2)}) async-start(), calls=%async_computation.11 | async-start | bytes 655360 | tf_op jit(solution)/shard_map/reduce_scatter | solution.py:238
  26.6 864.0 %copy-start.100 = (f32[896]{0:T(1024)}, f32[896]{0:T(1024)S(1)}, u32[]{:S(2)}) copy-start(f32[896]{0:T(1024)S(1)} %mul.1144) | copy-start | bytes 10756
  92.0 312.5 %copy-start.48 = (bf16[256,14,64]{0,2,1:T(8,128)(2,1)}, bf16[256,14,64]{0,2,1:T(8,128)(2,1)S(1)}, u32[]{:S(2)}) copy-start(bf16[256,14,64]{0,2,1:T(8,128)(2,1)S(1)} %maximum_convert_fusion) | copy-start | bytes 1376260
  97.9 452.8 %copy-start.10 = (f32[256,896]{1,0:T(8,128)}, f32[256,896]{1,0:T(8,128)S(1)}, u32[]{:S(2)}) copy-start(f32[256,896]{1,0:T(8,128)S(1)} %get-tuple-element.147) | copy-start | bytes 2752516
  98.5 306.0 %copy-start.105 = (f32[256]{0:T(256)}, f32[256]{0:T(256)S(1)}, u32[]{:S(2)}) copy-start(f32[256]{0:T(256)S(1)} %get-tuple-element.130) | copy-start | bytes 3076
  411.3 148.4 %copy-start.111 = (f32[256,32]{0,1:T(8,128)S(1)}, f32[256,32]{0,1:T(8,128)}, u32[]{:S(2)}) copy-start(f32[256,32]{0,1:T(8,128)} %get-tuple-element.140) | copy-start | bytes 98308
  411.3 148.7 %copy-start.114 = (s32[1,1,1024]{2,1,0:T(1,128)S(1)}, s32[1,1,1024]{2,1,0:T(1,128)}, u32[]{:S(2)}) copy-start(s32[1,1,1024]{2,1,0:T(1,128)} %get-tuple-element.124) | copy-start | bytes 12292
  411.3 148.7 %copy-start.139 = (s32[256]{0:T(256)S(1)}, s32[256]{0:T(256)}, u32[]{:S(2)}) copy-start(s32[256]{0:T(256)} %get-tuple-element.78) | copy-start | bytes 3076
  411.3 150.6 %copy-start.133 = (f32[1152]{0:T(1024)S(1)}, f32[1152]{0:T(1024)}, u32[]{:S(2)}) copy-start(f32[1152]{0:T(1024)} %copy-done.132) | copy-start | bytes 13828
  557.7 3.4 collective-permute-start
  599.0 219.7 %copy-start.107 = (f32[256]{0:T(256)}, f32[256]{0:T(256)S(1)}, u32[]{:S(2)}) copy-start(f32[256]{0:T(256)S(1)} %get-tuple-element.134) | copy-start | bytes 3076
  622.1 2.9 collective-permute-start.1
  625.3 148.3 %copy-start.115 = (f32[256]{0:T(256)}, f32[256]{0:T(256)S(1)}, u32[]{:S(2)}) copy-start(f32[256]{0:T(256)S(1)} %get-tuple-element.136) | copy-start | bytes 3076
  745.0 139.2 %reduce-scatter.15.cloned.1.call-start = ((), (), s32[]{:S(2)}) async-start(), calls=%async_computation.12 | async-start | bytes 655360 | tf_op jit(solution)/shard_map/reduce_scatter | solution.py:238
  774.9 20.7 collective-permute-start.2
  858.5 250.0 %reduce-scatter.17.cloned.1.call-start = ((), (), s32[]{:S(2)}) async-start(), calls=%async_computation.13 | async-start | bytes 655360 | tf_op jit(solution)/shard_map/reduce_scatter | solution.py:238
  892.0 9.5 collective-permute-start.3
  961.9 396.8 %reduce-scatter.21.cloned.1.call-start = ((), (), s32[]{:S(2)}) async-start(), calls=%async_computation.16 | async-start | bytes 18522112 | tf_op jit(solution)/shard_map/reduce_scatter | solution.py:390
  994.3 1081.8 %reduce-scatter.19.cloned.1.call-start = ((), (), s32[]{:S(2)}) async-start(), calls=%async_computation.14 | async-start | bytes 37044224 | tf_op jit(solution)/shard_map/reduce_scatter | solution.py:384
  1093.3 1096.1 %reduce-scatter.25.cloned.1.call-start = ((), (), s32[]{:S(2)}) async-start(), calls=%async_computation.19 | async-start | bytes 3411968
  1099.6 1208.3 %reduce-scatter.23.cloned.1.call-start = ((), (), s32[]{:S(2)}) async-start(), calls=%async_computation.18 | async-start | bytes 4386816
  1116.0 962.9 %copy-start.150 = (u32[32]{0:T(128)S(1)}, u32[32]{0:T(128)}, u32[]{:S(2)}) copy-start(u32[32]{0:T(128)} %constant.88) | copy-start | bytes 388
  1116.0 963.5 %copy-start.149 = (u32[32]{0:T(128)S(1)}, u32[32]{0:T(128)}, u32[]{:S(2)}) copy-start(u32[32]{0:T(128)} %constant.115) | copy-start | bytes 388
  1116.0 968.0 %copy-start.99 = (bf16[256,896]{1,0:T(8,128)(2,1)S(1)}, bf16[256,896]{1,0:T(8,128)(2,1)}, u32[]{:S(2)}) copy-start(bf16[256,896]{1,0:T(8,128)(2,1)} %copy-done.98) | copy-start | bytes 1376260
  1116.0 1229.1 %all-gather.17.cloned.1.call-start = ((), (), s32[]{:S(2)}) async-start(), calls=%async_computation.17 | async-start | bytes 2723840 | tf_op jit(solution)/shard_map/all_gather | solution.py:425
  1360.8 1041.0 %all-gather.15.cloned.1.call-start = ((), (), s32[]{:S(2)}) async-start(), calls=%async_computation.15 | async-start | bytes 5447680 | tf_op jit(solution)/shard_map/all_gather | solution.py:422
  2091.2 94.1 %copy-start.50 = (f32[256,896]{1,0:T(8,128)S(1)}, f32[256,896]{1,0:T(8,128)}, u32[]{:S(2)}) copy-start(f32[256,896]{1,0:T(8,128)} %get-tuple-element.76) | copy-start | bytes 2752516
  2091.2 94.0 %copy-start.136 = (f32[256]{0:T(256)S(1)}, f32[256]{0:T(256)}, u32[]{:S(2)}) copy-start(f32[256]{0:T(256)} %get-tuple-element.127) | copy-start | bytes 3076
  (165 other events, 1426.1 us)
Sparse Core Ops, SparseCore 0:
  9.6 48.1 all-gather.6
  59.4 36.1 all-gather.8
  97.3 297.8 all-gather.10
  396.6 154.0 all-gather.12
  745.1 22.0 reduce-scatter.12
  858.6 25.5 reduce-scatter.14
  962.0 25.6 reduce-scatter.16
  994.4 364.2 reduce-scatter.20
  1361.1 714.9 reduce-scatter.18
  2078.4 88.0 reduce-scatter.24
  2173.0 134.8 reduce-scatter.22
  2309.8 35.3 all-gather.16
  2347.7 54.0 all-gather.14
where the time goes:
time: 2420 us
  waiting for transfers between devices  1650 us (68%)
  matrix products  399 us (16%)
  blocking collectives  151 us (6%)
  other arithmetic  111 us (5%)
  local copies, waits for them, and re-layouts  77.4 us (3%)
    reduce_scatter x1, waiting for transfers between devices, per_device(): lax.psum_scatter(reorder(expand_grad, ctx_count, fsdp_count), ('ctx', 'fs...  715 us
    all_gather x1, waiting for transfers between devices, fetch_layer(): lax.all_gather(expand, 'fsdp', axis=1, tiled=True)  297 us
    reduce_scatter x1, waiting for transfers between devices, per_device(): lax.psum_scatter(reorder(down_grad, ctx_count, fsdp_count), ('ctx', 'fsdp...  243 us
    all_gather x1, waiting for transfers between devices, fetch_layer(): lax.all_gather(shrink, 'fsdp', axis=1, tiled=True)  139 us
    unnamed x15, waiting for transfers between devices  109 us
    unnamed x3, blocking collectives  97.6 us
    dot_general x3, matrix products, backward(): jnp.einsum('rd,rf->df', second_normed, widened_grad, preferred_element_ty...  74.5 us
    all_gather x1, waiting for transfers between devices, per_device(): lax.all_gather(totals[6].astype(jnp.bfloat16), 'ctx', axis=0, tiled=True)  52.7 us
  transfers between devices with their start and end apart: 17, of which 13 were waited for; matrix products, arithmetic and copies ran while one was open for 11% of the time, Pallas kernels for 0%

commit v1 on v0

v1 whole, which is shorter than its diff:
```python
import jax
import jax.numpy as jnp
from jax import lax
from jax.sharding import PartitionSpec as P

HEAD_DIM = 64
SECTION, CTX, FSDP = "section", "ctx", "fsdp"

epsilon = 1e-06
theta_base = 1000000.0
masked_value = -1e30

bf16 = jnp.bfloat16
f32 = jnp.float32


def swap_sections(block):
    return lax.ppermute(block, SECTION, [(0, 1), (1, 0)])


def from_peer(block, distance):
    count = lax.axis_size(CTX)
    return lax.ppermute(block, CTX, [(i, i ^ distance) for i in range(count)])


def normalize_rows(values, gain_row):
    norm_scale = lax.rsqrt(jnp.mean(values * values, axis=-1, keepdims=True) + epsilon)
    return (values * norm_scale * gain_row, norm_scale)


def norm_back(upstream, values, norm_scale, gain_row):
    scaled = upstream * gain_row
    gain_grad = jnp.sum(upstream * values * norm_scale, axis=0)
    scale_cubed = norm_scale * norm_scale * norm_scale
    values_grad = norm_scale * scaled - values * scale_cubed * jnp.mean(
        scaled * values, axis=-1, keepdims=True
    )
    return (values_grad, gain_grad)


def tables(positions_row):
    half_dim = HEAD_DIM // 2
    frequency = theta_base ** (-(jnp.arange(half_dim, dtype=f32) * 2.0) / HEAD_DIM)
    angles = positions_row.astype(f32)[:, None] * frequency[None, :]
    angles = jnp.concatenate([angles, angles], axis=-1)
    return (jnp.cos(angles)[:, None, :], jnp.sin(angles)[:, None, :])


def turned(values):
    half_dim = values.shape[-1] // 2
    return jnp.concatenate([-values[..., half_dim:], values[..., :half_dim]], axis=-1)


def rotate(values, cosine, sine):
    return values * cosine + turned(values) * sine


def unrotate(grads, cosine, sine):
    return grads * cosine - turned(grads * sine)


def dot(left, right):
    return jnp.dot(left, right, preferred_element_type=f32)


def pick(index, options):
    chosen = options[0]
    for position in range(1, len(options)):
        chosen = jnp.where(index == position, options[position], chosen)
    return chosen


def head_scores(queries, every_kv, head_index, group_size, key_positions, query_positions):
    grouped = queries[:, head_index * group_size : (head_index + 1) * group_size, :]
    key_block = every_kv[:, head_index * HEAD_DIM : (head_index + 1) * HEAD_DIM]
    scores = jnp.einsum(
        "qgd,kd->gqk", grouped, key_block, preferred_element_type=f32
    ) * HEAD_DIM ** (-0.5)
    allowed = key_positions[None, None, :] <= query_positions[None, :, None]
    return (jnp.where(allowed, scores, masked_value), grouped, key_block)


def attend(layer, hidden, place):
    first_gain, bias, second_gain, weights = layer[:4]
    cosine, sine, key_positions, query_positions = place
    row_count, model_width = hidden.shape
    pair_width = (bias.shape[0] - model_width) // 2
    head_count = model_width // HEAD_DIM
    kv_count = pair_width // HEAD_DIM
    group_size = head_count // kv_count
    wide = model_width + 2 * pair_width
    normed, first_scale = normalize_rows(hidden, first_gain)
    normed = normed.astype(bf16)
    combined = dot(normed, weights[:, :wide]) + bias
    queries = rotate(
        combined[:, :model_width].reshape(row_count, head_count, HEAD_DIM), cosine, sine
    ).astype(bf16)
    key_rows = rotate(
        combined[:, model_width : model_width + pair_width].reshape(row_count, kv_count, HEAD_DIM),
        cosine,
        sine,
    )
    local_kv = jnp.concatenate(
        [key_rows.reshape(row_count, pair_width), combined[:, model_width + pair_width :]], axis=1
    ).astype(bf16)
    every_kv = lax.all_gather(local_kv, CTX, axis=0, tiled=True)
    contexts = []
    row_maxes = []
    row_totals = []
    for head_index in range(kv_count):
        masked, grouped, key_block = head_scores(
            queries, every_kv, head_index, group_size, key_positions, query_positions
        )
        row_max = jnp.max(masked, axis=-1, keepdims=True)
        exponent = jnp.exp(masked - row_max)
        row_total = jnp.sum(exponent, axis=-1, keepdims=True)
        attention_low = (exponent / row_total).astype(bf16)
        value_block = every_kv[
            :, pair_width + head_index * HEAD_DIM : pair_width + (head_index + 1) * HEAD_DIM
        ]
        contexts.append(
            jnp.einsum("gqk,kd->qgd", attention_low, value_block, preferred_element_type=f32)
        )
        row_maxes.append(row_max)
        row_totals.append(row_total)
    context = jnp.concatenate(contexts, axis=1).reshape(row_count, model_width).astype(bf16)
    middle = hidden + dot(context, weights[:, wide:])
    second_normed, second_scale = normalize_rows(middle, second_gain)
    kept = (hidden, first_scale, normed, queries, every_kv, row_maxes, row_totals, context)
    return middle, second_normed.astype(bf16), second_scale, kept


def attend_back(layer, kept, middle_grad, place):
    first_gain, bias, second_gain, weights = layer[:4]
    cosine, sine, key_positions, query_positions = place
    hidden, first_scale, normed, queries, every_kv, row_maxes, row_totals, context = kept
    row_count, model_width = hidden.shape
    pair_width = every_kv.shape[1] // 2
    head_count = model_width // HEAD_DIM
    kv_count = pair_width // HEAD_DIM
    group_size = head_count // kv_count
    wide = model_width + 2 * pair_width
    middle_low = middle_grad.astype(bf16)
    output_grad = jnp.einsum("rd,re->de", context, middle_low, preferred_element_type=f32)
    context_grad = jnp.einsum(
        "re,de->rd", middle_low, weights[:, wide:], preferred_element_type=f32
    )
    context_grad = context_grad.astype(bf16).reshape(row_count, head_count, HEAD_DIM)
    query_grads = []
    key_grads = []
    value_grads = []
    for head_index in range(kv_count):
        masked, grouped, key_block = head_scores(
            queries, every_kv, head_index, group_size, key_positions, query_positions
        )
        attention_full = jnp.exp(masked - row_maxes[head_index]) / row_totals[head_index]
        attention_low = attention_full.astype(bf16)
        value_block = every_kv[
            :, pair_width + head_index * HEAD_DIM : pair_width + (head_index + 1) * HEAD_DIM
        ]
        context_block = context_grad[:, head_index * group_size : (head_index + 1) * group_size, :]
        probs_grad = jnp.einsum(
            "qgd,kd->gqk", context_block, value_block, preferred_element_type=f32
        )
        row_delta = jnp.sum(attention_full * probs_grad, axis=-1, keepdims=True)
        scores_grad = (attention_full * (probs_grad - row_delta)).astype(bf16)
        query_grads.append(
            jnp.einsum("gqk,kd->qgd", scores_grad, key_block, preferred_element_type=f32)
            * HEAD_DIM ** (-0.5)
        )
        key_grads.append(
            jnp.einsum("gqk,qgd->kd", scores_grad, grouped, preferred_element_type=f32)
            * HEAD_DIM ** (-0.5)
        )
        value_grads.append(
            jnp.einsum("gqk,qgd->kd", attention_low, context_block, preferred_element_type=f32)
        )
    every_grad = jnp.concatenate(key_grads + value_grads, axis=1)
    own_grad = lax.psum_scatter(
        every_grad.astype(bf16), CTX, scatter_dimension=0, tiled=True
    ).astype(f32)
    query_turned = unrotate(jnp.concatenate(query_grads, axis=1), cosine, sine).reshape(
        row_count, model_width
    )
    key_turned = unrotate(
        own_grad[:, :pair_width].reshape(row_count, kv_count, HEAD_DIM), cosine, sine
    ).reshape(row_count, pair_width)
    combined_grad = jnp.concatenate(
        [query_turned, key_turned, own_grad[:, pair_width:]], axis=1
    ).astype(bf16)
    project_grad = jnp.einsum("rd,rf->df", normed, combined_grad, preferred_element_type=f32)
    offset_grad = jnp.sum(combined_grad.astype(f32), axis=0)
    normed_grad = jnp.einsum(
        "rf,df->rd", combined_grad, weights[:, :wide], preferred_element_type=f32
    )
    hidden_part, first_grad = norm_back(normed_grad, hidden, first_scale, first_gain)
    attn_grad = jnp.concatenate([project_grad, output_grad], axis=1).astype(bf16)
    return middle_grad + hidden_part, first_grad, offset_grad, attn_grad


def feed(layer, second_normed):
    gate_w, up_w, down_w = layer[4:]
    count = lax.axis_size(CTX)
    blocks = [second_normed] + [from_peer(second_normed, k) for k in range(1, count)]
    gates, ups, acts = [], [], []
    total = None
    for k, block in enumerate(blocks):
        gate = dot(block, gate_w)
        up = dot(block, up_w)
        act = (jax.nn.silu(gate) * up).astype(bf16)
        part = dot(act, down_w)
        gates.append(gate)
        ups.append(up)
        acts.append(act)
        if k:
            part = from_peer(part.astype(bf16), k).astype(f32)
        total = part if total is None else total + part
    return total, (blocks, gates, ups, acts)


def feed_back(layer, kept, grad_out):
    gate_w, up_w, down_w = layer[4:]
    blocks, gates, ups, acts = kept
    count = lax.axis_size(CTX)
    grads = [grad_out] + [from_peer(grad_out, k) for k in range(1, count)]
    total = None
    gate_grads, up_grads = [], []
    for k in range(count):
        spread = jnp.einsum("rd,fd->rf", grads[k], down_w, preferred_element_type=f32)
        gate, up = gates[k], ups[k]
        sig = jax.nn.sigmoid(gate)
        gate_grad = (spread * up * sig * (1.0 + gate * (1.0 - sig))).astype(bf16)
        up_grad = (spread * (gate * sig)).astype(bf16)
        part = jnp.einsum("rf,df->rd", gate_grad, gate_w, preferred_element_type=f32) + jnp.einsum(
            "rf,df->rd", up_grad, up_w, preferred_element_type=f32
        )
        gate_grads.append(gate_grad)
        up_grads.append(up_grad)
        if k:
            part = from_peer(part.astype(bf16), k).astype(f32)
        total = part if total is None else total + part
    rows = jnp.concatenate(blocks, axis=0)
    down_grad = jnp.einsum(
        "rf,rd->fd",
        jnp.concatenate(acts, axis=0),
        jnp.concatenate(grads, axis=0),
        preferred_element_type=f32,
    ).astype(bf16)
    gate_w_grad = jnp.einsum(
        "rd,rf->df", rows, jnp.concatenate(gate_grads, axis=0), preferred_element_type=f32
    ).astype(bf16)
    up_w_grad = jnp.einsum(
        "rd,rf->df", rows, jnp.concatenate(up_grads, axis=0), preferred_element_type=f32
    ).astype(bf16)
    return total, down_grad, jnp.concatenate([gate_w_grad, up_w_grad], axis=1)


def per_device(
    inputs,
    attend_gain,
    projections,
    biases,
    output_weight,
    mixer_gain,
    expand_weight,
    down_weight,
    positions,
    cotangent,
):
    row_count, model_width = inputs.shape[2:]
    section = lax.axis_index(SECTION)
    is_first = section == 0
    ctx = lax.axis_index(CTX)
    fsdp = lax.axis_index(FSDP)
    ctx_count = lax.axis_size(CTX)
    fsdp_count = lax.axis_size(FSDP)
    shard_rows = projections.shape[1]
    half = shard_rows // 2
    wide = projections.shape[2]
    ff_width = expand_weight.shape[2] // 2
    shard_units = down_weight.shape[1]
    units = shard_units // ctx_count
    both = (FSDP, SECTION)

    def mine(array):
        return lax.dynamic_index_in_dim(array, section, 0, keepdims=False)

    source = mine(inputs)[0].astype(f32)
    upstream = mine(cotangent)[0]
    key_positions = mine(positions)[0]
    query_positions = lax.dynamic_slice_in_dim(key_positions, ctx * row_count, row_count)
    cosine, sine = tables(query_positions)
    place = (cosine, sine, key_positions, query_positions)

    small = jnp.concatenate([attend_gain, biases, mixer_gain], axis=1)
    small = lax.all_gather(small, (SECTION, FSDP), axis=0, tiled=True).astype(f32)
    small = small.reshape(2, fsdp_count, -1)
    bias_part = biases.shape[1]

    def small_of(layer):
        rows = small[layer]
        return (
            rows[:, :shard_rows].reshape(-1),
            rows[:, shard_rows : shard_rows + bias_part].reshape(-1),
            rows[:, shard_rows + bias_part :].reshape(-1),
        )

    attn_shard = jnp.concatenate([projections[0], output_weight[0]], axis=1)

    def unit_columns(side):
        pieces = []
        for shard in range(fsdp_count):
            start = side * ff_width + shard * shard_units
            pieces.append(
                pick(
                    ctx,
                    [
                        expand_weight[0, :, start + k * units : start + (k + 1) * units]
                        for k in range(ctx_count)
                    ],
                )
            )
        return jnp.concatenate(pieces, axis=1)

    gate_shard = unit_columns(0)
    up_shard = unit_columns(1)
    down_shard = lax.dynamic_slice_in_dim(down_weight[0], ctx * units, units)

    def halves(array):
        size = array.shape[0] // 2
        low, high = array[:size], array[size:]
        own = jnp.where(is_first, low, high)
        other = swap_sections(jnp.where(is_first, high, low))
        return jnp.where(is_first, own, other), jnp.where(is_first, other, own)

    attn_pair = halves(attn_shard)
    gate_pair = halves(gate_shard)
    up_pair = halves(up_shard)
    down_pair = halves(down_shard)

    def gather(piece):
        return lax.all_gather(piece, both, axis=0, tiled=True)

    layers = []
    for layer in range(2):
        layers.append(
            small_of(layer)
            + (
                gather(attn_pair[layer]),
                gather(gate_pair[layer]),
                gather(up_pair[layer]),
                gather(down_pair[layer]),
            )
        )

    hidden = source
    stored = []
    sent = []
    for layer in range(2):
        middle, second_normed, second_scale, kept = attend(layers[layer], hidden, place)
        total, fed = feed(layers[layer], second_normed)
        low = (middle + total).astype(bf16)
        sent.append(low)
        hidden = low.astype(f32)
        stored.append((middle, second_scale, kept, fed))

    grad = upstream
    hidden_grads = [None, None]
    small_grads = [None, None]
    weight_grads = [None, None]
    for layer in (1, 0):
        middle, second_scale, kept, fed = stored[layer]
        total, down_grad, expand_grad = feed_back(layers[layer], fed, grad)
        middle_part, second_grad = norm_back(total, middle, second_scale, layers[layer][2])
        middle_grad = grad.astype(f32) + middle_part
        hidden_grad, first_grad, offset_grad, attn_grad = attend_back(
            layers[layer], kept, middle_grad, place
        )
        attn_part = lax.psum_scatter(
            attn_grad.reshape(model_width, ctx_count, -1).swapaxes(0, 1).reshape(ctx_count * model_width, -1),
            CTX,
            scatter_dimension=0,
            tiled=True,
        )
        row_grad = jnp.concatenate([expand_grad, attn_part], axis=1)
        weight_grads[layer] = (
            lax.psum_scatter(row_grad, both, scatter_dimension=0, tiled=True),
            lax.psum_scatter(down_grad, both, scatter_dimension=0, tiled=True),
        )
        small_grads[layer] = jnp.concatenate([first_grad, offset_grad, second_grad])
        hidden_grads[layer] = hidden_grad
        grad = hidden_grad.astype(bf16)

    def to_layer(pair):
        own = jnp.where(is_first, pair[0], pair[1])
        other = swap_sections(jnp.where(is_first, pair[1], pair[0]))
        return jnp.where(is_first, own, other), jnp.where(is_first, other, own)

    def finish(pair):
        low, high = to_layer(pair)
        return lax.all_gather(jnp.concatenate([low, high], axis=0), CTX, axis=0).astype(f32)

    row_all = finish((weight_grads[0][0], weight_grads[1][0]))
    down_all = finish((weight_grads[0][1], weight_grads[1][1]))
    grad_down = down_all.reshape(1, shard_units, model_width)
    columns = []
    for side in range(2):
        for shard in range(fsdp_count):
            start = side * fsdp_count * units + shard * units
            for k in range(ctx_count):
                columns.append(row_all[k, :, start : start + units])
    grad_expand = jnp.concatenate(columns, axis=1)[None]
    attn_all = jnp.concatenate(
        [row_all[k, :, 2 * fsdp_count * units :] for k in range(ctx_count)], axis=1
    )
    grad_projections = attn_all[:, :wide][None]
    grad_output = attn_all[:, wide:][None]

    small_all = lax.psum(jnp.stack(small_grads), (CTX, FSDP, SECTION))
    small_own = mine(small_all)
    first_all, offset_all, second_all = (
        small_own[:model_width],
        small_own[model_width : model_width + wide],
        small_own[model_width + wide :],
    )
    pair_width = (wide - model_width) // 2

    def part(vector):
        size = vector.shape[0] // fsdp_count
        return lax.dynamic_slice_in_dim(vector, fsdp * size, size)[None]

    def from_both(pair):
        own = jnp.where(is_first, pair[0], pair[1])
        other = swap_sections(jnp.where(is_first, pair[1], pair[0]))
        return jnp.stack(
            [jnp.where(is_first, own, other), jnp.where(is_first, other, own)]
        )[None, :, None]

    activations = from_both(sent)
    input_grads = from_both([hidden_grads[0], hidden_grads[1].astype(bf16).astype(f32)])
    return (
        activations,
        input_grads,
        part(first_all),
        grad_projections,
        part(offset_all[: model_width + pair_width]),
        part(offset_all[model_width + pair_width :]),
        grad_output,
        part(second_all),
        grad_expand,
        grad_down,
    )


def solution(mesh):
    return jax.shard_map(
        per_device,
        mesh=mesh,
        in_specs=(
            P(None, FSDP, CTX, None),
            P(SECTION, FSDP),
            P(SECTION, FSDP, None),
            P(SECTION, FSDP),
            P(SECTION, FSDP, None),
            P(SECTION, FSDP),
            P(SECTION, FSDP, None),
            P(SECTION, FSDP, None),
            P(None, FSDP, None),
            P(None, FSDP, CTX, None),
        ),
        out_specs=(
            P(SECTION, None, FSDP, CTX, None),
            P(SECTION, None, FSDP, CTX, None),
            P(SECTION, FSDP),
            P(SECTION, FSDP, None),
            P(SECTION, FSDP),
            P(SECTION, FSDP),
            P(SECTION, FSDP, None),
            P(SECTION, FSDP),
            P(SECTION, FSDP, None),
            P(SECTION, FSDP, None),
        ),
        check_vma=False,
    )
```

time: 2420 us -> 980 us (0.40)
  waiting for transfers between devices: 1650 us -> 406 us
  matrix products: 399 us -> 245 us
  blocking collectives: 151 us -> 84.8 us
  starting transfers between devices: 7.04 us -> 33.3 us
    reduce_scatter x5 -> x2, waiting for transfers between devices: 995 us -> 20.1 us  [attend_back(): lax.psum_scatter(every_grad.astype(bf16), CTX, scatter_dimension=0, tiled...]
    all_gather x6 -> x10, waiting for transfers between devices: 543 us -> 79.2 us  [the longest x8 71.9 us: gather(): return lax.all_gather(piece, both, axis=0, tiled=True)]
    dot_general x66 -> x86, matrix products: 362 us -> 221 us  [the longest x28 73.3 us: dot(): return jnp.dot(left, right, preferred_element_type=f32)]
    unnamed x15 -> x24, waiting for transfers between devices: 109 us -> 216 us
    unnamed x3 -> x0, blocking collectives: 97.6 us -> none
    ppermute x4 -> x32, waiting for transfers between devices: 0.61 us -> 90.4 us  [the longest x24 79.3 us: from_peer(): return lax.ppermute(block, CTX, [(i, i ^ distance) for i in range(count)])]
    transpose x8 -> x0, local copies, waits for them, and re-layouts: 39.3 us -> none  [reorder(): return jnp.swapaxes(shaped, 0, 1).reshape(gradient.shape)]
    psum x0 -> x1, blocking collectives: none -> 38.5 us  [per_device(): small_all = lax.psum(jnp.stack(small_grads), (CTX, FSDP, SECTION))]
  transfers between devices with their start and end apart: 17 -> 50, of which waited for: 13 -> 31; matrix products, arithmetic and copies ran while one was open for 11% -> 31% of each run, Pallas kernels for 0% -> 0%
where the time goes in v1:
time: 980 us; the launch traced here: 970 us
  waiting for transfers between devices  406 us (41%)
  matrix products  245 us (25%)
  local copies, waits for them, and re-layouts  94.3 us (10%)
  other arithmetic  89.1 us (9%)
  blocking collectives  84.8 us (9%)
  starting transfers between devices  33.3 us (3%)
  between operations  17.1 us (2%)
    unnamed x24, waiting for transfers between devices  216 us
    ppermute x24, waiting for transfers between devices, from_peer(): return lax.ppermute(block, CTX, [(i, i ^ distance) for i in range(count)])  79.3 us
    dot_general x28, matrix products, dot(): return jnp.dot(left, right, preferred_element_type=f32)  73.3 us
    all_gather x8, waiting for transfers between devices, gather(): return lax.all_gather(piece, both, axis=0, tiled=True)  71.9 us
    unnamed x287, local copies, waits for them, and re-layouts  43.8 us
    psum x1, blocking collectives, per_device(): small_all = lax.psum(jnp.stack(small_grads), (CTX, FSDP, SECTION))  38.5 us
    ppermute x24, starting transfers between devices, from_peer(): return lax.ppermute(block, CTX, [(i, i ^ distance) for i in range(count)])  29.8 us
    convert_element_type x4, other arithmetic, attend_back(): scores_grad = (attention_full * (probs_grad - row_delta)).astype(bf16)  25.3 us
  transfers between devices with their start and end apart: 50, of which 31 were waited for; matrix products, arithmetic and copies ran while one was open for 31% of the time, Pallas kernels for 0%

profile of v1, /device:TPU:0, one launch (start us, length us, event | category | flops | bytes accessed | tf_op | source)
XLA Modules:
  0.0 969.7 jit_solution(16309457472581309250)
XLA Ops:
  35.4 24.1 %all-gather.2 = bf16[8,1,736]{2,1,0:T(2,128)(2,1)S(1)} all-gather(bf16[1,1,736]{2,1,0:T(2,128)(2,1)S(1)} %maximum_bitcast_fusion.2), channel_id=1, replica_groups=mesh['section'=2,'ctx'=4,'fsdp'=4] {'section','fsdp'}, dimensions={0}, use_global_device_ids=true | all-gather | bytes 13248 | tf_op jit(solution)/shard_map/all_gather | solution.py:296
  67.2 22.0 %all-gather.14.cloned.1.call-done = bf16[896,2048]{1,0:T(8,128)(2,1)} async-done(((bf16[112,2048]{1,0:T(8,128)(2,1)}), bf16[896,2048]{1,0:T(8,128)(2,1)}) %all-gather.14.cloned.1.call-update) | async-done | bytes 3670032 | tf_op jit(solution)/shard_map/all_gather | solution.py:342
  92.4 10.5 %all_gather.47 = bf16[1024,256]{1,0:T(8,128)(2,1)S(1)} all-gather(bf16[256,256]{1,0:T(8,128)(2,1)S(1)} %pad_maximum_fusion.24), channel_id=1, replica_groups=mesh['section'=2,'ctx'=4,'fsdp'=4] {'ctx'}, dimensions={0}, use_global_device_ids=true | all-gather | bytes 655360 | tf_op jit(solution)/shard_map/all_gather | solution.py:106
  144.0 9.4 all-gather.18.cloned.1.call-done
  157.8 26.4 %all-gather.20.cloned.1.call-done = bf16[1216,896]{1,0:T(8,128)(2,1)} async-done(((bf16[152,896]{1,0:T(8,128)(2,1)}), bf16[1216,896]{1,0:T(8,128)(2,1)}) %all-gather.20.cloned.1.call-update) | async-done | bytes 2179088 | tf_op jit(solution)/shard_map/all_gather | solution.py:342
  217.8 10.6 %all-gather.22.cloned.1.call-done = bf16[896,2048]{1,0:T(8,128)(2,1)} async-done(((bf16[112,2048]{1,0:T(8,128)(2,1)}), bf16[896,2048]{1,0:T(8,128)(2,1)}) %all-gather.22.cloned.1.call-update) | async-done | bytes 3670032 | tf_op jit(solution)/shard_map/all_gather | solution.py:342
  235.7 11.6 %all_gather.52 = bf16[1024,256]{1,0:T(8,128)(2,1)} all-gather(bf16[256,256]{1,0:T(8,128)(2,1)S(1)} %pad_maximum_fusion.25), channel_id=1, replica_groups=mesh['section'=2,'ctx'=4,'fsdp'=4] {'ctx'}, dimensions={0}, use_global_device_ids=true | all-gather | bytes 655360 | tf_op jit(solution)/shard_map/all_gather | solution.py:106
  248.4 6.6 fusion.340
  321.9 8.4 collective-permute-done.20
  348.4 6.4 fusion.12
  356.8 7.2 fusion.13
  364.0 6.3 fusion.15
  376.5 20.1 %reduce-scatter.21.cloned.1.call-done = bf16[256,256]{0,1:T(8,128)(2,1)} async-done(((bf16[1024,256]{0,1:T(8,128)(2,1)}), bf16[256,256]{0,1:T(8,128)(2,1)}) %reduce-scatter.21.cloned.1.call-update) | async-done | bytes 131088 | tf_op jit(solution)/shard_map/reduce_scatter | solution.py:179
  405.7 9.9 %collective-permute-done.23 = bf16[256,896]{1,0:T(8,128)(2,1)S(1)} collective-permute-done((bf16[256,896]{1,0:T(8,128)(2,1)S(1)}, bf16[256,896]{1,0:T(8,128)(2,1)S(1)}, u32[]{:S(2)}, u32[]{:S(2)}) %collective-permute-start.23) | collective-permute-done | bytes 458784 | tf_op jit(solution)/shard_map/ppermute | solution.py:23
  438.0 10.7 %collective-permute-done.26 = bf16[256,896]{1,0:T(8,128)(2,1)S(1)} collective-permute-done((bf16[256,896]{1,0:T(8,128)(2,1)S(1)}, bf16[256,896]{1,0:T(8,128)(2,1)S(1)}, u32[]{:S(2)}, u32[]{:S(2)}) %collective-permute-start.26) | collective-permute-done | bytes 458784 | tf_op jit(solution)/shard_map/ppermute | solution.py:23
  473.0 6.4 fusion.6
  496.5 7.2 convert_element_type.377
  522.6 7.3 convert_element_type.374
  573.2 7.8 copy.275
  581.1 6.7 convolution_convert_fusion.2
  593.4 24.9 %reduce-scatter.25.cloned.1.call-done = bf16[896,512]{1,0:T(8,128)(2,1)} async-done(((bf16[3584,512]{1,0:T(8,128)(2,1)}), bf16[896,512]{1,0:T(8,128)(2,1)}) %reduce-scatter.25.cloned.1.call-update) | async-done | bytes 917520
  625.0 8.1 copy.271
  633.2 26.9 %reduce-scatter.35.cloned.1.call-done = bf16[152,896]{1,0:T(8,128)(2,1)} async-done(((bf16[1216,896]{1,0:T(8,128)(2,1)}), bf16[152,896]{1,0:T(8,128)(2,1)}) %reduce-scatter.35.cloned.1.call-update) | async-done | bytes 272400
  660.1 39.6 %reduce-scatter.33.cloned.1.call-done = bf16[152,896]{1,0:T(8,128)(2,1)} async-done(((bf16[1216,896]{1,0:T(8,128)(2,1)}), bf16[152,896]{1,0:T(8,128)(2,1)}) %reduce-scatter.33.cloned.1.call-update) | async-done | bytes 272400
  704.5 57.3 %reduce-scatter.31.cloned.1.call-done = bf16[112,2944]{1,0:T(8,128)(2,1)} async-done(((bf16[896,2944]{1,0:T(8,128)(2,1)}), bf16[112,2944]{1,0:T(8,128)(2,1)}) %reduce-scatter.31.cloned.1.call-update) | async-done | bytes 659472
  763.3 59.6 %reduce-scatter.27.cloned.1.call-done = bf16[112,2944]{1,0:T(8,128)(2,1)} async-done(((bf16[896,2944]{1,0:T(8,128)(2,1)}), bf16[112,2944]{1,0:T(8,128)(2,1)}) %reduce-scatter.27.cloned.1.call-update) | async-done | bytes 659472
  844.8 13.1 %collective-permute-done.11 = bf16[256,896]{1,0:T(8,128)(2,1)S(1)} collective-permute-done((bf16[256,896]{1,0:T(8,128)(2,1)S(1)}, bf16[256,896]{1,0:T(8,128)(2,1)S(1)}, u32[]{:S(2)}, u32[]{:S(2)}) %collective-permute-start.11) | collective-permute-done | bytes 458784 | tf_op jit(solution)/shard_map/ppermute | solution.py:23
  857.8 9.6 collective-permute-done.13
  867.4 6.9 collective-permute-done.15
  885.5 38.5 %psum.7 = f32[2,2944]{1,0:T(2,128)S(1)} all-reduce(f32[2,2944]{1,0:T(2,128)S(1)} %pad_maximum_fusion.29), channel_id=1, replica_groups=mesh['section'=2,'ctx'=4,'fsdp'=4] {'ctx','fsdp','section'}, use_global_device_ids=true, to_apply=%region_28.29 | all-reduce | flops 5888 | bytes 47104 | tf_op jit(solution)/shard_map/psum | solution.py:419
  931.4 7.3 all-gather.30.cloned.1.call-done
  950.5 11.8 %concatenate.195 = f32[224,9728]{1,0:T(8,128)} concatenate(f32[224,304]{1,0:T(8,128)} %get-tuple-element.81, f32[224,304]{1,0:T(8,128)} %get-tuple-element.80, f32[224,304]{1,0:T(8,128)} %get-tuple-element.79, f32[224,304]{1,0:T(8,128)S(1)} %get-tuple-element.78, f32[224,304]{1,0:T(8,128)S(1)} %get-tuple-element.77, f32[224,304]{1,0:T(8,128)S(1)} %get-tuple-element.76, ...), dimensions={1} | concatenate | bytes 17432576 | tf_op jit(solution)/shard_map/concatenate | solution.py:412
  (604 shorter events, 423.5 us)
Async XLA Ops:
  7.2 56.3 %all-gather.28.cloned.1.call-start = ((), (), s32[]{:S(2)}) async-start(), calls=%async_computation.15 | async-start | bytes 2451456 | tf_op jit(solution)/shard_map/all_gather | solution.py:342
  12.1 77.1 %all-gather.14.cloned.1.call-start = ((), (), s32[]{:S(2)}) async-start(), calls=%async_computation.8 | async-start | bytes 4128768 | tf_op jit(solution)/shard_map/all_gather | solution.py:342
  15.4 119.3 %all-gather.16.cloned.1.call-start = ((), (), s32[]{:S(2)}) async-start(), calls=%async_computation.9 | async-start | bytes 2580480 | tf_op jit(solution)/shard_map/all_gather | solution.py:342
  25.0 128.3 %all-gather.18.cloned.1.call-start = ((), (), s32[]{:S(2)}) async-start(), calls=%async_computation.10 | async-start | bytes 2580480 | tf_op jit(solution)/shard_map/all_gather | solution.py:342
  28.2 155.9 %all-gather.20.cloned.1.call-start = ((), (), s32[]{:S(2)}) async-start(), calls=%async_computation.11 | async-start | bytes 2451456 | tf_op jit(solution)/shard_map/all_gather | solution.py:342
  28.8 199.5 %all-gather.22.cloned.1.call-start = ((), (), s32[]{:S(2)}) async-start(), calls=%async_computation.12 | async-start | bytes 4128768 | tf_op jit(solution)/shard_map/all_gather | solution.py:342
  29.4 247.9 %all-gather.26.cloned.1.call-start = ((), (), s32[]{:S(2)}) async-start(), calls=%async_computation.14 | async-start | bytes 2580480 | tf_op jit(solution)/shard_map/all_gather | solution.py:342
  30.1 261.3 %all-gather.24.cloned.1.call-start = ((), (), s32[]{:S(2)}) async-start(), calls=%async_computation.13 | async-start | bytes 2580480 | tf_op jit(solution)/shard_map/all_gather | solution.py:342
  31.0 240.6 %collective-permute-start.21 = (bf16[256,896]{1,0:T(8,128)(2,1)}, bf16[256,896]{1,0:T(8,128)(2,1)}, u32[]{:S(2)}, u32[]{:S(2)}) collective-permute-start(bf16[256,896]{1,0:T(8,128)(2,1)} %dynamic-slice_bitcast_fusion), channel_id=1, source_target_pairs={{0,12},{4,8},{8,4},{12,0},{1,13},{5,9},{9,5},{13,1},{2,14},{6,10},... | collective-permute-start | bytes 1376264 | tf_op jit(solution)/shard_map/ppermute | solution.py:23
  34.7 95.1 %collective-permute-start.19 = (bf16[256,896]{1,0:T(8,128)(2,1)}, bf16[256,896]{1,0:T(8,128)(2,1)}, u32[]{:S(2)}, u32[]{:S(2)}) collective-permute-start(bf16[256,896]{1,0:T(8,128)(2,1)} %dynamic-slice_bitcast_fusion), channel_id=1, source_target_pairs={{0,8},{4,12},{8,0},{12,4},{1,9},{5,13},{9,1},{13,5},{2,10},{6,14},... | collective-permute-start | bytes 1376264 | tf_op jit(solution)/shard_map/ppermute | solution.py:23
  35.2 91.6 %collective-permute-start.17 = (bf16[256,896]{1,0:T(8,128)(2,1)}, bf16[256,896]{1,0:T(8,128)(2,1)}, u32[]{:S(2)}, u32[]{:S(2)}) collective-permute-start(bf16[256,896]{1,0:T(8,128)(2,1)} %dynamic-slice_bitcast_fusion), channel_id=1, source_target_pairs={{0,4},{4,0},{8,12},{12,8},{1,5},{5,1},{9,13},{13,9},{2,6},{6,2},{1... | collective-permute-start | bytes 1376264 | tf_op jit(solution)/shard_map/ppermute | solution.py:23
  63.4 333.1 %reduce-scatter.21.cloned.1.call-start = ((), (), s32[]{:S(2)}) async-start(), calls=%async_computation.16 | async-start | bytes 655360 | tf_op jit(solution)/shard_map/reduce_scatter | solution.py:179
  132.7 56.8 %collective-permute-start.6 = (bf16[256,896]{1,0:T(8,128)(2,1)}, bf16[256,896]{1,0:T(8,128)(2,1)}, u32[]{:S(2)}, u32[]{:S(2)}) collective-permute-start(bf16[256,896]{1,0:T(8,128)(2,1)} %multiply_convert_fusion.25), channel_id=1, source_target_pairs={{0,8},{4,12},{8,0},{12,4},{1,9},{5,13},{9,1},{13,5},{2,10},{6,14},... | collective-permute-start | bytes 1376264 | tf_op jit(solution)/shard_map/ppermute | solution.py:23
  134.1 62.7 %collective-permute-start.4 = (bf16[256,896]{1,0:T(8,128)(2,1)}, bf16[256,896]{1,0:T(8,128)(2,1)}, u32[]{:S(2)}, u32[]{:S(2)}) collective-permute-start(bf16[256,896]{1,0:T(8,128)(2,1)} %multiply_convert_fusion.25), channel_id=1, source_target_pairs={{0,4},{4,0},{8,12},{12,8},{1,5},{5,1},{9,13},{13,9},{2,6},{6,2},{1... | collective-permute-start | bytes 1376264 | tf_op jit(solution)/shard_map/ppermute | solution.py:23
  187.0 22.4 %collective-permute-start.9 = (bf16[256,896]{1,0:T(8,128)(2,1)S(1)}, bf16[256,896]{1,0:T(8,128)(2,1)S(1)}, u32[]{:S(2)}, u32[]{:S(2)}) collective-permute-start(bf16[256,896]{1,0:T(8,128)(2,1)S(1)} %convolution_convert_fusion.13), channel_id=1, source_target_pairs={{0,12},{4,8},{8,4},{12,0},{1,13},{5,9},{9,5},{13,1},{2,14},{6,10},... | collective-permute-start | bytes 1376264 | tf_op jit(solution)/shard_map/ppermute | solution.py:23
  274.5 35.1 %collective-permute-start.14 = (bf16[256,896]{1,0:T(8,128)(2,1)}, bf16[256,896]{1,0:T(8,128)(2,1)}, u32[]{:S(2)}, u32[]{:S(2)}) collective-permute-start(bf16[256,896]{1,0:T(8,128)(2,1)} %multiply_convert_fusion.24), channel_id=1, source_target_pairs={{0,12},{4,8},{8,4},{12,0},{1,13},{5,9},{9,5},{13,1},{2,14},{6,10},... | collective-permute-start | bytes 1376264 | tf_op jit(solution)/shard_map/ppermute | solution.py:23
  275.9 24.9 %collective-permute-start.12 = (bf16[256,896]{1,0:T(8,128)(2,1)}, bf16[256,896]{1,0:T(8,128)(2,1)}, u32[]{:S(2)}, u32[]{:S(2)}) collective-permute-start(bf16[256,896]{1,0:T(8,128)(2,1)} %multiply_convert_fusion.24), channel_id=1, source_target_pairs={{0,8},{4,12},{8,0},{12,4},{1,9},{5,13},{9,1},{13,5},{2,10},{6,14},... | collective-permute-start | bytes 1376264 | tf_op jit(solution)/shard_map/ppermute | solution.py:23
  299.2 22.7 %collective-permute-start.18 = (bf16[256,896]{1,0:T(8,128)(2,1)S(1)}, bf16[256,896]{1,0:T(8,128)(2,1)S(1)}, u32[]{:S(2)}, u32[]{:S(2)}) collective-permute-start(bf16[256,896]{1,0:T(8,128)(2,1)S(1)} %fusion.136), channel_id=1, source_target_pairs={{0,4},{4,0},{8,12},{12,8},{1,5},{5,1},{9,13},{13,9},{2,6},{6,2},{1... | collective-permute-start | bytes 1376264 | tf_op jit(solution)/shard_map/ppermute | solution.py:23
  373.0 143.3 %reduce-scatter.23.cloned.1.call-start = ((), (), s32[]{:S(2)}) async-start(), calls=%async_computation.17 | async-start | bytes 655360 | tf_op jit(solution)/shard_map/reduce_scatter | solution.py:179
  403.7 27.7 %collective-permute-start.27 = (bf16[256,896]{1,0:T(8,128)(2,1)S(1)}, bf16[256,896]{1,0:T(8,128)(2,1)S(1)}, u32[]{:S(2)}, u32[]{:S(2)}) collective-permute-start(bf16[256,896]{1,0:T(8,128)(2,1)S(1)} %fusion.223), channel_id=1, source_target_pairs={{0,12},{4,8},{8,4},{12,0},{1,13},{5,9},{9,5},{13,1},{2,14},{6,10},... | collective-permute-start | bytes 1376264 | tf_op jit(solution)/shard_map/ppermute | solution.py:23
  405.2 22.4 %collective-permute-start.25 = (bf16[256,896]{1,0:T(8,128)(2,1)S(1)}, bf16[256,896]{1,0:T(8,128)(2,1)S(1)}, u32[]{:S(2)}, u32[]{:S(2)}) collective-permute-start(bf16[256,896]{1,0:T(8,128)(2,1)S(1)} %fusion.223), channel_id=1, source_target_pairs={{0,8},{4,12},{8,0},{12,4},{1,9},{5,13},{9,1},{13,5},{2,10},{6,14},... | collective-permute-start | bytes 1376264 | tf_op jit(solution)/shard_map/ppermute | solution.py:23
  490.2 76.3 %reduce-scatter.29.cloned.1.call-start = ((), (), s32[]{:S(2)}) async-start(), calls=%async_computation.22 | async-start | bytes 4587520
  508.4 110.0 %reduce-scatter.25.cloned.1.call-start = ((), (), s32[]{:S(2)}) async-start(), calls=%async_computation.20 | async-start | bytes 4587520
  534.8 125.3 %reduce-scatter.35.cloned.1.call-start = ((), (), s32[]{:S(2)}) async-start(), calls=%async_computation.25 | async-start | bytes 2451456
  542.1 157.6 %reduce-scatter.33.cloned.1.call-start = ((), (), s32[]{:S(2)}) async-start(), calls=%async_computation.24 | async-start | bytes 2451456
  548.5 213.3 %reduce-scatter.31.cloned.1.call-start = ((), (), s32[]{:S(2)}) async-start(), calls=%async_computation.23 | async-start | bytes 5935104
  581.0 241.9 %reduce-scatter.27.cloned.1.call-start = ((), (), s32[]{:S(2)}) async-start(), calls=%async_computation.21 | async-start | bytes 5935104
  633.1 294.3 %all-gather.32.cloned.1.call-start = ((), (), s32[]{:S(2)}) async-start(), calls=%async_computation.19 | async-start | bytes 2723840 | tf_op jit(solution)/shard_map/all_gather | solution.py:401
  704.2 234.5 %all-gather.30.cloned.1.call-start = ((), (), s32[]{:S(2)}) async-start(), calls=%async_computation.18 | async-start | bytes 6594560 | tf_op jit(solution)/shard_map/all_gather | solution.py:401
  841.6 25.8 %collective-permute-start.13 = (bf16[256,896]{1,0:T(8,128)(2,1)S(1)}, bf16[256,896]{1,0:T(8,128)(2,1)S(1)}, u32[]{:S(2)}, u32[]{:S(2)}) collective-permute-start(bf16[256,896]{1,0:T(8,128)(2,1)S(1)} %convolution_convert_fusion.11), channel_id=1, source_target_pairs={{0,8},{4,12},{8,0},{12,4},{1,9},{5,13},{9,1},{13,5},{2,10},{6,14},... | collective-permute-start | bytes 1376264 | tf_op jit(solution)/shard_map/ppermute | solution.py:23
  844.0 30.3 %collective-permute-start.15 = (bf16[256,896]{1,0:T(8,128)(2,1)S(1)}, bf16[256,896]{1,0:T(8,128)(2,1)S(1)}, u32[]{:S(2)}, u32[]{:S(2)}) collective-permute-start(bf16[256,896]{1,0:T(8,128)(2,1)S(1)} %convolution_convert_fusion.10), channel_id=1, source_target_pairs={{0,12},{4,8},{8,4},{12,0},{1,13},{5,9},{9,5},{13,1},{2,14},{6,10},... | collective-permute-start | bytes 1376264 | tf_op jit(solution)/shard_map/ppermute | solution.py:23
  883.7 42.2 %collective-permute-start.29 = (f32[256,896]{1,0:T(8,128)}, f32[256,896]{1,0:T(8,128)S(1)}, u32[]{:S(2)}, u32[]{:S(2)}) collective-permute-start(f32[256,896]{1,0:T(8,128)} %get-tuple-element.48), channel_id=1, source_target_pairs={{0,16},{16,0},{1,17},{17,1},{2,18},{18,2},{3,19},{19,3},{4,20},{20... | collective-permute-start | bytes 2752520 | tf_op jit(solution)/shard_map/ppermute | solution.py:18
  (157 other events, 1459.5 us)
Sparse Core Ops, SparseCore 0:
  12.3 32.4 all-gather.27
  47.0 42.1 all-gather.13
  91.4 29.5 all-gather.15
  123.1 30.1 all-gather.17
  154.8 29.2 all-gather.19
  186.2 42.0 all-gather.21
  230.0 29.5 all-gather.25
  261.2 30.1 all-gather.23
  373.1 23.3 reduce-scatter.20
  490.4 24.8 reduce-scatter.22
  518.2 48.3 reduce-scatter.28
  570.0 48.3 reduce-scatter.24
  620.7 39.3 reduce-scatter.34
  662.3 37.4 reduce-scatter.32
  701.9 59.8 reduce-scatter.30
  764.0 58.8 reduce-scatter.26
  825.1 50.6 all-gather.31
  878.1 60.6 all-gather.29

commit v2 on v1

v2 whole, which is shorter than its diff:
```python
import functools

import jax
import jax.numpy as jnp
from jax import lax
from jax.experimental import pallas as pl
from jax.experimental.pallas import tpu as pltpu
from jax.sharding import PartitionSpec as P

HEAD_DIM = 64
SECTION, CTX, FSDP = "section", "ctx", "fsdp"

epsilon = 1e-06
theta_base = 1000000.0
masked_value = -1e30

bf16 = jnp.bfloat16
f32 = jnp.float32


def swap_sections(block):
    return lax.ppermute(block, SECTION, [(0, 1), (1, 0)])


def tables(positions_row):
    half_dim = HEAD_DIM // 2
    frequency = theta_base ** (-(jnp.arange(half_dim, dtype=f32) * 2.0) / HEAD_DIM)
    angles = positions_row.astype(f32)[:, None] * frequency[None, :]
    cosine, sine = jnp.cos(angles), jnp.sin(angles)
    return (
        jnp.concatenate([cosine] * 4, axis=-1),
        jnp.concatenate([-sine, sine, -sine, sine], axis=-1),
    )


def from_peer(block, distance):
    count = lax.axis_size(CTX)
    return lax.ppermute(block, CTX, [(i, i ^ distance) for i in range(count)])


def pick(index, options):
    chosen = options[0]
    for position in range(1, len(options)):
        chosen = jnp.where(index == position, options[position], chosen)
    return chosen


MESH = pl.DeviceIdType.MESH
VMEM = pltpu.VMEM
LIMIT = 56 * 1024 * 1024


def flip(index, distance):
    place = 1
    while place <= distance:
        if (distance // place) % 2:
            index = index + place - 2 * place * ((index // place) % 2)
        place *= 2
    return index


def peer_of(distance):
    return (
        lax.axis_index(SECTION),
        flip(lax.axis_index(CTX), distance),
        lax.axis_index(FSDP),
    )


def greet(count):
    barrier = pltpu.get_barrier_semaphore()
    for k in range(1, count):
        pl.semaphore_signal(barrier, inc=1, device_id=peer_of(k), device_id_type=MESH)
    pl.semaphore_wait(barrier, count - 1)


def remote(source, target, send_sem, recv_sem, k):
    return pltpu.make_async_remote_copy(
        src_ref=source,
        dst_ref=target,
        send_sem=send_sem.at[k],
        recv_sem=recv_sem.at[k],
        device_id=peer_of(k),
        device_id_type=MESH,
    )


def matmul(left, right):
    return lax.dot_general(left, right, (((1,), (0,)), ((), ())), preferred_element_type=f32)


def matmul_nt(left, right):
    return lax.dot_general(left, right, (((1,), (1,)), ((), ())), preferred_element_type=f32)


def matmul_tn(left, right):
    return lax.dot_general(left, right, (((0,), (0,)), ((), ())), preferred_element_type=f32)


def tiles(size, step):
    return [(start, min(step, size - start)) for start in range(0, size, step)]


def row_scale(values):
    return lax.rsqrt(jnp.mean(values * values, axis=-1, keepdims=True) + epsilon)


def call(kernel, outs, scratch, cid, *args):
    return pl.pallas_call(
        kernel,
        out_shape=[jax.ShapeDtypeStruct(shape, kind) for shape, kind in outs],
        in_specs=[pl.BlockSpec(memory_space=VMEM)] * len(args),
        out_specs=[pl.BlockSpec(memory_space=VMEM)] * len(outs),
        scratch_shapes=scratch,
        compiler_params=pltpu.CompilerParams(
            collective_id=cid, has_side_effects=True, vmem_limit_bytes=LIMIT
        ),
    )(*args)


def turn_tile(values):
    lane = lax.broadcasted_iota(jnp.int32, values.shape, 1)
    width = values.shape[1]
    half = HEAD_DIM // 2
    ahead = pltpu.roll(values, width - half, 1)
    behind = pltpu.roll(values, half, 1)
    return jnp.where(lane % HEAD_DIM < half, ahead, behind)


def head_in_group(tile, head, group):
    lane = lax.broadcasted_iota(jnp.int32, tile.shape, 1)
    values = tile.astype(f32)
    moved = jnp.where(head % 2 == group, values, pltpu.roll(values, HEAD_DIM, 1))
    return jnp.where(lane // HEAD_DIM == group, moved, 0.0).astype(bf16)


def attend_kernel(
    count, x_ref, g1_ref, bias_ref, g2_ref, w_ref, cos_ref, sin_ref, kpos_ref, qpos_ref,
    normed_ref, q_ref, kv_ref, lse_ref, ctx_ref, mid_ref, low2_ref,
    mask_ref, s_ref, p_ref, vt_ref, ctxf_ref, send_sem, recv_sem,
):
    rows, width = x_ref.shape
    pair = kv_ref.shape[2] // 2
    wide = width + 2 * pair
    heads = width // HEAD_DIM
    group_size = heads // (pair // HEAD_DIM)
    greet(count)
    x = x_ref[...].astype(f32)
    normed = (x * row_scale(x) * g1_ref[...]).astype(bf16)
    normed_ref[...] = normed
    cos, sin = cos_ref[...], sin_ref[...]
    kv = matmul(normed, w_ref[:, width:wide]) + bias_ref[:, width:wide]
    keys = kv[:, :pair]
    kv_ref[0, :, :pair] = (keys * cos + turn_tile(keys) * sin).astype(bf16)
    kv_ref[0, :, pair:] = kv[:, pair:].astype(bf16)
    for k in range(1, count):
        remote(kv_ref.at[0], kv_ref.at[k], send_sem, recv_sem, k).start()
    merged = matmul(normed, w_ref[:, :width]) + bias_ref[:, :width]
    for start, size in tiles(width, 2 * HEAD_DIM):
        part = merged[:, start : start + size]
        turned_part = (part * cos + turn_tile(part) * sin) * HEAD_DIM ** (-0.5)
        q_ref[:, start : start + size] = turned_part.astype(bf16)
    for k in range(count):
        allowed = kpos_ref[k * rows : (k + 1) * rows, :] <= qpos_ref[...]
        mask_ref[k] = jnp.where(allowed, 0.0, masked_value)
    for k in range(count):
        if k:
            remote(kv_ref.at[0], kv_ref.at[k], send_sem, recv_sem, k).wait_recv()
        vt_ref[:, k * rows : (k + 1) * rows] = kv_ref[k, :, pair:].astype(f32).T.astype(bf16)

    def one_head(head, carry):
        group = head // group_size
        start = pl.multiple_of((head // 2) * (2 * HEAD_DIM), 2 * HEAD_DIM)
        tile = q_ref[:, pl.ds(start, 2 * HEAD_DIM)]
        query = head_in_group(tile, head, group)
        top = None
        for k in range(count):
            scores = matmul_nt(kv_ref[k, :, :pair], query) + mask_ref[k]
            s_ref[k] = scores
            here = jnp.max(scores, axis=0, keepdims=True)
            top = here if top is None else jnp.maximum(top, here)
        total = None
        for k in range(count):
            weight = jnp.exp(s_ref[k] - top)
            here = jnp.sum(weight, axis=0, keepdims=True)
            total = here if total is None else total + here
            p_ref[k * rows : (k + 1) * rows, :] = weight.astype(bf16)
        value_rows = vt_ref[pl.ds(pl.multiple_of(group * HEAD_DIM, HEAD_DIM), HEAD_DIM), :]
        context = matmul(value_rows, p_ref[...]) * (1.0 / total)
        place = pl.ds(pl.multiple_of(head * HEAD_DIM, HEAD_DIM), HEAD_DIM)
        ctxf_ref[place, :] = context
        lse_ref[pl.ds(head, 1), :] = top + jnp.log(total)
        return carry

    lax.fori_loop(0, heads, one_head, 0)
    context = ctxf_ref[...]
    ctx_ref[...] = context.astype(bf16)
    middle = x + matmul(context.T.astype(bf16), w_ref[:, wide:])
    mid_ref[...] = middle
    low2_ref[...] = (middle * row_scale(middle) * g2_ref[...]).astype(bf16)
    for k in range(1, count):
        remote(kv_ref.at[0], kv_ref.at[k], send_sem, recv_sem, k).wait_send()


def attend(layer, hidden, place):
    first_gain, bias, second_gain, weights = layer[:4]
    cosine, sine, key_positions, query_positions = place
    rows, width = hidden.shape
    count = lax.axis_size(CTX)
    wide = bias.shape[1]
    pair = (wide - width) // 2
    keys = count * rows
    heads = width // HEAD_DIM
    return call(
        functools.partial(attend_kernel, count),
        [
            ((rows, width), bf16),
            ((rows, width), bf16),
            ((count, rows, 2 * pair), bf16),
            ((-(-heads // 8) * 8, rows), f32),
            ((width, rows), bf16),
            ((rows, width), f32),
            ((rows, width), bf16),
        ],
        [
            VMEM((count, rows, rows), f32),
            VMEM((count, rows, rows), f32),
            VMEM((keys, rows), bf16),
            VMEM((pair, keys), bf16),
            VMEM((width, rows), f32),
            pltpu.SemaphoreType.DMA((count,)),
            pltpu.SemaphoreType.DMA((count,)),
        ],
        1,
        hidden, first_gain, bias, second_gain, weights, cosine, sine, key_positions, query_positions,
    )


def attend_back_kernel(
    count, dmid_ref, x_ref, g1_ref, w_ref, cos_ref, sin_ref, kpos_ref, qpos_ref,
    q_ref, kv_ref, lse_ref,
    dh_ref, merged_ref, gain_ref, bias_ref, low_ref,
    mask_ref, p_ref, dp_ref, ds_ref, kt_ref, dctx_ref, dq_ref, dkv_ref, out_ref, in_ref,
    send_sem, recv_sem,
):
    rows, width = x_ref.shape
    pair = kv_ref.shape[2] // 2
    wide = width + 2 * pair
    heads = width // HEAD_DIM
    group_size = heads // (pair // HEAD_DIM)
    greet(count)
    low = dmid_ref[...].astype(bf16)
    low_ref[...] = low
    dctx = matmul_nt(low, w_ref[:, wide:]).astype(bf16)
    dctx_ref[...] = dctx
    for k in range(count):
        allowed = kpos_ref[k * rows : (k + 1) * rows, :] <= qpos_ref[...]
        mask_ref[k] = jnp.where(allowed, 0.0, masked_value)
        kt_ref[:, k * rows : (k + 1) * rows] = kv_ref[k, :, :pair].astype(f32).T.astype(bf16)
    dkv_ref[...] = jnp.zeros_like(dkv_ref)

    def one_head(head, carry):
        group = head // group_size
        start = pl.multiple_of((head // 2) * (2 * HEAD_DIM), 2 * HEAD_DIM)
        query = head_in_group(q_ref[:, pl.ds(start, 2 * HEAD_DIM)], head, group)
        upstream = head_in_group(dctx_ref[:, pl.ds(start, 2 * HEAD_DIM)], head, group)
        lse = lse_ref[pl.ds(head, 1), :]
        delta = None
        for k in range(count):
            scores = matmul_nt(kv_ref[k, :, :pair], query) + mask_ref[k]
            weight = jnp.exp(scores - lse)
            weight_grad = matmul_nt(kv_ref[k, :, pair:], upstream)
            p_ref[k] = weight
            dp_ref[k] = weight_grad
            dkv_ref[k, :, pair:] += matmul(weight.astype(bf16), upstream)
            here = jnp.sum(weight * weight_grad, axis=0, keepdims=True)
            delta = here if delta is None else delta + here
        for k in range(count):
            score_grad = (p_ref[k] * (dp_ref[k] - delta)).astype(bf16)
            ds_ref[k * rows : (k + 1) * rows, :] = score_grad
            dkv_ref[k, :, :pair] += matmul(score_grad, query)
        key_rows = kt_ref[pl.ds(pl.multiple_of(group * HEAD_DIM, HEAD_DIM), HEAD_DIM), :]
        place = pl.ds(pl.multiple_of(head * HEAD_DIM, HEAD_DIM), HEAD_DIM)
        dq_ref[place, :] = matmul(key_rows, ds_ref[...]) * HEAD_DIM ** (-0.5)
        return carry

    lax.fori_loop(0, heads, one_head, 0)
    for k in range(1, count):
        out_ref[k] = dkv_ref[k].astype(bf16)
        remote(out_ref.at[k], in_ref.at[k], send_sem, recv_sem, k).start()
    cos, sin = cos_ref[...], sin_ref[...]
    dq = dq_ref[...].T

    def unturn(part):
        return (part * cos - turn_tile(part) * sin).astype(bf16)

    for start, size in tiles(width, 2 * HEAD_DIM):
        merged_ref[:, start : start + size] = unturn(dq[:, start : start + size])
    total = dkv_ref[0]
    for k in range(1, count):
        remote(out_ref.at[k], in_ref.at[k], send_sem, recv_sem, k).wait_recv()
        total = total + in_ref[k].astype(f32)
    merged_ref[:, width : width + pair] = unturn(total[:, :pair])
    merged_ref[:, width + pair :] = total[:, pair:].astype(bf16)
    merged = merged_ref[...]
    bias_ref[...] = jnp.sum(merged.astype(f32), axis=0, keepdims=True)
    normed_grad = matmul_nt(merged, w_ref[:, :wide])
    x = x_ref[...].astype(f32)
    scale = row_scale(x)
    gain_ref[...] = jnp.sum(normed_grad * x * scale, axis=0, keepdims=True)
    scaled = normed_grad * g1_ref[...]
    mean = jnp.mean(scaled * x, axis=-1, keepdims=True)
    dh_ref[...] = dmid_ref[...] + scale * scaled - x * (scale * scale * scale * mean)
    for k in range(1, count):
        remote(out_ref.at[k], in_ref.at[k], send_sem, recv_sem, k).wait_send()


def attend_back(layer, kept, middle_grad, place):
    first_gain, bias, second_gain, weights = layer[:4]
    cosine, sine, key_positions, query_positions = place
    hidden, normed, queries, every_kv, lse = kept
    rows, width = hidden.shape
    count = lax.axis_size(CTX)
    wide = bias.shape[1]
    pair = (wide - width) // 2
    keys = count * rows
    return call(
        functools.partial(attend_back_kernel, count),
        [
            ((rows, width), f32),
            ((rows, wide), bf16),
            ((1, width), f32),
            ((1, wide), f32),
            ((rows, width), bf16),
        ],
        [
            VMEM((count, rows, rows), f32),
            VMEM((count, rows, rows), f32),
            VMEM((count, rows, rows), f32),
            VMEM((keys, rows), bf16),
            VMEM((pair, keys), bf16),
            VMEM((rows, width), bf16),
            VMEM((width, rows), f32),
            VMEM((count, rows, 2 * pair), f32),
            VMEM((count, rows, 2 * pair), bf16),
            VMEM((count, rows, 2 * pair), bf16),
            pltpu.SemaphoreType.DMA((count,)),
            pltpu.SemaphoreType.DMA((count,)),
        ],
        2,
        middle_grad, hidden, first_gain, weights, cosine, sine, key_positions, query_positions,
        queries, every_kv, lse,
    )


def unit_chunks(units):
    main = units // 128 * 128
    chunks = [(start, main + start, start, size) for start, size in tiles(main, 512)]
    if units > main:
        chunks.append((2 * main, main + units, main, units - main))
    return chunks


def pack_units(gate, up):
    main = gate.shape[1] // 128 * 128
    return jnp.concatenate([gate[:, :main], up[:, :main], gate[:, main:], up[:, main:]], axis=1)


def unpack_units(packed):
    units = packed.shape[-1] // 2
    main = units // 128 * 128
    gate = jnp.concatenate([packed[..., :main], packed[..., 2 * main : main + units]], axis=-1)
    up = jnp.concatenate([packed[..., main : 2 * main], packed[..., main + units :]], axis=-1)
    return gate, up


def gate_and_up(block, expand_ref, gate_start, up_start, size):
    if size % 128:
        both = matmul(block, expand_ref[:, gate_start : up_start + size])
        return both[:, :size], both[:, size:]
    gate = matmul(block, expand_ref[:, gate_start : gate_start + size])
    return gate, matmul(block, expand_ref[:, up_start : up_start + size])


def feed_kernel(
    count, low_ref, mid_ref, expand_ref, down_ref,
    out_ref, blocks_ref, kept_gate_ref, kept_up_ref,
    act_ref, part_ref, sent_ref, got_ref, send_sem, recv_sem, send_sem2, recv_sem2,
):
    units = down_ref.shape[0]
    greet(count)
    for k in range(1, count):
        remote(low_ref, blocks_ref.at[k], send_sem, recv_sem, k).start()
    blocks_ref[0] = low_ref[...]
    for k in range(count):
        if k:
            remote(low_ref, blocks_ref.at[k], send_sem, recv_sem, k).wait_recv()
        block = blocks_ref[k]
        for gate_start, up_start, start, size in unit_chunks(units):
            gate, up = gate_and_up(block, expand_ref, gate_start, up_start, size)
            kept_gate_ref[k, :, start : start + size] = gate.astype(bf16)
            kept_up_ref[k, :, start : start + size] = up.astype(bf16)
            act_ref[:, start : start + size] = (gate / (1.0 + jnp.exp(-gate)) * up).astype(bf16)
        part = matmul(act_ref[...], down_ref[...])
        if k:
            sent_ref[k] = part.astype(bf16)
            remote(sent_ref.at[k], got_ref.at[k], send_sem2, recv_sem2, k).start()
        else:
            part_ref[...] = part
    total = mid_ref[...] + part_ref[...]
    for k in range(1, count):
        remote(sent_ref.at[k], got_ref.at[k], send_sem2, recv_sem2, k).wait_recv()
        total = total + got_ref[k].astype(f32)
    out_ref[...] = total.astype(bf16)
    for k in range(1, count):
        remote(low_ref, blocks_ref.at[k], send_sem, recv_sem, k).wait_send()
        remote(sent_ref.at[k], got_ref.at[k], send_sem2, recv_sem2, k).wait_send()


def feed(layer, second_normed, middle):
    expand_w, down_w = layer[4:]
    count = lax.axis_size(CTX)
    rows, width = second_normed.shape
    units = down_w.shape[0]
    sems = [pltpu.SemaphoreType.DMA((count,))] * 4
    return call(
        functools.partial(feed_kernel, count),
        [
            ((rows, width), bf16),
            ((count, rows, width), bf16),
            ((count, rows, units), bf16),
            ((count, rows, units), bf16),
        ],
        [
            VMEM((rows, units), bf16),
            VMEM((rows, width), f32),
            VMEM((count, rows, width), bf16),
            VMEM((count, rows, width), bf16),
        ]
        + sems,
        3,
        second_normed, middle, expand_w, down_w,
    )


def feed_back_kernel(
    count, grad_ref, mid_ref, g2_ref, blocks_ref, kept_gate_ref, kept_up_ref, expand_ref, down_ref,
    dmid_ref, gain_ref, dexpand_ref, ddown_ref,
    grads_ref, act_ref, dwide_ref, part_ref, sent_ref, got_ref,
    send_sem, recv_sem, send_sem2, recv_sem2,
):
    rows, width = grad_ref.shape
    units = down_ref.shape[0]
    greet(count)
    for k in range(1, count):
        remote(grad_ref, grads_ref.at[k], send_sem, recv_sem, k).start()
    grads_ref[0] = grad_ref[...]
    for k in range(count):
        if k:
            remote(grad_ref, grads_ref.at[k], send_sem, recv_sem, k).wait_recv()
        block = grads_ref[k]
        for gate_start, up_start, start, size in unit_chunks(units):
            cut = slice(start, start + size)
            spread = matmul_nt(block, down_ref[cut, :])
            gate = kept_gate_ref[k, :, cut].astype(f32)
            up = kept_up_ref[k, :, cut].astype(f32)
            sig = 1.0 / (1.0 + jnp.exp(-gate))
            silu = gate * sig
            act_ref[k, :, cut] = (silu * up).astype(bf16)
            dgate = (spread * up * sig * (1.0 + gate * (1.0 - sig))).astype(bf16)
            dup = (spread * silu).astype(bf16)
            if size % 128:
                dwide_ref[k, :, gate_start : up_start + size] = jnp.concatenate([dgate, dup], axis=1)
            else:
                dwide_ref[k, :, gate_start : gate_start + size] = dgate
                dwide_ref[k, :, up_start : up_start + size] = dup
        part = matmul_nt(dwide_ref[k], expand_ref[...])
        if k:
            sent_ref[k] = part.astype(bf16)
            remote(sent_ref.at[k], got_ref.at[k], send_sem2, recv_sem2, k).start()
        else:
            part_ref[...] = part
    tall = count * rows
    grads = grads_ref[...].reshape(tall, width)
    for start, size in tiles(units // 128 * 128, 384) + [(units // 128 * 128, units % 128)] * (units % 128 > 0):
        act = act_ref[:, :, start : start + size].reshape(tall, size)
        ddown_ref[start : start + size, :] = matmul_tn(act, grads).astype(bf16)
    blocks = blocks_ref[...].reshape(tall, width)
    for start, size in tiles(2 * units, 512):
        dwide = dwide_ref[:, :, start : start + size].reshape(tall, size)
        dexpand_ref[:, start : start + size] = matmul_tn(blocks, dwide).astype(bf16)
    total = part_ref[...]
    for k in range(1, count):
        remote(sent_ref.at[k], got_ref.at[k], send_sem2, recv_sem2, k).wait_recv()
        total = total + got_ref[k].astype(f32)
    middle = mid_ref[...]
    scale = row_scale(middle)
    gain_ref[...] = jnp.sum(total * middle * scale, axis=0, keepdims=True)
    scaled = total * g2_ref[...]
    mean = jnp.mean(scaled * middle, axis=-1, keepdims=True)
    dmid_ref[...] = (
        grad_ref[...].astype(f32) + scale * scaled - middle * (scale * scale * scale * mean)
    )
    for k in range(1, count):
        remote(grad_ref, grads_ref.at[k], send_sem, recv_sem, k).wait_send()
        remote(sent_ref.at[k], got_ref.at[k], send_sem2, recv_sem2, k).wait_send()


def feed_back(layer, middle, blocks, kept_gate, kept_up, grad_out):
    second_gain = layer[2]
    expand_w, down_w = layer[4:]
    count = lax.axis_size(CTX)
    rows, width = grad_out.shape
    units = down_w.shape[0]
    sems = [pltpu.SemaphoreType.DMA((count,))] * 4
    return call(
        functools.partial(feed_back_kernel, count),
        [
            ((rows, width), f32),
            ((1, width), f32),
            ((width, 2 * units), bf16),
            ((units, width), bf16),
        ],
        [
            VMEM((count, rows, width), bf16),
            VMEM((count, rows, units), bf16),
            VMEM((count, rows, 2 * units), bf16),
            VMEM((rows, width), f32),
            VMEM((count, rows, width), bf16),
            VMEM((count, rows, width), bf16),
        ]
        + sems,
        4,
        grad_out, middle, second_gain, blocks, kept_gate, kept_up, expand_w, down_w,
    )


def per_device(
    inputs,
    attend_gain,
    projections,
    biases,
    output_weight,
    mixer_gain,
    expand_weight,
    down_weight,
    positions,
    cotangent,
):
    row_count, model_width = inputs.shape[2:]
    section = lax.axis_index(SECTION)
    is_first = section == 0
    ctx = lax.axis_index(CTX)
    fsdp = lax.axis_index(FSDP)
    ctx_count = lax.axis_size(CTX)
    fsdp_count = lax.axis_size(FSDP)
    shard_rows = projections.shape[1]
    half = shard_rows // 2
    wide = projections.shape[2]
    ff_width = expand_weight.shape[2] // 2
    shard_units = down_weight.shape[1]
    units = shard_units // ctx_count
    both = (FSDP, SECTION)

    def mine(array):
        return lax.dynamic_index_in_dim(array, section, 0, keepdims=False)

    source = mine(inputs)[0]
    upstream = mine(cotangent)[0]
    key_positions = mine(positions)[0]
    query_positions = lax.dynamic_slice_in_dim(key_positions, ctx * row_count, row_count)
    cosine, sine = tables(query_positions)
    by_distance = jnp.concatenate(
        [
            lax.dynamic_slice_in_dim(key_positions, (ctx ^ k) * row_count, row_count)
            for k in range(ctx_count)
        ]
    )
    place = (cosine, sine, by_distance[:, None], query_positions[None])

    small = jnp.concatenate([attend_gain, biases, mixer_gain], axis=1)
    small = lax.all_gather(small, (SECTION, FSDP), axis=0, tiled=True).astype(f32)
    small = small.reshape(2, fsdp_count, -1)
    bias_part = biases.shape[1]

    def small_of(layer):
        rows = small[layer]
        return (
            rows[:, :shard_rows].reshape(1, -1),
            rows[:, shard_rows : shard_rows + bias_part].reshape(1, -1),
            rows[:, shard_rows + bias_part :].reshape(1, -1),
        )

    attn_shard = jnp.concatenate([projections[0], output_weight[0]], axis=1)

    def unit_columns(side):
        pieces = []
        for shard in range(fsdp_count):
            start = side * ff_width + shard * shard_units
            pieces.append(
                pick(
                    ctx,
                    [
                        expand_weight[0, :, start + k * units : start + (k + 1) * units]
                        for k in range(ctx_count)
                    ],
                )
            )
        return jnp.concatenate(pieces, axis=1)

    expand_shard = pack_units(unit_columns(0), unit_columns(1))
    down_shard = lax.dynamic_slice_in_dim(down_weight[0], ctx * units, units)

    def halves(array):
        size = array.shape[0] // 2
        low, high = array[:size], array[size:]
        own = jnp.where(is_first, low, high)
        other = swap_sections(jnp.where(is_first, high, low))
        return jnp.where(is_first, own, other), jnp.where(is_first, other, own)

    attn_pair = halves(attn_shard)
    expand_pair = halves(expand_shard)
    down_pair = halves(down_shard)

    def gather(piece):
        return lax.all_gather(piece, both, axis=0, tiled=True)

    layers = []
    for layer in range(2):
        layers.append(
            small_of(layer)
            + (
                gather(attn_pair[layer]),
                gather(expand_pair[layer]),
                gather(down_pair[layer]),
            )
        )

    hidden = source
    stored = []
    sent = []
    for layer in range(2):
        normed, queries, every_kv, lse, context, middle, second_normed = attend(
            layers[layer], hidden, place
        )
        kept = (hidden, normed, queries, every_kv, lse, context)
        hidden, blocks, kept_gate, kept_up = feed(layers[layer], second_normed, middle)
        sent.append(hidden)
        stored.append((middle, kept, blocks, kept_gate, kept_up))

    chain = []

    def scatter(array):
        if chain:
            array = lax.optimization_barrier((array, chain[-1]))[0]
        chain.append(lax.psum_scatter(array, both, scatter_dimension=0, tiled=True))
        return chain[-1]

    def from_peers(array):
        return [array] + [from_peer(array, k) for k in range(1, ctx_count)]

    def ctx_sum(array):
        size = array.shape[1] // ctx_count
        total = None
        for k in range(ctx_count):
            cut = lax.dynamic_slice_in_dim(array, (ctx ^ k) * size, size, axis=1)
            cut = (from_peer(cut, k) if k else cut).astype(f32)
            total = cut if total is None else total + cut
        return total.astype(bf16)

    grad = upstream
    hidden_grads = [None, None]
    small_grads = [None, None]
    down_parts = [None, None]
    expand_parts = [None, None]
    attn_parts = [None, None]
    waiting = None
    for layer in (1, 0):
        middle, kept, blocks, kept_gate, kept_up = stored[layer]
        middle_grad, second_grad, expand_grad, down_grad = feed_back(
            layers[layer], middle, blocks, kept_gate, kept_up, grad
        )
        down_parts[layer] = from_peers(scatter(down_grad))
        if waiting is not None:
            expand_grad = jnp.concatenate([expand_grad, waiting], axis=1)
        part = scatter(expand_grad)
        if waiting is not None:
            attn_parts[1] = from_peers(part[:, 2 * units * fsdp_count :])
            part = part[:, : 2 * units * fsdp_count]
        expand_parts[layer] = from_peers(part)
        hidden_grad, merged_grad, first_grad, offset_grad, middle_low = attend_back(
            layers[layer], kept[:5], middle_grad, place
        )
        attn_grad = jnp.concatenate(
            [
                jnp.einsum("rd,rf->df", kept[1], merged_grad, preferred_element_type=f32),
                jnp.dot(kept[5], middle_low, preferred_element_type=f32),
            ],
            axis=1,
        ).astype(bf16)
        waiting = ctx_sum(attn_grad)
        small_grads[layer] = jnp.concatenate([first_grad, offset_grad, second_grad], axis=1)[0]
        hidden_grads[layer] = hidden_grad
        grad = hidden_grad.astype(bf16)
    attn_parts[0] = from_peers(scatter(waiting))

    def finish(parts):
        own = [jnp.where(is_first, low, high) for low, high in zip(*parts)]
        other = [swap_sections(jnp.where(is_first, high, low)) for low, high in zip(*parts)]
        whole = [
            jnp.concatenate(
                [jnp.where(is_first, one, two), jnp.where(is_first, two, one)], axis=0
            )
            for one, two in zip(own, other)
        ]
        return [pick(ctx ^ k, whole) for k in range(ctx_count)]

    down_all = finish(down_parts)
    expand_all = [unpack_units(array) for array in finish(expand_parts)]
    attn_all = jnp.concatenate(finish(attn_parts), axis=1).astype(f32)
    grad_down = jnp.concatenate(down_all, axis=0).astype(f32)[None]
    columns = [
        expand_all[k][side][:, shard * units : (shard + 1) * units]
        for side in range(2)
        for shard in range(fsdp_count)
        for k in range(ctx_count)
    ]
    grad_expand = jnp.concatenate(columns, axis=1).astype(f32)[None]
    grad_projections = attn_all[:, :wide][None]
    grad_output = attn_all[:, wide:][None]

    small_all = lax.psum(jnp.stack(small_grads), (CTX, FSDP, SECTION))
    small_own = mine(small_all)
    first_all, offset_all, second_all = (
        small_own[:model_width],
        small_own[model_width : model_width + wide],
        small_own[model_width + wide :],
    )
    pair_width = (wide - model_width) // 2

    def part(vector):
        size = vector.shape[0] // fsdp_count
        return lax.dynamic_slice_in_dim(vector, fsdp * size, size)[None]

    def from_both(pair):
        own = jnp.where(is_first, pair[0], pair[1])
        other = swap_sections(jnp.where(is_first, pair[1], pair[0]))
        return jnp.stack(
            [jnp.where(is_first, own, other), jnp.where(is_first, other, own)]
        )[None, :, None]

    activations = from_both(sent)
    input_grads = from_both([hidden_grads[0], hidden_grads[1].astype(bf16).astype(f32)])
    return (
        activations,
        input_grads,
        part(first_all),
        grad_projections,
        part(offset_all[: model_width + pair_width]),
        part(offset_all[model_width + pair_width :]),
        grad_output,
        part(second_all),
        grad_expand,
        grad_down,
    )


def solution(mesh):
    return jax.shard_map(
        per_device,
        mesh=mesh,
        in_specs=(
            P(None, FSDP, CTX, None),
            P(SECTION, FSDP),
            P(SECTION, FSDP, None),
            P(SECTION, FSDP),
            P(SECTION, FSDP, None),
            P(SECTION, FSDP),
            P(SECTION, FSDP, None),
            P(SECTION, FSDP, None),
            P(None, FSDP, None),
            P(None, FSDP, CTX, None),
        ),
        out_specs=(
            P(SECTION, None, FSDP, CTX, None),
            P(SECTION, None, FSDP, CTX, None),
            P(SECTION, FSDP),
            P(SECTION, FSDP, None),
            P(SECTION, FSDP),
            P(SECTION, FSDP),
            P(SECTION, FSDP, None),
            P(SECTION, FSDP),
            P(SECTION, FSDP, None),
            P(SECTION, FSDP, None),
        ),
        check_vma=False,
    )
```

time: 980 us -> 813 us (0.83)
  Pallas kernels: 0 us -> 319 us
  matrix products: 245 us -> 4.01 us
  waiting for transfers between devices: 406 us -> 224 us
  local copies, waits for them, and re-layouts: 94.3 us -> 30.7 us
  other arithmetic: 89.1 us -> 65.1 us
  blocking collectives: 84.8 us -> 105 us
    pallas_call x0 -> x8, Pallas kernels: none -> 319 us  [call(): pl.pallas_call(kernel, out_shape=[jax.ShapeDtypeStruct(shape, kind) for s...]
    dot_general x86 -> x4, matrix products: 221 us -> 4.01 us  [the longest x2 2.38 us: per_device(): jnp.dot(kept[5], middle_low, preferred_element_type=f32)]
    unnamed x24 -> x13, waiting for transfers between devices: 216 us -> 40 us
    unnamed x287 -> x71, local copies, waits for them, and re-layouts: 43.8 us -> 2.52 us
    psum x1, blocking collectives: 38.5 us -> 79.7 us  [per_device(): small_all = lax.psum(jnp.stack(small_grads), (CTX, FSDP, SECTION))]
    sub x4 -> x0, matrix products: 23.7 us -> none  [attend(): exponent = jnp.exp(masked - row_max)]
    all_gather x8 -> x6, waiting for transfers between devices: 71.9 us -> 95.1 us  [gather(): return lax.all_gather(piece, both, axis=0, tiled=True)]
    all_gather x2 -> x0, blocking collectives: 22.1 us -> none  [attend(): every_kv = lax.all_gather(local_kv, CTX, axis=0, tiled=True)]
  transfers between devices with their start and end apart: 50 -> 52, of which waited for: 31 -> 21; matrix products, arithmetic and copies ran while one was open for 31% -> 11% of each run, Pallas kernels for 0% -> 27%
where the time goes in v2:
time: 813 us; the launch traced here: 806 us
  Pallas kernels  319 us (39%)
  waiting for transfers between devices  224 us (28%)
  blocking collectives  105 us (13%)
  other arithmetic  65.1 us (8%)
  starting transfers between devices  42.3 us (5%)
  local copies, waits for them, and re-layouts  30.7 us (4%)
  between operations  15.4 us (2%)
    pallas_call x8, Pallas kernels, call(): pl.pallas_call(kernel, out_shape=[jax.ShapeDtypeStruct(shape, kind) for s...  319 us
    all_gather x6, waiting for transfers between devices, gather(): return lax.all_gather(piece, both, axis=0, tiled=True)  95.1 us
    ppermute x24, waiting for transfers between devices, from_peer(): return lax.ppermute(block, CTX, [(i, i ^ distance) for i in range(count)])  82.9 us
    psum x1, blocking collectives, per_device(): small_all = lax.psum(jnp.stack(small_grads), (CTX, FSDP, SECTION))  79.7 us
    unnamed x13, waiting for transfers between devices  40 us
    ppermute x24, starting transfers between devices, from_peer(): return lax.ppermute(block, CTX, [(i, i ^ distance) for i in range(count)])  34.2 us
    all_gather x1, blocking collectives, per_device(): lax.all_gather(small, (SECTION, FSDP), axis=0, tiled=True).astype(f32)  25.5 us
  transfers between devices with their start and end apart: 52, of which 21 were waited for; matrix products, arithmetic and copies ran while one was open for 11% of the time, Pallas kernels for 27%

profile of v2, /device:TPU:0, one launch (start us, length us, event | category | flops | bytes accessed | tf_op | source)
XLA Modules:
  0.0 805.9 jit_solution(625077909205122385)
XLA Ops:
  10.8 2.6 broadcast_select_fusion.20
  16.2 3.2 select_bitcast_fusion.10
  19.5 3.1 select_bitcast_fusion.9
  31.2 25.5 %all-gather = bf16[8,1,736]{2,1,0:T(2,128)(2,1)S(1)} all-gather(bf16[1,1,736]{2,1,0:T(2,128)(2,1)S(1)} %maximum_bitcast_fusion.2), channel_id=1, replica_groups=mesh['section'=2,'ctx'=4,'fsdp'=4] {'section','fsdp'}, dimensions={0}, use_global_device_ids=true | all-gather | bytes 13248 | tf_op jit(solution)/shard_map/all_gather | solution.py:582
  64.1 28.0 %shard_map.177 = (bf16[256,896]{1,0:T(8,128)(2,1)}, bf16[256,896]{1,0:T(8,128)(2,1)}, bf16[4,256,256]{2,1,0:T(8,128)(2,1)}, f32[16,256]{1,0:T(8,128)}, bf16[896,...) custom-call(bf16[256,896]{1,0:T(8,128)(2,1)} %dynamic-slice_bitcast_fusion.1.x_ref, ...), custom_call_target="tpu_custom_call" | custom-call | tf_op jit(solution)/shard_map/pallas_call | solution.py:109
  92.1 47.9 %all-gather.10.cloned.1.call-done.expand_ref = bf16[896,2432]{1,0:T(8,128)(2,1)} async-done(((bf16[112,2432]{1,0:T(8,128)(2,1)}), bf16[896,2432]{1,0:T(8,128)(2,1)}) %all-gather.10.cloned.1.call-update) | async-done | bytes 4358160 | tf_op jit(solution)/shard_map/all_gather | solution.py:626
  140.0 49.7 %shard_map.178 = (bf16[256,896]{1,0:T(8,128)(2,1)}, bf16[4,256,896]{2,1,0:T(8,128)(2,1)}, bf16[4,256,1216]{2,1,0:T(8,128)(2,1)}, bf16[4,256,1216]{2,1,0:T(8,128)(2,1)}) custom-call(bf16[256,896]{1,0:T(8,128)(2,1)} %get-tuple-element.54.low_ref, f32[256,896]{1,0:T(8,128)} %get-tuple-element.55.mid_ref, ...), custom_call_target="tpu_custom_call" | custom-call | tf_op jit(solution)/shard_map/pallas_call | solution.py:109
  189.8 27.1 %shard_map.179 = (bf16[256,896]{1,0:T(8,128)(2,1)}, bf16[256,896]{1,0:T(8,128)(2,1)}, bf16[4,256,256]{2,1,0:T(8,128)(2,1)}, f32[16,256]{1,0:T(8,128)}, bf16[896,...) custom-call(bf16[256,896]{1,0:T(8,128)(2,1)} %get-tuple-element.56.x_ref, ...), custom_call_target="tpu_custom_call" | custom-call | tf_op jit(solution)/shard_map/pallas_call | solution.py:109
  216.9 47.1 %all-gather.16.cloned.1.call-done.expand_ref = bf16[896,2432]{1,0:T(8,128)(2,1)} async-done(((bf16[112,2432]{1,0:T(8,128)(2,1)}), bf16[896,2432]{1,0:T(8,128)(2,1)}) %all-gather.16.cloned.1.call-update) | async-done | bytes 4358160 | tf_op jit(solution)/shard_map/all_gather | solution.py:626
  264.1 49.7 %shard_map.180 = (bf16[256,896]{1,0:T(8,128)(2,1)}, bf16[4,256,896]{2,1,0:T(8,128)(2,1)}, bf16[4,256,1216]{2,1,0:T(8,128)(2,1)}, bf16[4,256,1216]{2,1,0:T(8,128)(2,1)}) custom-call(bf16[256,896]{1,0:T(8,128)(2,1)} %get-tuple-element.57.low_ref, f32[256,896]{1,0:T(8,128)} %get-tuple-element.58.mid_ref, ...), custom_call_target="tpu_custom_call" | custom-call | tf_op jit(solution)/shard_map/pallas_call | solution.py:109
  313.7 51.3 %shard_map.181 = (f32[256,896]{1,0:T(8,128)}, f32[1,896]{1,0:T(1,128)}, bf16[896,2432]{1,0:T(8,128)(2,1)}, bf16[1216,896]{1,0:T(8,128)(2,1)}) custom-call(bf16[256,896]{1,0:T(8,128)(2,1)} %dynamic-slice_bitcast_fusion.grad_ref, f32[256,896]{1,0:T(8,128)} %get-tuple-element.58.mid_ref, f32[1,896]{1,0:T(1,128)} %reshape.874.g2_ref, ...), custom_call_target="tpu_custom_call" | custom-call | tf_op jit(solution)/shard_map/pallas_call | solution.py:109
  365.1 38.3 %reduce-scatter.16.cloned.1.call-done = bf16[152,896]{1,0:T(8,128)(2,1)} async-done(((bf16[1216,896]{1,0:T(8,128)(2,1)}), bf16[152,896]{1,0:T(8,128)(2,1)}) %reduce-scatter.16.cloned.1.call-update) | async-done | bytes 272400
  403.4 31.7 %shard_map.182 = (f32[256,896]{1,0:T(8,128)}, bf16[256,1152]{1,0:T(8,128)(2,1)}, f32[1,896]{1,0:T(1,128)}, f32[1,1152]{1,0:T(1,128)}, bf16[256,896]{1,0:T(8,128)(2,1)}) custom-call(f32[256,896]{1,0:T(8,128)} %get-tuple-element.63.dmid_ref, bf16[256,896]{1,0:T(8,128)(2,1)} %get-tuple-element.56.x_ref, f32[1,896]{1,0:T(1,128)} %reshape.872.g1_ref, ...), custom_call_target="tpu_custom_call" | custom-call | tf_op jit(solution)/shard_map/pallas_call | solution.py:109
  437.1 48.2 %shard_map.183 = (f32[256,896]{1,0:T(8,128)}, f32[1,896]{1,0:T(1,128)}, bf16[896,2432]{1,0:T(8,128)(2,1)}, bf16[1216,896]{1,0:T(8,128)(2,1)}) custom-call(bf16[256,896]{1,0:T(8,128)(2,1)} %convert_element_type.74.grad_ref, f32[256,896]{1,0:T(8,128)} %get-tuple-element.55.mid_ref, f32[1,896]{1,0:T(1,128)} %reshape.871.g2_ref, ...), custom_call_target="tpu_custom_call" | custom-call | tf_op jit(solution)/shard_map/pallas_call | solution.py:109
  488.0 2.4 fusion.2
  493.8 21.0 %collective-permute-done.10 = bf16[896,512]{1,0:T(8,128)(2,1)} collective-permute-done((bf16[896,512]{1,0:T(8,128)(2,1)}, bf16[896,512]{1,0:T(8,128)(2,1)}, u32[]{:S(2)}, u32[]{:S(2)}) %collective-permute-start.10) | collective-permute-done | bytes 917536 | tf_op jit(solution)/shard_map/ppermute | solution.py:38
  514.8 13.9 %collective-permute-done.8 = bf16[896,512]{1,0:T(8,128)(2,1)} collective-permute-done((bf16[896,512]{1,0:T(8,128)(2,1)}, bf16[896,512]{1,0:T(8,128)(2,1)}, u32[]{:S(2)}, u32[]{:S(2)}) %collective-permute-start.8) | collective-permute-done | bytes 917536 | tf_op jit(solution)/shard_map/ppermute | solution.py:38
  528.8 2.4 add_convert_fusion
  531.2 5.0 pad_maximum_fusion
  536.3 33.3 %shard_map.184 = (f32[256,896]{1,0:T(8,128)}, bf16[256,1152]{1,0:T(8,128)(2,1)}, f32[1,896]{1,0:T(1,128)}, f32[1,1152]{1,0:T(1,128)}, bf16[256,896]{1,0:T(8,128)(2,1)}) custom-call(f32[256,896]{1,0:T(8,128)} %get-tuple-element.71.dmid_ref, bf16[256,896]{1,0:T(8,128)(2,1)} %dynamic-slice_bitcast_fusion.1.x_ref, f32[1,896]{1,0:T(1,128)} %reshape.869.g1_ref, ...), custom_call_target="tpu_custom_call" | custom-call | tf_op jit(solution)/shard_map/pallas_call | solution.py:109
  578.2 79.7 %psum.7 = f32[2,2944]{1,0:T(2,128)S(1)} all-reduce(f32[2,2944]{1,0:T(2,128)S(1)} %maximum_maximum_fusion), channel_id=1, replica_groups=mesh['section'=2,'ctx'=4,'fsdp'=4] {'ctx','fsdp','section'}, use_global_device_ids=true, to_apply=%region_0.1 | all-reduce | flops 5888 | bytes 47104 | tf_op jit(solution)/shard_map/psum | solution.py:732
  665.5 3.4 add_convert_fusion.1
  670.6 2.4 collective-permute-start.32
  681.1 2.4 collective-permute-start.22
  683.5 3.4 collective-permute-done.31
  689.2 3.6 collective-permute-done.35
  695.1 13.9 %collective-permute-done.34 = bf16[152,896]{1,0:T(8,128)(2,1)S(1)} collective-permute-done((bf16[152,896]{1,0:T(8,128)(2,1)S(1)}, bf16[152,896]{1,0:T(8,128)(2,1)S(1)}, u32[]{:S(2)}, u32[]{:S(2)}) %collective-permute-start.34) | collective-permute-done | bytes 272416 | tf_op jit(solution)/shard_map/ppermute | solution.py:38
  726.4 12.1 %collective-permute-done.21 = bf16[112,2432]{1,0:T(8,128)(2,1)} collective-permute-done((bf16[112,2432]{1,0:T(8,128)(2,1)}, bf16[112,2432]{1,0:T(8,128)(2,1)}, u32[]{:S(2)}, u32[]{:S(2)}) %collective-permute-start.21) | collective-permute-done | bytes 544800 | tf_op jit(solution)/shard_map/ppermute | solution.py:38
  739.7 9.9 %collective-permute-done.24 = bf16[112,2432]{1,0:T(8,128)(2,1)S(1)} collective-permute-done((bf16[112,2432]{1,0:T(8,128)(2,1)}, bf16[112,2432]{1,0:T(8,128)(2,1)S(1)}, u32[]{:S(2)}, u32[]{:S(2)}) %collective-permute-start.24) | collective-permute-done | bytes 544800 | tf_op jit(solution)/shard_map/ppermute | solution.py:38
  763.0 3.0 collective-permute-start.20
  770.3 10.3 %concatenate.354 = bf16[1,224,9728]{2,1,0:T(8,128)(2,1)} concatenate(bf16[1,224,304]{2,1,0:T(8,128)(2,1)} %get-tuple-element.209, bf16[1,224,304]{2,1,0:T(8,128)(2,1)} %get-tuple-element.203, bf16[1,224,304]{2,1,0:T(8,128)(2,1)} %get-tuple-element.197, bf16[1,224,304]{2,1,0:T(8,128)(2,1)} %get-tuple-element.191, bf16[1,224,304]{2,1,0:T(8,128)(2,1)} %get-tuple-element.208, ...), dimensions={2} | concatenate | bytes 8716288 | tf_op jit(solution)/shard_map/concatenate | solution.py:728
  780.6 6.8 convert_element_type.87
  (280 shorter events, 108.3 us)
Async XLA Ops:
  7.2 56.9 %all-gather.8.cloned.1.call-start = ((), (), s32[]{:S(2)}) async-start(), calls=%async_computation.5 | async-start | bytes 4128768 | tf_op jit(solution)/shard_map/all_gather | solution.py:626
  13.4 78.7 %all-gather.12.cloned.1.call-start = ((), (), s32[]{:S(2)}) async-start(), calls=%async_computation.7 | async-start | bytes 2451456 | tf_op jit(solution)/shard_map/all_gather | solution.py:626
  16.2 123.9 %all-gather.10.cloned.1.call-start = ((), (), s32[]{:S(2)}) async-start(), calls=%async_computation.6 | async-start | bytes 4902912 | tf_op jit(solution)/shard_map/all_gather | solution.py:626
  28.2 161.6 %all-gather.14.cloned.1.call-start = ((), (), s32[]{:S(2)}) async-start(), calls=%async_computation.8 | async-start | bytes 4128768 | tf_op jit(solution)/shard_map/all_gather | solution.py:626
  28.8 188.2 %all-gather.18.cloned.1.call-start = ((), (), s32[]{:S(2)}) async-start(), calls=%async_computation.10 | async-start | bytes 2451456 | tf_op jit(solution)/shard_map/all_gather | solution.py:626
  29.3 234.7 %all-gather.16.cloned.1.call-start = ((), (), s32[]{:S(2)}) async-start(), calls=%async_computation.9 | async-start | bytes 4902912 | tf_op jit(solution)/shard_map/all_gather | solution.py:626
  29.9 373.4 %reduce-scatter.16.cloned.1.call-start = ((), (), s32[]{:S(2)}) async-start(), calls=%async_computation.14 | async-start | bytes 2451456
  365.0 120.3 %reduce-scatter.10.cloned.1.call-start = ((), (), s32[]{:S(2)}) async-start(), calls=%async_computation.11 | async-start | bytes 4902912 | tf_op jit(solution)/shard_map/reduce_scatter | solution.py:656
  403.4 132.8 %reduce-scatter.18.cloned.1.call-start = ((), (), s32[]{:S(2)}) async-start(), calls=%async_computation.15 | async-start | bytes 2451456
  485.4 228.5 %reduce-scatter.12.cloned.1.call-start = ((), (), s32[]{:S(2)}) async-start(), calls=%async_computation.12 | async-start | bytes 5935104 | tf_op jit(solution)/shard_map/reduce_scatter | solution.py:656
  490.3 24.5 %collective-permute-start.10 = (bf16[896,512]{1,0:T(8,128)(2,1)}, bf16[896,512]{1,0:T(8,128)(2,1)}, u32[]{:S(2)}, u32[]{:S(2)}) collective-permute-start(bf16[896,512]{1,0:T(8,128)(2,1)} %get-tuple-element.148), channel_id=1, source_target_pairs={{0,12},{4,8},{8,4},{12,0},{1,13},{5,9},{9,5},{13,1},{2,14},{6,10},... | collective-permute-start | bytes 2752520 | tf_op jit(solution)/shard_map/ppermute | solution.py:38
  492.6 36.2 %collective-permute-start.8 = (bf16[896,512]{1,0:T(8,128)(2,1)}, bf16[896,512]{1,0:T(8,128)(2,1)}, u32[]{:S(2)}, u32[]{:S(2)}) collective-permute-start(bf16[896,512]{1,0:T(8,128)(2,1)} %get-tuple-element.146), channel_id=1, source_target_pairs={{0,4},{4,0},{8,12},{12,8},{1,5},{5,1},{9,13},{13,9},{2,6},{6,2},{1... | collective-permute-start | bytes 2752520 | tf_op jit(solution)/shard_map/ppermute | solution.py:38
  493.2 35.5 %collective-permute-start.9 = (bf16[896,512]{1,0:T(8,128)(2,1)S(1)}, bf16[896,512]{1,0:T(8,128)(2,1)}, u32[]{:S(2)}, u32[]{:S(2)}) collective-permute-start(bf16[896,512]{1,0:T(8,128)(2,1)S(1)} %get-tuple-element.147), channel_id=1, source_target_pairs={{0,8},{4,12},{8,0},{12,4},{1,9},{5,13},{9,1},{13,5},{2,10},{6,14},... | collective-permute-start | bytes 2752520 | tf_op jit(solution)/shard_map/ppermute | solution.py:38
  536.2 226.8 %reduce-scatter.14.cloned.1.call-start = ((), (), s32[]{:S(2)}) async-start(), calls=%async_computation.13 | async-start | bytes 1032192 | tf_op jit(solution)/shard_map/reduce_scatter | solution.py:656
  574.7 90.2 %collective-permute-start.5 = (bf16[896,512]{1,0:T(8,128)(2,1)}, bf16[896,512]{1,0:T(8,128)(2,1)}, u32[]{:S(2)}, u32[]{:S(2)}) collective-permute-start(bf16[896,512]{1,0:T(8,128)(2,1)} %get-tuple-element.149), channel_id=1, source_target_pairs={{0,4},{4,0},{8,12},{12,8},{1,5},{5,1},{9,13},{13,9},{2,6},{6,2},{1... | collective-permute-start | bytes 2752520 | tf_op jit(solution)/shard_map/ppermute | solution.py:38
  576.0 88.9 %collective-permute-start.6 = (bf16[896,512]{1,0:T(8,128)(2,1)}, bf16[896,512]{1,0:T(8,128)(2,1)}, u32[]{:S(2)}, u32[]{:S(2)}) collective-permute-start(bf16[896,512]{1,0:T(8,128)(2,1)} %get-tuple-element.150), channel_id=1, source_target_pairs={{0,8},{4,12},{8,0},{12,4},{1,9},{5,13},{9,1},{13,5},{2,10},{6,14},... | collective-permute-start | bytes 2752520 | tf_op jit(solution)/shard_map/ppermute | solution.py:38
  577.5 87.4 %collective-permute-start.7 = (bf16[896,512]{1,0:T(8,128)(2,1)}, bf16[896,512]{1,0:T(8,128)(2,1)}, u32[]{:S(2)}, u32[]{:S(2)}) collective-permute-start(bf16[896,512]{1,0:T(8,128)(2,1)} %get-tuple-element.151), channel_id=1, source_target_pairs={{0,12},{4,8},{8,4},{12,0},{1,13},{5,9},{9,5},{13,1},{2,14},{6,10},... | collective-permute-start | bytes 2752520 | tf_op jit(solution)/shard_map/ppermute | solution.py:38
  670.6 10.5 %collective-permute-start.32 = (bf16[152,896]{1,0:T(8,128)(2,1)S(1)}, bf16[152,896]{1,0:T(8,128)(2,1)S(1)}, u32[]{:S(2)}, u32[]{:S(2)}) collective-permute-start(bf16[152,896]{1,0:T(8,128)(2,1)S(1)} %copy-done.10), channel_id=1, source_target_pairs={{0,12},{4,8},{8,4},{12,0},{1,13},{5,9},{9,5},{13,1},{2,14},{6,10},... | collective-permute-start | bytes 817160 | tf_op jit(solution)/shard_map/ppermute | solution.py:38
  673.0 13.8 %collective-permute-start.31 = (bf16[152,896]{1,0:T(8,128)(2,1)S(1)}, bf16[152,896]{1,0:T(8,128)(2,1)S(1)}, u32[]{:S(2)}, u32[]{:S(2)}) collective-permute-start(bf16[152,896]{1,0:T(8,128)(2,1)S(1)} %copy-done.11), channel_id=1, source_target_pairs={{0,12},{4,8},{8,4},{12,0},{1,13},{5,9},{9,5},{13,1},{2,14},{6,10},... | collective-permute-start | bytes 817160 | tf_op jit(solution)/shard_map/ppermute | solution.py:38
  674.9 17.8 %collective-permute-start.35 = (bf16[152,896]{1,0:T(8,128)(2,1)S(1)}, bf16[152,896]{1,0:T(8,128)(2,1)S(1)}, u32[]{:S(2)}, u32[]{:S(2)}) collective-permute-start(bf16[152,896]{1,0:T(8,128)(2,1)S(1)} %copy-done.10), channel_id=1, source_target_pairs={{0,8},{4,12},{8,0},{12,4},{1,9},{5,13},{9,1},{13,5},{2,10},{6,14},... | collective-permute-start | bytes 817160 | tf_op jit(solution)/shard_map/ppermute | solution.py:38
  677.2 32.5 %collective-permute-start.38 = (bf16[152,896]{1,0:T(8,128)(2,1)S(1)}, bf16[152,896]{1,0:T(8,128)(2,1)S(1)}, u32[]{:S(2)}, u32[]{:S(2)}) collective-permute-start(bf16[152,896]{1,0:T(8,128)(2,1)S(1)} %copy-done.10), channel_id=1, source_target_pairs={{0,4},{4,0},{8,12},{12,8},{1,5},{5,1},{9,13},{13,9},{2,6},{6,2},{1... | collective-permute-start | bytes 817160 | tf_op jit(solution)/shard_map/ppermute | solution.py:38
  677.9 31.1 %collective-permute-start.34 = (bf16[152,896]{1,0:T(8,128)(2,1)S(1)}, bf16[152,896]{1,0:T(8,128)(2,1)S(1)}, u32[]{:S(2)}, u32[]{:S(2)}) collective-permute-start(bf16[152,896]{1,0:T(8,128)(2,1)S(1)} %copy-done.11), channel_id=1, source_target_pairs={{0,8},{4,12},{8,0},{12,4},{1,9},{5,13},{9,1},{13,5},{2,10},{6,14},... | collective-permute-start | bytes 817160 | tf_op jit(solution)/shard_map/ppermute | solution.py:38
  681.1 43.5 %collective-permute-start.22 = (bf16[112,2432]{1,0:T(8,128)(2,1)S(1)}, bf16[112,2432]{1,0:T(8,128)(2,1)}, u32[]{:S(2)}, u32[]{:S(2)}) collective-permute-start(bf16[112,2432]{1,0:T(8,128)(2,1)S(1)} %copy-done.8), channel_id=1, source_target_pairs={{0,12},{4,8},{8,4},{12,0},{1,13},{5,9},{9,5},{13,1},{2,14},{6,10},... | collective-permute-start | bytes 1634312 | tf_op jit(solution)/shard_map/ppermute | solution.py:38
  686.9 25.2 %collective-permute-start.37 = (bf16[152,896]{1,0:T(8,128)(2,1)S(1)}, bf16[152,896]{1,0:T(8,128)(2,1)S(1)}, u32[]{:S(2)}, u32[]{:S(2)}) collective-permute-start(bf16[152,896]{1,0:T(8,128)(2,1)S(1)} %copy-done.11), channel_id=1, source_target_pairs={{0,4},{4,0},{8,12},{12,8},{1,5},{5,1},{9,13},{13,9},{2,6},{6,2},{1... | collective-permute-start | bytes 817160 | tf_op jit(solution)/shard_map/ppermute | solution.py:38
  692.8 46.9 %collective-permute-start.25 = (bf16[112,2432]{1,0:T(8,128)(2,1)S(1)}, bf16[112,2432]{1,0:T(8,128)(2,1)}, u32[]{:S(2)}, u32[]{:S(2)}) collective-permute-start(bf16[112,2432]{1,0:T(8,128)(2,1)S(1)} %copy-done.8), channel_id=1, source_target_pairs={{0,8},{4,12},{8,0},{12,4},{1,9},{5,13},{9,1},{13,5},{2,10},{6,14},... | collective-permute-start | bytes 1634312 | tf_op jit(solution)/shard_map/ppermute | solution.py:38
  709.7 41.1 %collective-permute-start.28 = (bf16[112,2432]{1,0:T(8,128)(2,1)S(1)}, bf16[112,2432]{1,0:T(8,128)(2,1)}, u32[]{:S(2)}, u32[]{:S(2)}) collective-permute-start(bf16[112,2432]{1,0:T(8,128)(2,1)S(1)} %copy-done.8), channel_id=1, source_target_pairs={{0,4},{4,0},{8,12},{12,8},{1,5},{5,1},{9,13},{13,9},{2,6},{6,2},{1... | collective-permute-start | bytes 1634312 | tf_op jit(solution)/shard_map/ppermute | solution.py:38
  719.8 18.6 %collective-permute-start.21 = (bf16[112,2432]{1,0:T(8,128)(2,1)}, bf16[112,2432]{1,0:T(8,128)(2,1)}, u32[]{:S(2)}, u32[]{:S(2)}) collective-permute-start(bf16[112,2432]{1,0:T(8,128)(2,1)} %get-tuple-element.220), channel_id=1, source_target_pairs={{0,12},{4,8},{8,4},{12,0},{1,13},{5,9},{9,5},{13,1},{2,14},{6,10},... | collective-permute-start | bytes 1634312 | tf_op jit(solution)/shard_map/ppermute | solution.py:38
  724.3 25.3 %collective-permute-start.24 = (bf16[112,2432]{1,0:T(8,128)(2,1)}, bf16[112,2432]{1,0:T(8,128)(2,1)S(1)}, u32[]{:S(2)}, u32[]{:S(2)}) collective-permute-start(bf16[112,2432]{1,0:T(8,128)(2,1)} %get-tuple-element.220), channel_id=1, source_target_pairs={{0,8},{4,12},{8,0},{12,4},{1,9},{5,13},{9,1},{13,5},{2,10},{6,14},... | collective-permute-start | bytes 1634312 | tf_op jit(solution)/shard_map/ppermute | solution.py:38
  724.5 26.3 %collective-permute-start.27 = (bf16[112,2432]{1,0:T(8,128)(2,1)}, bf16[112,2432]{1,0:T(8,128)(2,1)S(1)}, u32[]{:S(2)}, u32[]{:S(2)}) collective-permute-start(bf16[112,2432]{1,0:T(8,128)(2,1)} %get-tuple-element.220), channel_id=1, source_target_pairs={{0,4},{4,0},{8,12},{12,8},{1,5},{5,1},{9,13},{13,9},{2,6},{6,2},{1... | collective-permute-start | bytes 1634312 | tf_op jit(solution)/shard_map/ppermute | solution.py:38
  739.6 12.5 %collective-permute-start.23 = (bf16[112,2432]{1,0:T(8,128)(2,1)S(1)}, bf16[112,2432]{1,0:T(8,128)(2,1)S(1)}, u32[]{:S(2)}, u32[]{:S(2)}) collective-permute-start(bf16[112,2432]{1,0:T(8,128)(2,1)S(1)} %broadcast_select_fusion.14), channel_id=1, source_target_pairs={{0,16},{16,0},{1,17},{17,1},{2,18},{18,2},{3,19},{19,3},{4,20},{20... | collective-permute-start | bytes 1634312 | tf_op jit(solution)/shard_map/ppermute | solution.py:22
  766.2 23.9 %collective-permute-start.11 = (bf16[112,512]{1,0:T(8,128)(2,1)}, bf16[112,512]{1,0:T(8,128)(2,1)S(1)}, u32[]{:S(2)}, u32[]{:S(2)}) collective-permute-start(bf16[112,512]{1,0:T(8,128)(2,1)} %reduce-scatter.14.cloned.1.call-done), channel_id=1, source_target_pairs={{0,12},{4,8},{8,4},{12,0},{1,13},{5,9},{9,5},{13,1},{2,14},{6,10},... | collective-permute-start | bytes 344072 | tf_op jit(solution)/shard_map/ppermute | solution.py:38
  768.6 22.8 %collective-permute-start.12 = (bf16[112,512]{1,0:T(8,128)(2,1)S(1)}, bf16[112,512]{1,0:T(8,128)(2,1)S(1)}, u32[]{:S(2)}, u32[]{:S(2)}) collective-permute-start(bf16[112,512]{1,0:T(8,128)(2,1)S(1)} %get-tuple-element.221), channel_id=1, source_target_pairs={{0,12},{4,8},{8,4},{12,0},{1,13},{5,9},{9,5},{13,1},{2,14},{6,10},... | collective-permute-start | bytes 344072 | tf_op jit(solution)/shard_map/ppermute | solution.py:38
  (55 other events, 501.5 us)
Sparse Core Ops, SparseCore 0:
  13.5 45.6 all-gather.7
  60.9 28.6 all-gather.11
  91.8 48.1 all-gather.9
  142.1 41.4 all-gather.13
  185.1 28.7 all-gather.17
  215.9 48.1 all-gather.15
  365.1 38.1 reduce-scatter.15
  405.6 50.5 reduce-scatter.9
  485.5 40.6 reduce-scatter.17
  536.3 67.8 reduce-scatter.11
  724.4 30.1 reduce-scatter.13

commit v3 on v2

--- a/solution.py
+++ b/solution.py
@@ -33,11 +33,6 @@
     )
 
 
-def from_peer(block, distance):
-    count = lax.axis_size(CTX)
-    return lax.ppermute(block, CTX, [(i, i ^ distance) for i in range(count)])
-
-
 def pick(index, options):
     chosen = options[0]
     for position in range(1, len(options)):
@@ -59,30 +54,39 @@
     return index
 
 
+def place_of():
+    return lax.axis_index(SECTION), lax.axis_index(CTX), lax.axis_index(FSDP)
+
+
 def peer_of(distance):
-    return (
-        lax.axis_index(SECTION),
-        flip(lax.axis_index(CTX), distance),
-        lax.axis_index(FSDP),
-    )
+    section, ctx, fsdp = place_of()
+    return (section, flip(ctx, distance), fsdp)
+
+
+def greet_all(devices):
+    barrier = pltpu.get_barrier_semaphore()
+    for device in devices:
+        pl.semaphore_signal(barrier, inc=1, device_id=device, device_id_type=MESH)
+    pl.semaphore_wait(barrier, len(devices))
 
 
 def greet(count):
-    barrier = pltpu.get_barrier_semaphore()
-    for k in range(1, count):
-        pl.semaphore_signal(barrier, inc=1, device_id=peer_of(k), device_id_type=MESH)
-    pl.semaphore_wait(barrier, count - 1)
-
-
-def remote(source, target, send_sem, recv_sem, k):
+    greet_all([peer_of(k) for k in range(1, count)])
+
+
+def send(source, target, send_sem, recv_sem, device):
     return pltpu.make_async_remote_copy(
         src_ref=source,
         dst_ref=target,
-        send_sem=send_sem.at[k],
-        recv_sem=recv_sem.at[k],
-        device_id=peer_of(k),
+        send_sem=send_sem,
+        recv_sem=recv_sem,
+        device_id=device,
         device_id_type=MESH,
     )
+
+
+def remote(source, target, send_sem, recv_sem, k):
+    return send(source, target, send_sem.at[k], recv_sem.at[k], peer_of(k))
 
 
 def matmul(left, right):
@@ -105,17 +109,243 @@
     return lax.rsqrt(jnp.mean(values * values, axis=-1, keepdims=True) + epsilon)
 
 
-def call(kernel, outs, scratch, cid, *args):
+def call(kernel, outs, scratch, cid, *args, far=(), far_outs=()):
+    def spec(position, away):
+        return pl.BlockSpec(memory_space=pl.ANY if position in away else VMEM)
+
     return pl.pallas_call(
         kernel,
         out_shape=[jax.ShapeDtypeStruct(shape, kind) for shape, kind in outs],
-        in_specs=[pl.BlockSpec(memory_space=VMEM)] * len(args),
-        out_specs=[pl.BlockSpec(memory_space=VMEM)] * len(outs),
+        in_specs=[spec(position, far) for position in range(len(args))],
+        out_specs=[spec(position, far_outs) for position in range(len(outs))],
         scratch_shapes=scratch,
         compiler_params=pltpu.CompilerParams(
             collective_id=cid, has_side_effects=True, vmem_limit_bytes=LIMIT
         ),
     )(*args)
+
+
+def dma(*shape):
+    return pltpu.SemaphoreType.DMA(shape)
+
+
+class Collect:
+    def __init__(self, ctx_count, fsdp_count, shard_ref, w_ref, sems):
+        self.shard_ref, self.w_ref = shard_ref, w_ref
+        self.z_send, self.z_recv, self.y_send, self.y_recv, self.v_send, self.v_recv, self.own_sem = sems
+        self.shards = range(1, fsdp_count)
+        self.places = range(1, ctx_count)
+        self.fsdp_count = fsdp_count
+        self.section, self.ctx, self.fsdp = place_of()
+        self.sister = (1 - self.section, self.ctx, self.fsdp)
+        self.rows, width = shard_ref.shape
+        self.piece = width // (2 * ctx_count)
+        self.mine = pl.ds(pl.multiple_of(self.fsdp * self.rows, self.rows), self.rows)
+        self.friends = (
+            [self.ahead(d) for d in self.shards] + [peer_of(k) for k in self.places] + [self.sister]
+        )
+
+    def ahead(self, d):
+        return (self.section, self.ctx, lax.rem(self.fsdp + d, self.fsdp_count))
+
+    def behind(self, d):
+        return lax.rem(self.fsdp + self.fsdp_count - d, self.fsdp_count)
+
+    def columns(self, where, core):
+        return pl.ds(pl.multiple_of((where * 2 + core) * self.piece, self.piece), self.piece)
+
+    def block(self, d, where, core):
+        start = pl.multiple_of(self.behind(d) * self.rows, self.rows)
+        return self.w_ref.at[pl.ds(start, self.rows), self.columns(where, core)]
+
+    def own(self, d):
+        cols = self.columns(self.ctx, self.section)
+        source, target = self.shard_ref.at[:, cols], self.w_ref.at[self.mine, cols]
+        return send(source, target, self.z_send.at[d], self.z_recv.at[d], self.ahead(d))
+
+    def kept(self):
+        return pltpu.make_async_copy(self.shard_ref, self.w_ref.at[self.mine], self.own_sem.at[0])
+
+    def spread(self, d, k):
+        source = self.block(d, self.ctx, self.section)
+        device = peer_of(k) if k else self.sister
+        return send(source, source, self.y_send.at[d, k], self.y_recv.at[d, k], device)
+
+    def passed(self, d, k):
+        source = self.block(d, flip(self.ctx, k), self.section)
+        return send(source, source, self.v_send.at[d, k], self.v_recv.at[d, k], self.sister)
+
+    def begin(self):
+        for d in self.shards:
+            self.own(d).start()
+        self.kept().start()
+
+    def relay(self):
+        for d in self.shards:
+            came = self.block(d, self.ctx, self.section)
+            send(came, came, self.z_send.at[d], self.z_recv.at[d], self.sister).wait_recv()
+            for k in (*self.places, 0):
+                self.spread(d, k).start()
+
+    def hand(self):
+        for d in self.shards:
+            for k in self.places:
+                came = self.block(d, flip(self.ctx, k), self.section)
+                send(came, came, self.y_send.at[d, k], self.y_recv.at[d, k], self.sister).wait_recv()
+                self.passed(d, k).start()
+
+    def finish(self):
+        for d in self.shards:
+            for k in (0, *self.places):
+                came = self.block(d, flip(self.ctx, k), 1 - self.section)
+                recv = (self.v_recv if k else self.y_recv).at[d, k]
+                send(came, came, self.v_send.at[d, k], recv, self.sister).wait_recv()
+        for d in self.shards:
+            self.own(d).wait_send()
+            self.spread(d, 0).wait_send()
+            for k in self.places:
+                self.spread(d, k).wait_send()
+                self.passed(d, k).wait_send()
+        self.kept().wait()
+
+
+def collect_sems(ctx_count, fsdp_count):
+    table = dma(fsdp_count, ctx_count)
+    return [dma(fsdp_count), dma(fsdp_count), table, table, table, table, dma(1)]
+
+
+def collect_kernel(
+    ctx_count, fsdp_count, shard_ref, small_ref, w_ref, smalls_ref, s_send, s_recv, *sems
+):
+    steps = Collect(ctx_count, fsdp_count, shard_ref, w_ref, sems)
+
+    def small(d):
+        target = smalls_ref.at[steps.fsdp]
+        return send(small_ref, target, s_send.at[d], s_recv.at[d], steps.ahead(d))
+
+    greet_all(steps.friends)
+    steps.begin()
+    for d in steps.shards:
+        small(d).start()
+    smalls_ref[steps.fsdp] = small_ref[...]
+    steps.relay()
+    steps.hand()
+    steps.finish()
+    for d in steps.shards:
+        came = smalls_ref.at[steps.behind(d)]
+        send(came, came, s_send.at[d], s_recv.at[d], steps.sister).wait_recv()
+    for d in steps.shards:
+        small(d).wait_send()
+
+
+def collect(shard, small):
+    ctx_count, fsdp_count = lax.axis_size(CTX), lax.axis_size(FSDP)
+    rows, width = shard.shape
+    return call(
+        functools.partial(collect_kernel, ctx_count, fsdp_count),
+        [((fsdp_count * rows, width), bf16), ((fsdp_count,) + small.shape, bf16)],
+        [dma(fsdp_count), dma(fsdp_count)] + collect_sems(ctx_count, fsdp_count),
+        5,
+        shard, small, far_outs=(0,),
+    )
+
+
+class SquareSum:
+    def __init__(self, ctx_count, grad_ref, a_ref, b_out, b_in, sems):
+        self.grad_ref, self.a_ref, self.b_out, self.b_in = grad_ref, a_ref, b_out, b_in
+        self.a_send, self.a_recv, self.b_send, self.b_recv = sems
+        self.places = range(1, ctx_count)
+        self.section, self.ctx, fsdp = place_of()
+        self.sister = (1 - self.section, self.ctx, fsdp)
+        self.piece = grad_ref.shape[1] // (2 * ctx_count)
+
+    def columns(self, k, core):
+        start = (flip(self.ctx, k) * 2 + core) * self.piece
+        return pl.ds(pl.multiple_of(start, self.piece), self.piece)
+
+    def chip(self, k):
+        source = self.grad_ref.at[:, self.columns(k, 1 - self.section)]
+        return send(source, self.a_ref.at[k], self.a_send.at[k], self.a_recv.at[k], self.sister)
+
+    def square(self, k):
+        return remote(self.b_out.at[k], self.b_in.at[k], self.b_send, self.b_recv, k)
+
+    def begin(self):
+        for k in (*self.places, 0):
+            self.chip(k).start()
+
+    def middle(self):
+        for k in (*self.places, 0):
+            self.chip(k).wait_recv()
+            own = self.grad_ref[:, self.columns(k, self.section)].astype(f32)
+            self.b_out[k] = (own + self.a_ref[k].astype(f32)).astype(bf16)
+            if k:
+                self.square(k).start()
+
+    def end(self):
+        total = self.b_out[0].astype(f32)
+        for k in self.places:
+            self.square(k).wait_recv()
+            total = total + self.b_in[k].astype(f32)
+        return total.astype(bf16)
+
+    def sent(self):
+        self.chip(0).wait_send()
+        for k in self.places:
+            self.chip(k).wait_send()
+            self.square(k).wait_send()
+
+
+def square_scratch(ctx_count, grad):
+    width, both = grad.shape
+    piece = VMEM((ctx_count, width, both // (2 * ctx_count)), bf16)
+    return [piece, piece, piece, dma(ctx_count), dma(ctx_count), dma(ctx_count), dma(ctx_count)]
+
+
+def every_owner(ctx_count, layer, start_or_wait, sources, targets, send_sem, recv_sem):
+    section, ctx, fsdp = place_of()
+    for k in range(ctx_count):
+        device = (layer, flip(ctx, k), fsdp)
+
+        def go():
+            for i, (source, target) in enumerate(zip(sources, targets)):
+                copy = send(
+                    source,
+                    target.at[ctx, section],
+                    send_sem.at[i, k],
+                    recv_sem.at[i, section, k],
+                    device,
+                )
+                copy.start() if start_or_wait == "start" else copy.wait_send()
+
+        pl.when(section != layer)(go) if k == 0 else go()
+
+
+def from_owners(ctx_count, layer, targets, send_sem, recv_sem):
+    section, ctx, fsdp = place_of()
+    for core in range(2):
+        for k in range(ctx_count):
+            if core == layer and k == 0:
+                continue
+
+            def go():
+                for i, target in enumerate(targets):
+                    came = target.at[flip(ctx, k), core]
+                    send(
+                        came, came, send_sem.at[i, k], recv_sem.at[i, core, k], (1 - section, ctx, fsdp)
+                    ).wait_recv()
+
+            pl.when(section == layer)(go)
+
+
+def chip_square(ctx_count):
+    section, ctx, fsdp = place_of()
+    return [
+        (section if same else 1 - section, flip(ctx, k), fsdp)
+        for k in range(ctx_count)
+        for same in (True, False)
+        if k or not same
+    ]
 
 
 def turn_tile(values):
@@ -130,21 +360,29 @@
 def head_in_group(tile, head, group):
     lane = lax.broadcasted_iota(jnp.int32, tile.shape, 1)
     values = tile.astype(f32)
-    moved = jnp.where(head % 2 == group, values, pltpu.roll(values, HEAD_DIM, 1))
+    moved = values if head % 2 == group else pltpu.roll(values, HEAD_DIM, 1)
     return jnp.where(lane // HEAD_DIM == group, moved, 0.0).astype(bf16)
 
 
-def attend_kernel(
-    count, x_ref, g1_ref, bias_ref, g2_ref, w_ref, cos_ref, sin_ref, kpos_ref, qpos_ref,
-    normed_ref, q_ref, kv_ref, lse_ref, ctx_ref, mid_ref, low2_ref,
-    mask_ref, s_ref, p_ref, vt_ref, ctxf_ref, send_sem, recv_sem,
-):
+def attend_kernel(count, fsdp_count, fetch, *refs):
+    x_ref, g1_ref, bias_ref, g2_ref, w_ref, cos_ref, sin_ref, kpos_ref, qpos_ref = refs[:9]
+    refs = refs[9:]
+    shard_ref, refs = (refs[0], refs[1:]) if fetch else (None, refs)
+    normed_ref, q_ref, kv_ref, lse_ref, ctx_ref, mid_ref, low2_ref = refs[:7]
+    refs = refs[7:]
+    next_ref, refs = (refs[0], refs[1:]) if fetch else (None, refs)
+    mask_ref, s_ref, p_ref, vt_ref, ctxf_ref, send_sem, recv_sem, *sems = refs
     rows, width = x_ref.shape
     pair = kv_ref.shape[2] // 2
     wide = width + 2 * pair
     heads = width // HEAD_DIM
     group_size = heads // (pair // HEAD_DIM)
-    greet(count)
+    if fetch:
+        steps = Collect(count, fsdp_count, shard_ref, next_ref, sems)
+        greet_all(steps.friends)
+        steps.begin()
+    else:
+        greet(count)
     x = x_ref[...].astype(f32)
     normed = (x * row_scale(x) * g1_ref[...]).astype(bf16)
     normed_ref[...] = normed
@@ -163,16 +401,17 @@
     for k in range(count):
         allowed = kpos_ref[k * rows : (k + 1) * rows, :] <= qpos_ref[...]
         mask_ref[k] = jnp.where(allowed, 0.0, masked_value)
+    if fetch:
+        steps.relay()
     for k in range(count):
         if k:
             remote(kv_ref.at[0], kv_ref.at[k], send_sem, recv_sem, k).wait_recv()
         vt_ref[:, k * rows : (k + 1) * rows] = kv_ref[k, :, pair:].astype(f32).T.astype(bf16)
 
-    def one_head(head, carry):
+    for head in range(heads):
         group = head // group_size
-        start = pl.multiple_of((head // 2) * (2 * HEAD_DIM), 2 * HEAD_DIM)
-        tile = q_ref[:, pl.ds(start, 2 * HEAD_DIM)]
-        query = head_in_group(tile, head, group)
+        start = head // 2 * (2 * HEAD_DIM)
+        query = head_in_group(q_ref[:, start : start + 2 * HEAD_DIM], head, group)
         top = None
         for k in range(count):
             scores = matmul_nt(kv_ref[k, :, :pair], query) + mask_ref[k]
@@ -185,14 +424,12 @@
             here = jnp.sum(weight, axis=0, keepdims=True)
             total = here if total is None else total + here
             p_ref[k * rows : (k + 1) * rows, :] = weight.astype(bf16)
-        value_rows = vt_ref[pl.ds(pl.multiple_of(group * HEAD_DIM, HEAD_DIM), HEAD_DIM), :]
+        value_rows = vt_ref[group * HEAD_DIM : (group + 1) * HEAD_DIM, :]
         context = matmul(value_rows, p_ref[...]) * (1.0 / total)
-        place = pl.ds(pl.multiple_of(head * HEAD_DIM, HEAD_DIM), HEAD_DIM)
-        ctxf_ref[place, :] = context
-        lse_ref[pl.ds(head, 1), :] = top + jnp.log(total)
-        return carry
-
-    lax.fori_loop(0, heads, one_head, 0)
+        ctxf_ref[head * HEAD_DIM : (head + 1) * HEAD_DIM, :] = context
+        lse_ref[head : head + 1, :] = top + jnp.log(total)
+        if fetch and head == heads // 2:
+            steps.hand()
     context = ctxf_ref[...]
     ctx_ref[...] = context.astype(bf16)
     middle = x + matmul(context.T.astype(bf16), w_ref[:, wide:])
@@ -200,9 +437,11 @@
     low2_ref[...] = (middle * row_scale(middle) * g2_ref[...]).astype(bf16)
     for k in range(1, count):
         remote(kv_ref.at[0], kv_ref.at[k], send_sem, recv_sem, k).wait_send()
-
-
-def attend(layer, hidden, place):
+    if fetch:
+        steps.finish()
+
+
+def attend(layer, hidden, place, shard=None):
     first_gain, bias, second_gain, weights = layer[:4]
     cosine, sine, key_positions, query_positions = place
     rows, width = hidden.shape
@@ -211,8 +450,13 @@
     pair = (wide - width) // 2
     keys = count * rows
     heads = width // HEAD_DIM
+    fetch = shard is not None
+    fsdp_count = lax.axis_size(FSDP)
+    args = (
+        hidden, first_gain, bias, second_gain, weights, cosine, sine, key_positions, query_positions,
+    )
     return call(
-        functools.partial(attend_kernel, count),
+        functools.partial(attend_kernel, count, fsdp_count, fetch),
         [
             ((rows, width), bf16),
             ((rows, width), bf16),
@@ -221,34 +465,49 @@
             ((width, rows), bf16),
             ((rows, width), f32),
             ((rows, width), bf16),
-        ],
+        ]
+        + [(weights.shape, bf16)] * fetch,
         [
             VMEM((count, rows, rows), f32),
             VMEM((count, rows, rows), f32),
             VMEM((keys, rows), bf16),
             VMEM((pair, keys), bf16),
             VMEM((width, rows), f32),
-            pltpu.SemaphoreType.DMA((count,)),
-            pltpu.SemaphoreType.DMA((count,)),
-        ],
-        1,
-        hidden, first_gain, bias, second_gain, weights, cosine, sine, key_positions, query_positions,
-    )
-
-
-def attend_back_kernel(
-    count, dmid_ref, x_ref, g1_ref, w_ref, cos_ref, sin_ref, kpos_ref, qpos_ref,
-    q_ref, kv_ref, lse_ref,
-    dh_ref, merged_ref, gain_ref, bias_ref, low_ref,
-    mask_ref, p_ref, dp_ref, ds_ref, kt_ref, dctx_ref, dq_ref, dkv_ref, out_ref, in_ref,
-    send_sem, recv_sem,
-):
+            dma(count),
+            dma(count),
+        ]
+        + (collect_sems(count, fsdp_count) if fetch else []),
+        10 if fetch else 1,
+        *args, *([shard] if fetch else []),
+        far_outs=(7,) if fetch else (),
+    )
+
+
+def attend_back_kernel(count, carried, *refs):
+    (
+        dmid_ref, x_ref, g1_ref, w_ref, cos_ref, sin_ref, kpos_ref, qpos_ref,
+        normed_ref, q_ref, kv_ref, lse_ref, ctx_ref,
+    ) = refs[:13]
+    refs = refs[13:]
+    load_ref, refs = (refs[0], refs[1:]) if carried else (None, refs)
+    dh_ref, gain_ref, bias_ref, grad_ref = refs[:4]
+    refs = refs[4:]
+    summed_ref, refs = (refs[0], refs[1:]) if carried else (None, refs)
+    (
+        mask_ref, p_ref, dp_ref, ds_ref, kt_ref, dctx_ref, dq_ref, dkv_ref, out_ref, in_ref,
+        merged_ref, low_ref, send_sem, recv_sem, *scratch,
+    ) = refs
     rows, width = x_ref.shape
     pair = kv_ref.shape[2] // 2
     wide = width + 2 * pair
     heads = width // HEAD_DIM
     group_size = heads // (pair // HEAD_DIM)
-    greet(count)
+    if carried:
+        steps = SquareSum(count, load_ref, *scratch[:3], scratch[3:])
+        greet_all([peer_of(k) for k in range(1, count)] + [steps.sister])
+        steps.begin()
+    else:
+        greet(count)
     low = dmid_ref[...].astype(bf16)
     low_ref[...] = low
     dctx = matmul_nt(low, w_ref[:, wide:]).astype(bf16)
@@ -259,12 +518,12 @@
         kt_ref[:, k * rows : (k + 1) * rows] = kv_ref[k, :, :pair].astype(f32).T.astype(bf16)
     dkv_ref[...] = jnp.zeros_like(dkv_ref)
 
-    def one_head(head, carry):
+    for head in range(heads):
         group = head // group_size
-        start = pl.multiple_of((head // 2) * (2 * HEAD_DIM), 2 * HEAD_DIM)
-        query = head_in_group(q_ref[:, pl.ds(start, 2 * HEAD_DIM)], head, group)
-        upstream = head_in_group(dctx_ref[:, pl.ds(start, 2 * HEAD_DIM)], head, group)
-        lse = lse_ref[pl.ds(head, 1), :]
+        start = head // 2 * (2 * HEAD_DIM)
+        query = head_in_group(q_ref[:, start : start + 2 * HEAD_DIM], head, group)
+        upstream = head_in_group(dctx_ref[:, start : start + 2 * HEAD_DIM], head, group)
+        lse = lse_ref[head : head + 1, :]
         delta = None
         for k in range(count):
             scores = matmul_nt(kv_ref[k, :, :pair], query) + mask_ref[k]
@@ -279,12 +538,12 @@
             score_grad = (p_ref[k] * (dp_ref[k] - delta)).astype(bf16)
             ds_ref[k * rows : (k + 1) * rows, :] = score_grad
             dkv_ref[k, :, :pair] += matmul(score_grad, query)
-        key_rows = kt_ref[pl.ds(pl.multiple_of(group * HEAD_DIM, HEAD_DIM), HEAD_DIM), :]
-        place = pl.ds(pl.multiple_of(head * HEAD_DIM, HEAD_DIM), HEAD_DIM)
-        dq_ref[place, :] = matmul(key_rows, ds_ref[...]) * HEAD_DIM ** (-0.5)
-        return carry
-
-    lax.fori_loop(0, heads, one_head, 0)
+        key_rows = kt_ref[group * HEAD_DIM : (group + 1) * HEAD_DIM, :]
+        dq_ref[head * HEAD_DIM : (head + 1) * HEAD_DIM, :] = (
+            matmul(key_rows, ds_ref[...]) * HEAD_DIM ** (-0.5)
+        )
+        if carried and head == heads // 3:
+            steps.middle()
     for k in range(1, count):
         out_ref[k] = dkv_ref[k].astype(bf16)
         remote(out_ref.at[k], in_ref.at[k], send_sem, recv_sem, k).start()
@@ -296,15 +555,25 @@
 
     for start, size in tiles(width, 2 * HEAD_DIM):
         merged_ref[:, start : start + size] = unturn(dq[:, start : start + size])
+    grad_ref[:, wide:] = matmul(ctx_ref[...], low_ref[...]).astype(bf16)
+    normed = normed_ref[...]
+
+    def project_grad(first, last):
+        for start, size in tiles(last - first, 512):
+            cut = slice(first + start, first + start + size)
+            grad_ref[:, cut] = matmul_tn(normed, merged_ref[:, cut]).astype(bf16)
+
+    project_grad(0, width)
+    normed_grad = matmul_nt(merged_ref[:, :width], w_ref[:, :width])
     total = dkv_ref[0]
     for k in range(1, count):
         remote(out_ref.at[k], in_ref.at[k], send_sem, recv_sem, k).wait_recv()
         total = total + in_ref[k].astype(f32)
     merged_ref[:, width : width + pair] = unturn(total[:, :pair])
     merged_ref[:, width + pair :] = total[:, pair:].astype(bf16)
-    merged = merged_ref[...]
-    bias_ref[...] = jnp.sum(merged.astype(f32), axis=0, keepdims=True)
-    normed_grad = matmul_nt(merged, w_ref[:, :wide])
+    project_grad(width, wide)
+    normed_grad = normed_grad + matmul_nt(merged_ref[:, width:], w_ref[:, width:wide])
+    bias_ref[...] = jnp.sum(merged_ref[...].astype(f32), axis=0, keepdims=True)
     x = x_ref[...].astype(f32)
     scale = row_scale(x)
     gain_ref[...] = jnp.sum(normed_grad * x * scale, axis=0, keepdims=True)
@@ -313,26 +582,34 @@
     dh_ref[...] = dmid_ref[...] + scale * scaled - x * (scale * scale * scale * mean)
     for k in range(1, count):
         remote(out_ref.at[k], in_ref.at[k], send_sem, recv_sem, k).wait_send()
-
-
-def attend_back(layer, kept, middle_grad, place):
+    if carried:
+        summed_ref[...] = steps.end()
+        steps.sent()
+
+
+def attend_back(layer, kept, middle_grad, place, load=None):
     first_gain, bias, second_gain, weights = layer[:4]
     cosine, sine, key_positions, query_positions = place
-    hidden, normed, queries, every_kv, lse = kept
+    hidden, normed, queries, every_kv, lse, context = kept
     rows, width = hidden.shape
     count = lax.axis_size(CTX)
     wide = bias.shape[1]
     pair = (wide - width) // 2
     keys = count * rows
+    carried = load is not None
+    args = (
+        middle_grad, hidden, first_gain, weights, cosine, sine, key_positions, query_positions,
+        normed, queries, every_kv, lse, context,
+    )
     return call(
-        functools.partial(attend_back_kernel, count),
+        functools.partial(attend_back_kernel, count, carried),
         [
             ((rows, width), f32),
-            ((rows, wide), bf16),
             ((1, width), f32),
             ((1, wide), f32),
-            ((rows, width), bf16),
-        ],
+            ((width, wide + width), bf16),
+        ]
+        + [((width, (wide + width) // (2 * count)), bf16)] * carried,
         [
             VMEM((count, rows, rows), f32),
             VMEM((count, rows, rows), f32),
@@ -344,12 +621,14 @@
             VMEM((count, rows, 2 * pair), f32),
             VMEM((count, rows, 2 * pair), bf16),
             VMEM((count, rows, 2 * pair), bf16),
-            pltpu.SemaphoreType.DMA((count,)),
-            pltpu.SemaphoreType.DMA((count,)),
-        ],
-        2,
-        middle_grad, hidden, first_gain, weights, cosine, sine, key_positions, query_positions,
-        queries, every_kv, lse,
+            VMEM((rows, wide), bf16),
+            VMEM((rows, width), bf16),
+            dma(count),
+            dma(count),
+        ]
+        + (square_scratch(count, load) if carried else []),
+        6 if carried else 2,
+        *args, *([load] if carried else []),
     )
 
 
@@ -383,14 +662,31 @@
 
 
 def feed_kernel(
-    count, low_ref, mid_ref, expand_ref, down_ref,
+    count, turns, low_ref, mid_ref, expand_ref, down_ref,
     out_ref, blocks_ref, kept_gate_ref, kept_up_ref,
-    act_ref, part_ref, sent_ref, got_ref, send_sem, recv_sem, send_sem2, recv_sem2,
+    act_ref, part_ref, sent_ref, got_ref, send_sem, recv_sem, send_sem2, recv_sem2, turn_sem,
 ):
     units = down_ref.shape[0]
-    greet(count)
+    if turns:
+        section, ctx, fsdp = place_of()
+        greet_all([peer_of(k) for k in range(1, count)] + [(1 - section, ctx, fsdp)])
+
+        @pl.when(section == 1)
+        def _():
+            pl.semaphore_wait(turn_sem, 1)
+    else:
+        greet(count)
     for k in range(1, count):
         remote(low_ref, blocks_ref.at[k], send_sem, recv_sem, k).start()
+    if turns:
+
+        @pl.when(section == 0)
+        def _():
+            for k in range(1, count):
+                remote(low_ref, blocks_ref.at[k], send_sem, recv_sem, k).wait_send()
+            pl.semaphore_signal(
+                turn_sem, inc=1, device_id=(1 - section, ctx, fsdp), device_id_type=MESH
+            )
     blocks_ref[0] = low_ref[...]
     for k in range(count):
         if k:
@@ -413,18 +709,26 @@
         total = total + got_ref[k].astype(f32)
     out_ref[...] = total.astype(bf16)
     for k in range(1, count):
-        remote(low_ref, blocks_ref.at[k], send_sem, recv_sem, k).wait_send()
         remote(sent_ref.at[k], got_ref.at[k], send_sem2, recv_sem2, k).wait_send()
-
-
-def feed(layer, second_normed, middle):
+    if turns:
+
+        @pl.when(section == 1)
+        def _():
+            for k in range(1, count):
+                remote(low_ref, blocks_ref.at[k], send_sem, recv_sem, k).wait_send()
+    else:
+        for k in range(1, count):
+            remote(low_ref, blocks_ref.at[k], send_sem, recv_sem, k).wait_send()
+
+
+def feed(layer, second_normed, middle, turns):
     expand_w, down_w = layer[4:]
     count = lax.axis_size(CTX)
     rows, width = second_normed.shape
     units = down_w.shape[0]
     sems = [pltpu.SemaphoreType.DMA((count,))] * 4
     return call(
-        functools.partial(feed_kernel, count),
+        functools.partial(feed_kernel, count, turns),
         [
             ((rows, width), bf16),
             ((count, rows, width), bf16),
@@ -437,8 +741,9 @@
             VMEM((count, rows, width), bf16),
             VMEM((count, rows, width), bf16),
         ]
-        + sems,
-        3,
+        + sems
+        + [pltpu.SemaphoreType.REGULAR],
+        3 if turns else 9,
         second_normed, middle, expand_w, down_w,
     )
 
@@ -535,6 +840,224 @@
     )
 
 
+def attn_sum_kernel(
+    ctx_count, fsdp_count, wide, low_ref, high_ref, small_ref, expand_ref, down_ref,
+    projections_ref, output_ref, total_ref, expand_all_ref, down_all_ref,
+    c_out, c_in, d_out, whole_ref, s_out, s_in,
+    c_send, c_recv, d_send, d_recv, s_send, s_recv, e_send, e_recv, e_own, *square_refs,
+):
+    section, ctx, fsdp = place_of()
+    sister = (1 - section, ctx, fsdp)
+    width, piece = high_ref.shape
+    rows = width // fsdp_count
+    places = range(1, ctx_count)
+    shards = range(1, fsdp_count)
+    steps = SquareSum(ctx_count, low_ref, *square_refs[:3], square_refs[3:])
+    sources, targets = (expand_ref, down_ref), (expand_all_ref, down_all_ref)
+    kept = [
+        pltpu.make_async_copy(source, target.at[ctx, section], e_own.at[i])
+        for i, (source, target) in enumerate(zip(sources, targets))
+    ]
+
+    def ahead(d):
+        return (section, ctx, lax.rem(fsdp + d, fsdp_count))
+
+    def c_copy(layer, d):
+        target = lax.rem(fsdp + d, fsdp_count)
+        source = c_out.at[layer, pl.ds(pl.multiple_of(target * rows, rows), rows)]
+        return send(source, c_in.at[layer, d], c_send.at[layer, d], c_recv.at[layer, d], ahead(d))
+
+    def s_copy(step, source, device):
+        return send(s_out.at[source], s_in.at[step], s_send.at[step], s_recv.at[step], device)
+
+    def line_sum(layer):
+        total = c_out[layer, pl.ds(pl.multiple_of(fsdp * rows, rows), rows)].astype(f32)
+        for d in shards:
+            c_copy(layer, d).wait_recv()
+            total = total + c_in[layer, d].astype(f32)
+        d_out[layer] = total.astype(bf16)
+        every_owner(
+            ctx_count, layer, "start", [d_out.at[layer]], [whole_ref], d_send.at[layer], d_recv
+        )
+
+        @pl.when(section == layer)
+        def _():
+            whole_ref[ctx, section] = d_out[layer]
+
+    hops = [(0, 0, sister)]
+    hops += [(k, 1, peer_of(k)) for k in places]
+    hops += [(ctx_count - 1 + d, 2, ahead(d)) for d in shards]
+
+    greet_all(chip_square(ctx_count) + [ahead(d) for d in shards])
+    steps.begin()
+    s_out[0] = small_ref[...]
+    s_copy(*hops[0]).start()
+    c_out[1] = high_ref[...]
+    for d in shards:
+        c_copy(1, d).start()
+
+    @pl.when(section == 1)
+    def _():
+        for copy in kept:
+            copy.start()
+
+    steps.middle()
+    s_copy(*hops[0]).wait_recv()
+    s_out[1] = s_out[0] + s_in[0]
+    for k in places:
+        s_copy(*hops[k]).start()
+    line_sum(1)
+    c_out[0] = steps.end()
+    for d in shards:
+        c_copy(0, d).start()
+    every_owner(ctx_count, 1, "start", sources, targets, e_send, e_recv)
+    part = s_out[1]
+    for k in places:
+        s_copy(*hops[k]).wait_recv()
+        part = part + s_in[k]
+    s_out[2] = part
+    for d in shards:
+        s_copy(*hops[ctx_count - 1 + d]).start()
+    line_sum(0)
+    part = s_out[2]
+    for d in shards:
+        s_copy(*hops[ctx_count - 1 + d]).wait_recv()
+        part = part + s_in[ctx_count - 1 + d]
+    total_ref[...] = part
+    for layer in (1, 0):
+        from_owners(ctx_count, layer, [whole_ref], d_send.at[layer], d_recv)
+    for where in range(ctx_count):
+        for core in range(2):
+            start = (where * 2 + core) * piece
+            block = whole_ref[where, core].astype(f32)
+            size = max(min(wide - start, piece), 0)
+            if size:
+                projections_ref[:, start : start + size] = block[:, :size]
+            if size < piece:
+                first = start + size - wide
+                output_ref[:, first : first + piece - size] = block[:, size:]
+    from_owners(ctx_count, 1, targets, e_send, e_recv)
+    steps.sent()
+    for layer in (1, 0):
+        for d in shards:
+            c_copy(layer, d).wait_send()
+        every_owner(
+            ctx_count, layer, "wait", [d_out.at[layer]], [whole_ref], d_send.at[layer], d_recv
+        )
+    every_owner(ctx_count, 1, "wait", sources, targets, e_send, e_recv)
+    for hop in hops:
+        s_copy(*hop).wait_send()
+
+    @pl.when(section == 1)
+    def _():
+        for copy in kept:
+            copy.wait()
+
+
+def attn_sum(low, high, small, expand_part, down_part, wide):
+    ctx_count, fsdp_count = lax.axis_size(CTX), lax.axis_size(FSDP)
+    width, both = low.shape
+    rows = width // fsdp_count
+    piece = both // (2 * ctx_count)
+    hops = ctx_count + fsdp_count - 1
+    return call(
+        functools.partial(attn_sum_kernel, ctx_count, fsdp_count, wide),
+        [
+            ((rows, wide), f32),
+            ((rows, both - wide), f32),
+            (small.shape, f32),
+            ((ctx_count, 2) + expand_part.shape, bf16),
+            ((ctx_count, 2) + down_part.shape, bf16),
+        ],
+        [
+            VMEM((2, width, piece), bf16),
+            VMEM((2, fsdp_count, rows, piece), bf16),
+            VMEM((2, rows, piece), bf16),
+            VMEM((ctx_count, 2, rows, piece), bf16),
+            VMEM((3,) + small.shape, f32),
+            VMEM((hops,) + small.shape, f32),
+            dma(2, fsdp_count), dma(2, fsdp_count),
+            dma(2, 1, ctx_count), dma(1, 2, ctx_count),
+            dma(hops), dma(hops),
+            dma(2, ctx_count), dma(2, 2, ctx_count), dma(2),
+        ]
+        + square_scratch(ctx_count, low),
+        7,
+        low, high, small, expand_part, down_part, far_outs=(3, 4),
+    )
+
+
+def settle_kernel(
+    ctx_count, expand_ref, down_ref, expand_all_ref, down_all_ref,
+    expand_out, down_out, send_sem, recv_sem, own_sem,
+):
+    section, ctx, _ = place_of()
+    greet_all(chip_square(ctx_count))
+    sources, targets = (expand_ref, down_ref), (expand_out, down_out)
+    every_owner(ctx_count, 0, "start", sources, targets, send_sem, recv_sem)
+    kept = [
+        pltpu.make_async_copy(source, target.at[ctx, section], own_sem.at[i])
+        for i, (source, target) in enumerate(zip(sources, targets))
+    ]
+    loads = [
+        pltpu.make_async_copy(source, target, own_sem.at[2 + i])
+        for i, (source, target) in enumerate(zip((expand_all_ref, down_all_ref), targets))
+    ]
+
+    @pl.when(section == 0)
+    def _():
+        for copy in kept:
+            copy.start()
+        for copy in kept:
+            copy.wait()
+
+    @pl.when(section == 1)
+    def _():
+        for copy in loads:
+            copy.start()
+        for copy in loads:
+            copy.wait()
+
+    from_owners(ctx_count, 0, targets, send_sem, recv_sem)
+    every_owner(ctx_count, 0, "wait", sources, targets, send_sem, recv_sem)
+
+
+def spread_kernel(chunk, shards, side_width, block_ref, out_ref):
+    count = block_ref.shape[0]
+    for where in range(count):
+        sides = unpack_units(block_ref[where].astype(f32))
+        for side, values in enumerate(sides):
+            for shard in range(shards):
+                start = side * side_width + (shard * count + where) * chunk
+                out_ref[:, start : start + chunk] = values[:, shard * chunk : (shard + 1) * chunk]
+
+
+def finish(expand_part, down_part, expand_all, down_all, ff_width):
+    ctx_count, fsdp_count = lax.axis_size(CTX), lax.axis_size(FSDP)
+    half, packed = expand_part.shape
+    half_units, width = down_part.shape
+    expand_all, down_all = call(
+        functools.partial(settle_kernel, ctx_count),
+        [(expand_all.shape, bf16), (down_all.shape, bf16)],
+        [dma(2, ctx_count), dma(2, 2, ctx_count), dma(4)],
+        8,
+        expand_part, down_part, expand_all, down_all,
+        far=(2, 3),
+    )
+    rows = 2 * half
+    step = 32 if rows % 32 == 0 else 16
+    grad_expand = pl.pallas_call(
+        functools.partial(spread_kernel, packed // 2 // fsdp_count, fsdp_count, ff_width),
+        grid=(rows // step,),
+        out_shape=jax.ShapeDtypeStruct((rows, 2 * ff_width), f32),
+        in_specs=[pl.BlockSpec((ctx_count, step, packed), lambda i: (0, i, 0))],
+        out_specs=pl.BlockSpec((step, 2 * ff_width), lambda i: (i, 0)),
+        compiler_params=pltpu.CompilerParams(vmem_limit_bytes=LIMIT),
+    )(expand_all.reshape(ctx_count, rows, packed))
+    grad_down = down_all.astype(f32).reshape(2 * ctx_count * half_units, width)
+    return grad_expand, grad_down
+
+
 def per_device(
     inputs,
     attend_gain,
@@ -555,7 +1078,6 @@
     ctx_count = lax.axis_size(CTX)
     fsdp_count = lax.axis_size(FSDP)
     shard_rows = projections.shape[1]
-    half = shard_rows // 2
     wide = projections.shape[2]
     ff_width = expand_weight.shape[2] // 2
     shard_units = down_weight.shape[1]
@@ -578,20 +1100,20 @@
     )
     place = (cosine, sine, by_distance[:, None], query_positions[None])
 
-    small = jnp.concatenate([attend_gain, biases, mixer_gain], axis=1)
-    small = lax.all_gather(small, (SECTION, FSDP), axis=0, tiled=True).astype(f32)
-    small = small.reshape(2, fsdp_count, -1)
     bias_part = biases.shape[1]
-
-    def small_of(layer):
-        rows = small[layer]
-        return (
-            rows[:, :shard_rows].reshape(1, -1),
-            rows[:, shard_rows : shard_rows + bias_part].reshape(1, -1),
-            rows[:, shard_rows + bias_part :].reshape(1, -1),
-        )
-
+    small_width = -(-bias_part // 128) * 128
+
+    def padded(row):
+        return jnp.pad(row, ((0, 0), (0, small_width - row.shape[1])))
+
+    small_shard = jnp.concatenate(
+        [padded(attend_gain), padded(biases), padded(mixer_gain), jnp.zeros((13, small_width), bf16)]
+    )
     attn_shard = jnp.concatenate([projections[0], output_weight[0]], axis=1)
+
+    def in_order(array):
+        other = swap_sections(array)
+        return jnp.where(is_first, array, other), jnp.where(is_first, other, array)
 
     def unit_columns(side):
         pieces = []
@@ -618,123 +1140,93 @@
         other = swap_sections(jnp.where(is_first, high, low))
         return jnp.where(is_first, own, other), jnp.where(is_first, other, own)
 
-    attn_pair = halves(attn_shard)
     expand_pair = halves(expand_shard)
     down_pair = halves(down_shard)
+    first_shard, second_shard = in_order(attn_shard)
+    small_pair = jnp.concatenate(in_order(small_shard))
 
     def gather(piece):
         return lax.all_gather(piece, both, axis=0, tiled=True)
 
+    expands, downs = [None, None], [None, None]
+    expands[0], downs[0] = gather(expand_pair[0]), gather(down_pair[0])
+    first_shard, small_pair = lax.optimization_barrier(
+        (first_shard, small_pair, expand_pair[0], down_pair[0])
+    )[:2]
+    weights, smalls = collect(first_shard, small_pair)
+    smalls = smalls.astype(f32)
+    weights = [weights, None]
+    expands[1], downs[1] = gather(expand_pair[1]), gather(down_pair[1])
+
+    def layer_of(layer):
+        first = 16 * layer
+        return (
+            smalls[:, first, :shard_rows].reshape(1, -1),
+            smalls[:, first + 1, :bias_part].reshape(1, -1),
+            smalls[:, first + 2, :shard_rows].reshape(1, -1),
+            weights[layer],
+            expands[layer],
+            downs[layer],
+        )
+
     layers = []
-    for layer in range(2):
-        layers.append(
-            small_of(layer)
-            + (
-                gather(attn_pair[layer]),
-                gather(expand_pair[layer]),
-                gather(down_pair[layer]),
-            )
-        )
-
     hidden = source
     stored = []
     sent = []
     for layer in range(2):
-        normed, queries, every_kv, lse, context, middle, second_normed = attend(
-            layers[layer], hidden, place
+        layers.append(layer_of(layer))
+        normed, queries, every_kv, lse, context, middle, second_normed, *fetched = attend(
+            layers[layer], hidden, place, None if layer else second_shard
         )
+        if fetched:
+            weights[1] = fetched[0]
         kept = (hidden, normed, queries, every_kv, lse, context)
-        hidden, blocks, kept_gate, kept_up = feed(layers[layer], second_normed, middle)
+        hidden, blocks, kept_gate, kept_up = feed(layers[layer], second_normed, middle, False)
         sent.append(hidden)
         stored.append((middle, kept, blocks, kept_gate, kept_up))
 
-    chain = []
-
     def scatter(array):
-        if chain:
-            array = lax.optimization_barrier((array, chain[-1]))[0]
-        chain.append(lax.psum_scatter(array, both, scatter_dimension=0, tiled=True))
-        return chain[-1]
-
-    def from_peers(array):
-        return [array] + [from_peer(array, k) for k in range(1, ctx_count)]
-
-    def ctx_sum(array):
-        size = array.shape[1] // ctx_count
-        total = None
-        for k in range(ctx_count):
-            cut = lax.dynamic_slice_in_dim(array, (ctx ^ k) * size, size, axis=1)
-            cut = (from_peer(cut, k) if k else cut).astype(f32)
-            total = cut if total is None else total + cut
-        return total.astype(bf16)
+        return lax.psum_scatter(array, both, scatter_dimension=0, tiled=True)
 
     grad = upstream
     hidden_grads = [None, None]
     small_grads = [None, None]
-    down_parts = [None, None]
-    expand_parts = [None, None]
-    attn_parts = [None, None]
-    waiting = None
+    attn_grads = [None, None]
+    scattered = ()
+    summed = ()
     for layer in (1, 0):
         middle, kept, blocks, kept_gate, kept_up = stored[layer]
         middle_grad, second_grad, expand_grad, down_grad = feed_back(
             layers[layer], middle, blocks, kept_gate, kept_up, grad
         )
-        down_parts[layer] = from_peers(scatter(down_grad))
-        if waiting is not None:
-            expand_grad = jnp.concatenate([expand_grad, waiting], axis=1)
-        part = scatter(expand_grad)
-        if waiting is not None:
-            attn_parts[1] = from_peers(part[:, 2 * units * fsdp_count :])
-            part = part[:, : 2 * units * fsdp_count]
-        expand_parts[layer] = from_peers(part)
-        hidden_grad, merged_grad, first_grad, offset_grad, middle_low = attend_back(
-            layers[layer], kept[:5], middle_grad, place
+        if scattered:
+            expand_grad, down_grad, *scattered = lax.optimization_barrier(
+                (expand_grad, down_grad, *scattered)
+            )
+        hidden_grad, first_grad, offset_grad, attn_grads[layer], *summed = attend_back(
+            layers[layer], kept, middle_grad, place, attn_grads[1]
         )
-        attn_grad = jnp.concatenate(
-            [
-                jnp.einsum("rd,rf->df", kept[1], merged_grad, preferred_element_type=f32),
-                jnp.dot(kept[5], middle_low, preferred_element_type=f32),
-            ],
-            axis=1,
-        ).astype(bf16)
-        waiting = ctx_sum(attn_grad)
+        earlier, scattered = scattered, (scatter(expand_grad), scatter(down_grad))
         small_grads[layer] = jnp.concatenate([first_grad, offset_grad, second_grad], axis=1)[0]
         hidden_grads[layer] = hidden_grad
         grad = hidden_grad.astype(bf16)
-    attn_parts[0] = from_peers(scatter(waiting))
-
-    def finish(parts):
-        own = [jnp.where(is_first, low, high) for low, high in zip(*parts)]
-        other = [swap_sections(jnp.where(is_first, high, low)) for low, high in zip(*parts)]
-        whole = [
-            jnp.concatenate(
-                [jnp.where(is_first, one, two), jnp.where(is_first, two, one)], axis=0
-            )
-            for one, two in zip(own, other)
-        ]
-        return [pick(ctx ^ k, whole) for k in range(ctx_count)]
-
-    down_all = finish(down_parts)
-    expand_all = [unpack_units(array) for array in finish(expand_parts)]
-    attn_all = jnp.concatenate(finish(attn_parts), axis=1).astype(f32)
-    grad_down = jnp.concatenate(down_all, axis=0).astype(f32)[None]
-    columns = [
-        expand_all[k][side][:, shard * units : (shard + 1) * units]
-        for side in range(2)
-        for shard in range(fsdp_count)
-        for k in range(ctx_count)
-    ]
-    grad_expand = jnp.concatenate(columns, axis=1).astype(f32)[None]
-    grad_projections = attn_all[:, :wide][None]
-    grad_output = attn_all[:, wide:][None]
-
-    small_all = lax.psum(jnp.stack(small_grads), (CTX, FSDP, SECTION))
-    small_own = mine(small_all)
+
+    spare = -small_grads[0].shape[0] % model_width
+    small_rows = [jnp.pad(vector, (0, spare)).reshape(-1, model_width) for vector in small_grads]
+    small_count = small_rows[0].shape[0]
+    rows_left = -2 * small_count % 8
+    small_stack = jnp.pad(jnp.concatenate(small_rows), ((0, rows_left), (0, 0)))
+    grad_projections, grad_output, small_all, *gathered = attn_sum(
+        attn_grads[0], *summed, small_stack, *earlier, wide
+    )
+    grad_expand, grad_down = finish(*scattered, *gathered, ff_width)
+    small_own = jnp.where(
+        is_first, small_all[:small_count], small_all[small_count : 2 * small_count]
+    ).reshape(-1)
     first_all, offset_all, second_all = (
         small_own[:model_width],
         small_own[model_width : model_width + wide],
-        small_own[model_width + wide :],
+        small_own[model_width + wide : 2 * model_width + wide],
     )
     pair_width = (wide - model_width) // 2
 
@@ -755,13 +1247,13 @@
         activations,
         input_grads,
         part(first_all),
-        grad_projections,
+        grad_projections[None],
         part(offset_all[: model_width + pair_width]),
         part(offset_all[model_width + pair_width :]),
-        grad_output,
+        grad_output[None],
         part(second_all),
-        grad_expand,
-        grad_down,
+        grad_expand[None],
+        grad_down[None],
     )
 
 

time: 813 us -> 581 us (0.71)
  waiting for transfers between devices: 224 us -> 19.9 us
  Pallas kernels: 319 us -> 495 us
  blocking collectives: 105 us -> 0 us
  starting transfers between devices: 42.3 us -> 2.99 us
  other arithmetic: 65.1 us -> 28.4 us
  local copies, waits for them, and re-layouts: 30.7 us -> 14.4 us
    pallas_call x8 -> x11, Pallas kernels: 319 us -> 487 us  [call(): pl.pallas_call(kernel, out_shape=[jax.ShapeDtypeStruct(shape, kind) for s...]
    all_gather x6 -> x4, waiting for transfers between devices: 95.1 us -> 3.2 us  [gather(): return lax.all_gather(piece, both, axis=0, tiled=True)]
    ppermute x24 -> x0, waiting for transfers between devices: 82.9 us -> none  [from_peer(): return lax.ppermute(block, CTX, [(i, i ^ distance) for i in range(count)])]
    psum x1 -> x0, blocking collectives: 79.7 us -> none  [per_device(): small_all = lax.psum(jnp.stack(small_grads), (CTX, FSDP, SECTION))]
    unnamed x13 -> x9, waiting for transfers between devices: 40 us -> 2.49 us
    ppermute x24 -> x0, starting transfers between devices: 34.2 us -> none  [from_peer(): return lax.ppermute(block, CTX, [(i, i ^ distance) for i in range(count)])]
    all_gather x1 -> x0, blocking collectives: 25.5 us -> none  [per_device(): lax.all_gather(small, (SECTION, FSDP), axis=0, tiled=True).astype(f32)]
    concatenate x5 -> x1, local copies, waits for them, and re-layouts: 15.3 us -> 0.08 us  [per_device(): jnp.concatenate([padded(attend_gain), padded(biases), padded(mixer_gain),...]
  transfers between devices with their start and end apart: 52 -> 14, of which waited for: 21 -> 5; matrix products, arithmetic and copies ran while one was open for 11% -> 6% of each run, Pallas kernels for 27% -> 60%
where the time goes in v3:
time: 581 us; the launch traced here: 576 us
  Pallas kernels  495 us (85%)
  other arithmetic  28.4 us (5%)
  waiting for transfers between devices  19.9 us (3%)
  between operations  14.9 us (3%)
  local copies, waits for them, and re-layouts  14.4 us (2%)
    pallas_call x11, Pallas kernels, call(): pl.pallas_call(kernel, out_shape=[jax.ShapeDtypeStruct(shape, kind) for s...  487 us
  transfers between devices with their start and end apart: 14, of which 5 were waited for; matrix products, arithmetic and copies ran while one was open for 6% of the time, Pallas kernels for 60%

profile of v3, /device:TPU:0, one launch (start us, length us, event | category | flops | bytes accessed | tf_op | source)
XLA Modules:
  0.0 575.8 jit_solution(8232779387181034980)
XLA Ops:
  7.3 1.2 select_bitcast_fusion.4
  8.9 1.2 collective-permute-done.3
  10.1 2.0 bitcast_select_fusion
  12.2 3.2 select_bitcast_fusion.6
  15.5 3.1 select_bitcast_fusion.5
  19.8 1.1 concatenate.41
  21.5 1.6 collective-permute-done.2
  23.1 1.1 broadcast_select_fusion.2
  27.5 1.0 pad_maximum_fusion.1
  30.2 1.0 copy.35.refs_7_.refs_6_
  31.9 2.8 broadcast_select_fusion
  34.7 33.2 %shard_map.177 = (bf16[896,2048]{1,0:T(8,128)(2,1)}, bf16[4,32,384]{2,1,0:T(8,128)(2,1)}) custom-call(bf16[224,2048]{1,0:T(8,128)(2,1)} %get-tuple-element.65.shard_ref, bf16[32,384]{1,0:T(8,128)(2,1)} %pad_maximum_fusion.4.small_ref), custom_call_target="tpu_custom_call" | custom-call | tf_op jit(solution)/shard_map/pallas_call | solution.py:116
  73.0 40.3 %shard_map.178 = (bf16[256,896]{1,0:T(8,128)(2,1)}, bf16[256,896]{1,0:T(8,128)(2,1)}, bf16[4,256,256]{2,1,0:T(8,128)(2,1)}, f32[16,256]{1,0:T(8,128)}, bf16[896,...) custom-call(bf16[256,896]{1,0:T(8,128)(2,1)} %dynamic-slice_bitcast_fusion.1.refs_0_, ...), custom_call_target="tpu_custom_call" | custom-call | tf_op jit(solution)/shard_map/pallas_call | solution.py:116
  113.4 49.5 %shard_map.179 = (bf16[256,896]{1,0:T(8,128)(2,1)}, bf16[4,256,896]{2,1,0:T(8,128)(2,1)}, bf16[4,256,1216]{2,1,0:T(8,128)(2,1)}, bf16[4,256,1216]{2,1,0:T(8,128)(2,1)}) custom-call(bf16[256,896]{1,0:T(8,128)(2,1)} %get-tuple-element.69.low_ref, f32[256,896]{1,0:T(8,128)} %get-tuple-element.70.mid_ref, ...), custom_call_target="tpu_custom_call" | custom-call | tf_op jit(solution)/shard_map/pallas_call | solution.py:116
  162.9 21.4 %shard_map.180 = (bf16[256,896]{1,0:T(8,128)(2,1)}, bf16[256,896]{1,0:T(8,128)(2,1)}, bf16[4,256,256]{2,1,0:T(8,128)(2,1)}, f32[16,256]{1,0:T(8,128)}, bf16[896,...) custom-call(bf16[256,896]{1,0:T(8,128)(2,1)} %get-tuple-element.71.refs_0_.refs_1_, ...), custom_call_target="tpu_custom_call" | custom-call | tf_op jit(solution)/shard_map/pallas_call | solution.py:116
  184.3 3.1 all-gather.9.cloned.1.call-done.expand_ref
  187.5 49.7 %shard_map.181 = (bf16[256,896]{1,0:T(8,128)(2,1)}, bf16[4,256,896]{2,1,0:T(8,128)(2,1)}, bf16[4,256,1216]{2,1,0:T(8,128)(2,1)}, bf16[4,256,1216]{2,1,0:T(8,128)(2,1)}) custom-call(bf16[256,896]{1,0:T(8,128)(2,1)} %get-tuple-element.73.low_ref, f32[256,896]{1,0:T(8,128)} %get-tuple-element.74.mid_ref, ...), custom_call_target="tpu_custom_call" | custom-call | tf_op jit(solution)/shard_map/pallas_call | solution.py:116
  237.1 51.3 %shard_map.182 = (f32[256,896]{1,0:T(8,128)}, f32[1,896]{1,0:T(1,128)}, bf16[896,2432]{1,0:T(8,128)(2,1)}, bf16[1216,896]{1,0:T(8,128)(2,1)}) custom-call(bf16[256,896]{1,0:T(8,128)(2,1)} %dynamic-slice_bitcast_fusion.grad_ref, f32[256,896]{1,0:T(8,128)} %get-tuple-element.74.mid_ref, f32[1,896]{1,0:T(1,128)} %reshape_squeeze.23.refs_3_.g2_ref, ...), custom_call_target="tpu_custom_call" | custom-call | tf_op jit(solution)/shard_map/pallas_call | solution.py:116
  289.0 29.1 %shard_map.183 = (f32[256,896]{1,0:T(8,128)}, f32[1,896]{1,0:T(1,128)}, f32[1,1152]{1,0:T(1,128)}, bf16[896,2048]{1,0:T(8,128)(2,1)}) custom-call(f32[256,896]{1,0:T(8,128)} %get-tuple-element.79.refs_0_, bf16[256,896]{1,0:T(8,128)(2,1)} %get-tuple-element.71.refs_0_.refs_1_, f32[1,896]{1,0:T(1,128)} %reshape_squeeze.21.refs_1_.refs_2_, ...), custom_call_target="tpu_custom_call" | custom-call | tf_op jit(solution)/shard_map/pallas_call | solution.py:116
  318.1 2.0 convert_element_type.28.grad_ref
  320.1 49.6 %shard_map.184 = (f32[256,896]{1,0:T(8,128)}, f32[1,896]{1,0:T(1,128)}, bf16[896,2432]{1,0:T(8,128)(2,1)}, bf16[1216,896]{1,0:T(8,128)(2,1)}) custom-call(bf16[256,896]{1,0:T(8,128)(2,1)} %convert_element_type.28.grad_ref, f32[256,896]{1,0:T(8,128)} %get-tuple-element.70.mid_ref, f32[1,896]{1,0:T(1,128)} %reshape_squeeze.20.refs_3_.g2_ref, ...), custom_call_target="tpu_custom_call" | custom-call | tf_op jit(solution)/shard_map/pallas_call | solution.py:116
  369.8 9.9 %reduce-scatter.9.cloned.1.call-done.expand_ref = bf16[112,2432]{1,0:T(8,128)(2,1)} async-done(((bf16[896,2432]{1,0:T(8,128)(2,1)}), bf16[112,2432]{1,0:T(8,128)(2,1)}) %reduce-scatter.9.cloned.1.call-update) | async-done | bytes 544784 | tf_op jit(solution)/shard_map/reduce_scatter | solution.py:1189
  380.4 43.8 %shard_map.185 = (f32[256,896]{1,0:T(8,128)}, f32[1,896]{1,0:T(1,128)}, f32[1,1152]{1,0:T(1,128)}, bf16[896,2048]{1,0:T(8,128)(2,1)}, bf16[896,256]{1,0:T(8,128)(2,1)}) custom-call(f32[256,896]{1,0:T(8,128)} %get-tuple-element.89.refs_0_, bf16[256,896]{1,0:T(8,128)(2,1)} %dynamic-slice_bitcast_fusion.1.refs_0_.refs_1_, ...), custom_call_target="tpu_custom_call" | custom-call | tf_op jit(solution)/shard_map/pallas_call | solution.py:116
  424.3 1.0 convert_select_fusion
  427.6 1.6 collective-permute-done.4
  429.3 1.0 maximum_bitcast_fusion.1
  430.3 1.3 select_bitcast_fusion.1
  431.7 1.3 maximum_bitcast_fusion
  433.0 76.2 %shard_map.186 = (f32[224,1152]{1,0:T(8,128)}, f32[224,896]{1,0:T(8,128)}, f32[8,896]{1,0:T(8,128)}, bf16[4,2,112,2432]{3,2,1,0:T(8,128)(2,1)}, bf16[4,2,152,896]{3,2,1,0:T(8,128)(2,1)}) custom-call(bf16[896,2048]{1,0:T(8,128)(2,1)} %get-tuple-element.97.low_ref, bf16[896,256]{1,0:T(8,128)(2,1)} %get-tuple-element.98.high_ref, ...), custom_call_target="tpu_custom_call" | custom-call | tf_op jit(solution)/shard_map/pallas_call | solution.py:116
  512.6 43.1 %shard_map.187 = (bf16[4,2,112,2432]{3,2,1,0:T(8,128)(2,1)}, bf16[4,2,152,896]{3,2,1,0:T(8,128)(2,1)}) custom-call(bf16[112,2432]{1,0:T(8,128)(2,1)} %reduce-scatter.11.cloned.1.call-done.expand_ref, bf16[152,896]{1,0:T(8,128)(2,1)} %reduce-scatter.15.cloned.1.call-done.down_ref, bf16[4,2,112,2432]{3,2,1,0:T(8,128)(2,1)} %get-tuple-element.116.expand_all_ref, ...), custom_call_target="tpu_custom_call" | custom-call | tf_op jit(solution)/shard_map/pallas_call | solution.py:116
  555.7 8.2 %shard_map.188 = f32[224,9728]{1,0:T(8,128)} custom-call(bf16[4,224,2432]{2,1,0:T(8,128)(2,1)} %bitcast.61), custom_call_target="tpu_custom_call" | custom-call | tf_op jit(solution)/shard_map/pallas_call | solution.py:1049
  563.9 2.3 convert.1
  (127 shorter events, 22.6 us)
Async XLA Ops:
  7.2 21.4 %copy-start = (bf16[2,1,256,896]{3,2,1,0:T(8,128)(2,1)S(1)}, bf16[2,1,256,896]{3,2,1,0:T(8,128)(2,1)}, u32[]{:S(2)}) copy-start(bf16[2,1,256,896]{3,2,1,0:T(8,128)(2,1)} %param.10) | copy-start | bytes 2752516
  7.2 106.2 %all-gather.7.cloned.1.call-start = ((), (), s32[]{:S(2)}) async-start(), calls=%async_computation.5 | async-start | bytes 2451456 | tf_op jit(solution)/shard_map/all_gather | solution.py:1149
  8.4 1.7 collective-permute-start.3
  12.1 101.3 %all-gather.5.cloned.1.call-start = ((), (), s32[]{:S(2)}) async-start(), calls=%async_computation.4 | async-start | bytes 4902912 | tf_op jit(solution)/shard_map/all_gather | solution.py:1149
  21.0 5.1 copy-start.13
  21.0 5.1 copy-start.16
  21.0 5.1 copy-start.17
  21.0 5.5 copy-start.6
  21.0 5.5 copy-start.8
  21.0 2.0 collective-permute-start.2
  24.2 2.7 copy-start.22
  24.2 160.1 %all-gather.11.cloned.1.call-start = ((), (), s32[]{:S(2)}) async-start(), calls=%async_computation.7 | async-start | bytes 2451456 | tf_op jit(solution)/shard_map/all_gather | solution.py:1149
  24.9 162.5 %all-gather.9.cloned.1.call-start = ((), (), s32[]{:S(2)}) async-start(), calls=%async_computation.6 | async-start | bytes 4902912 | tf_op jit(solution)/shard_map/all_gather | solution.py:1149
  25.5 344.2 %reduce-scatter.13.cloned.1.call-start = ((), (), s32[]{:S(2)}) async-start(), calls=%async_computation.10 | async-start | bytes 2451456
  26.2 5.0 collective-permute-start.1
  26.7 5.2 collective-permute-start
  27.0 7.8 %copy-start.12 = (s32[1,1,256]{2,1,0:T(1,128)}, s32[1,1,256]{2,1,0:T(1,128)S(1)}, u32[]{:S(2)}) copy-start(s32[1,1,256]{2,1,0:T(1,128)S(1)} %get-tuple-element.187) | copy-start | bytes 3076
  288.4 91.2 %reduce-scatter.9.cloned.1.call-start = ((), (), s32[]{:S(2)}) async-start(), calls=%async_computation.8 | async-start | bytes 4902912 | tf_op jit(solution)/shard_map/reduce_scatter | solution.py:1189
  289.0 223.6 %reduce-scatter.15.cloned.1.call-start = ((), (), s32[]{:S(2)}) async-start(), calls=%async_computation.11 | async-start | bytes 2451456
  379.6 133.0 %reduce-scatter.11.cloned.1.call-start = ((), (), s32[]{:S(2)}) async-start(), calls=%async_computation.9 | async-start | bytes 4902912 | tf_op jit(solution)/shard_map/reduce_scatter | solution.py:1189
  380.4 43.9 %copy-start.2 = (f32[256,896]{1,0:T(8,128)S(1)}, f32[256,896]{1,0:T(8,128)}, u32[]{:S(2)}) copy-start(f32[256,896]{1,0:T(8,128)} %get-tuple-element.85) | copy-start | bytes 2752516
  424.2 2.6 copy-start.15
  424.2 2.6 copy-start.20
  424.2 2.6 copy-start.21
  424.2 2.7 copy-start.14
  424.2 2.7 copy-start.18
  424.2 2.7 copy-start.19
  425.3 5.0 collective-permute-start.5
  426.8 2.4 collective-permute-start.4
  426.8 3.5 copy-start.4
  555.7 8.2 %copy-start.5 = (bf16[4,2,152,896]{3,2,1,0:T(8,128)(2,1)S(1)}, bf16[4,2,152,896]{3,2,1,0:T(8,128)(2,1)}, u32[]{:S(2)}) copy-start(bf16[4,2,152,896]{3,2,1,0:T(8,128)(2,1)} %get-tuple-element.119) | copy-start | bytes 6537220
  563.9 4.8 copy-start.1
  (5 other events, 9.9 us)
Sparse Core Ops, SparseCore 0:
  12.3 32.3 all-gather.6
  46.9 60.0 all-gather.4
  108.6 28.4 all-gather.10
  139.2 48.2 all-gather.8
  288.5 38.3 reduce-scatter.12
  329.1 50.5 reduce-scatter.8
  381.9 37.3 reduce-scatter.14
  421.7 67.2 reduce-scatter.10

commit v4 on v3

--- a/solution.py
+++ b/solution.py
@@ -252,9 +252,10 @@
 
 class SquareSum:
     def __init__(self, ctx_count, grad_ref, a_ref, b_out, b_in, sems):
-        self.grad_ref, self.a_ref, self.b_out, self.b_in = grad_ref, a_ref, b_out, b_in
-        self.a_send, self.a_recv, self.b_send, self.b_recv = sems
-        self.places = range(1, ctx_count)
+        self.grad_ref, self.a_ref, self.b_out = grad_ref, a_ref, b_out
+        self.a_send, self.a_recv, b_send, b_recv = sems
+        self.parts = Parts(ctx_count, b_out, b_in, b_send, b_recv)
+        self.order = (*range(ctx_count - 1, 0, -1), 0)
         self.section, self.ctx, fsdp = place_of()
         self.sister = (1 - self.section, self.ctx, fsdp)
         self.piece = grad_ref.shape[1] // (2 * ctx_count)
@@ -267,39 +268,37 @@
         source = self.grad_ref.at[:, self.columns(k, 1 - self.section)]
         return send(source, self.a_ref.at[k], self.a_send.at[k], self.a_recv.at[k], self.sister)
 
-    def square(self, k):
-        return remote(self.b_out.at[k], self.b_in.at[k], self.b_send, self.b_recv, k)
-
     def begin(self):
-        for k in (*self.places, 0):
+        for k in self.order:
             self.chip(k).start()
 
     def middle(self):
-        for k in (*self.places, 0):
+        for k in self.order:
             self.chip(k).wait_recv()
             own = self.grad_ref[:, self.columns(k, self.section)].astype(f32)
-            self.b_out[k] = (own + self.a_ref[k].astype(f32)).astype(bf16)
+            total = own + self.a_ref[k].astype(f32)
             if k:
-                self.square(k).start()
+                self.parts.put(k, total)
+            else:
+                self.b_out[0] = total.astype(bf16)
+
+    def merge(self):
+        self.parts.merge()
 
     def end(self):
-        total = self.b_out[0].astype(f32)
-        for k in self.places:
-            self.square(k).wait_recv()
-            total = total + self.b_in[k].astype(f32)
-        return total.astype(bf16)
+        return self.parts.total(self.b_out[0].astype(f32)).astype(bf16)
 
     def sent(self):
-        self.chip(0).wait_send()
-        for k in self.places:
+        for k in self.order:
             self.chip(k).wait_send()
-            self.square(k).wait_send()
+        self.parts.sent()
 
 
 def square_scratch(ctx_count, grad):
     width, both = grad.shape
     piece = VMEM((ctx_count, width, both // (2 * ctx_count)), bf16)
-    return [piece, piece, piece, dma(ctx_count), dma(ctx_count), dma(ctx_count), dma(ctx_count)]
+    sems = [dma(ctx_count), dma(ctx_count), dma(ctx_count, 2), dma(ctx_count, 2)]
+    return [piece, piece, piece] + sems
 
 
 def every_owner(ctx_count, layer, start_or_wait, sources, targets, send_sem, recv_sem):
@@ -336,6 +335,104 @@
                     ).wait_recv()
 
             pl.when(section == layer)(go)
+
+
+class Owners:
+    def __init__(self, ctx_count, layer, sources, targets, send_sem, recv_sem, onward_sem):
+        self.layer, self.targets = layer, targets
+        self.send_sem, self.recv_sem, self.onward_sem = send_sem, recv_sem, onward_sem
+        self.section, self.ctx, self.fsdp = place_of()
+        self.count, self.square = ctx_count, ctx_count == 4
+        rows = sources[0].shape[0]
+        cut = rows * 5 // 7 // 16 * 16
+        self.square = self.square and 0 < cut < rows and rows % 16 == 0
+        if self.square:
+            low, high = pl.ds(0, cut), pl.ds(cut, rows - cut)
+            self.pieces = [(sources[0].at[low], 0, low), (sources[0].at[high], 0, high)]
+            self.pieces.append((sources[1], 1, None))
+        else:
+            self.pieces = [(source, i, None) for i, source in enumerate(sources)]
+        self.keeper = self.section == layer
+
+    def spot(self, i, k, core):
+        _, which, rows = self.pieces[i]
+        spot = self.targets[which].at[flip(self.ctx, k), core]
+        return spot if rows is None else spot.at[rows]
+
+    def peer(self, k):
+        return (self.layer, flip(self.ctx, k), self.fsdp)
+
+    def own(self, i, k):
+        return send(
+            self.pieces[i][0],
+            self.spot(i, 0, self.section),
+            self.send_sem.at[i, k],
+            self.recv_sem.at[i, self.section, k],
+            self.peer(k),
+        )
+
+    def onward(self, i, core):
+        came = 2 if i == 0 else 1
+        spot = self.spot(i, came, core)
+        return send(
+            spot, spot, self.onward_sem.at[i, core], self.recv_sem.at[i, core, 3], self.peer(3 - came)
+        )
+
+    def outgoing(self):
+        if self.square:
+            return [(1, 1), (2, 1), (0, 2), (0, 1), (1, 2), (2, 2)]
+        return [(i, k) for k in range(1, self.count) for i in range(len(self.pieces))]
+
+    def begin(self):
+        for i, k in self.outgoing():
+            self.own(i, k).start()
+
+        @pl.when(jnp.logical_not(self.keeper))
+        def _():
+            for i in range(len(self.pieces)):
+                self.own(i, 0).start()
+
+    def arrival(self, i, core, k):
+        spot = self.spot(i, k, core)
+        recv = self.recv_sem.at[i, core, k]
+        send(spot, spot, self.send_sem.at[i, k], recv, (1 - self.section, self.ctx, self.fsdp)).wait_recv()
+
+    def relay(self):
+        if self.square:
+
+            @pl.when(self.keeper)
+            def _():
+                for i, k in ((1, 1), (2, 1), (0, 2)):
+                    for core in range(2):
+                        self.arrival(i, core, k)
+                        self.onward(i, core).start()
+
+    def end(self):
+        early = ((1, 1), (2, 1), (0, 2)) if self.square else ()
+
+        @pl.when(self.keeper)
+        def _():
+            for k in range(self.count):
+                for core in range(2):
+                    for i in range(len(self.pieces)):
+                        if (i, k) not in early and (k or core != self.layer):
+                            self.arrival(i, core, k)
+            if self.square:
+                for i in range(3):
+                    for core in range(2):
+                        self.onward(i, core).wait_send()
+
+        @pl.when(jnp.logical_not(self.keeper))
+        def _():
+            for i in range(len(self.pieces)):
+                self.own(i, 0).wait_send()
+
+        for i, k in self.outgoing():
+            self.own(i, k).wait_send()
+
+
+def owner_sems(ctx_count):
+    return [dma(3, ctx_count), dma(3, 2, ctx_count), dma(3, 2)]
 
 
 def chip_square(ctx_count):
@@ -542,8 +639,10 @@
         dq_ref[head * HEAD_DIM : (head + 1) * HEAD_DIM, :] = (
             matmul(key_rows, ds_ref[...]) * HEAD_DIM ** (-0.5)
         )
-        if carried and head == heads // 3:
+        if carried and head == 1:
             steps.middle()
+        if carried and head == heads // 2:
+            steps.merge()
     for k in range(1, count):
         out_ref[k] = dkv_ref[k].astype(bf16)
         remote(out_ref.at[k], in_ref.at[k], send_sem, recv_sem, k).start()
@@ -653,6 +752,112 @@
     return gate, up
 
 
+class Rows:
+    def __init__(self, count, own_ref, slots_ref, send_sem, recv_sem):
+        self.own_ref, self.slots_ref = own_ref, slots_ref
+        self.send_sem, self.recv_sem = send_sem, recv_sem
+        self.count, self.square = count, count == 4
+        self.half = own_ref.shape[0] // 2
+
+    def rows(self, h):
+        return pl.ds(h * self.half, self.half)
+
+    def copy(self, source, k, h, peer):
+        target = self.slots_ref.at[k, self.rows(h)]
+        return send(source, target, self.send_sem.at[k, h], self.recv_sem.at[k, h], peer_of(peer))
+
+    def own(self, k, h):
+        return self.copy(self.own_ref.at[self.rows(h)], k, h, k)
+
+    def onward(self, h):
+        came = 1 if h else 2
+        return self.copy(self.slots_ref.at[came, self.rows(h)], 3, h, 3 - came)
+
+    def order(self):
+        if self.square:
+            return [(1, 1), (2, 0), (1, 0), (2, 1)]
+        return [(k, h) for k in range(1, self.count) for h in range(2)]
+
+    def begin(self):
+        for k, h in self.order():
+            self.own(k, h).start()
+
+    def relay(self):
+        if self.square:
+            for k, h in ((1, 1), (2, 0)):
+                self.own(k, h).wait_recv()
+                self.onward(h).start()
+
+    def take(self, k):
+        for h in range(2):
+            if not (self.square and (k, h) in ((1, 1), (2, 0))):
+                self.copy(self.own_ref.at[self.rows(h)], k, h, k).wait_recv()
+
+    def sent(self):
+        for k, h in self.order():
+            self.own(k, h).wait_send()
+        if self.square:
+            for h in range(2):
+                self.onward(h).wait_send()
+
+
+class Parts:
+    def __init__(self, count, parts_ref, got_ref, send_sem, recv_sem):
+        self.parts_ref, self.got_ref = parts_ref, got_ref
+        self.send_sem, self.recv_sem = send_sem, recv_sem
+        self.count, self.square = count, count == 4
+        self.half = parts_ref.shape[1] // 2
+
+    def rows(self, h):
+        return pl.ds(h * self.half, self.half)
+
+    def copy(self, k, h):
+        peer = 1 + h if self.square and k == 3 else k
+        source, target = self.parts_ref.at[k, self.rows(h)], self.got_ref.at[k, self.rows(h)]
+        return send(source, target, self.send_sem.at[k, h], self.recv_sem.at[k, h], peer_of(peer))
+
+    def put(self, k, part):
+        self.parts_ref[k] = part.astype(bf16)
+        for h in range(2):
+            if not (self.square and (k, h) in ((1, 1), (2, 0))):
+                self.copy(k, h).start()
+
+    def merge(self):
+        if self.square:
+            for k, h in ((2, 0), (1, 1)):
+                self.copy(3, h).wait_recv()
+                rows = slice(h * self.half, (h + 1) * self.half)
+                total = self.parts_ref[k, rows].astype(f32) + self.got_ref[3, rows].astype(f32)
+                self.parts_ref[k, rows] = total.astype(bf16)
+                self.copy(k, h).start()
+
+    def total(self, own):
+        for k in range(1, 3 if self.square else self.count):
+            for h in range(2):
+                self.copy(k, h).wait_recv()
+            own = own + self.got_ref[k].astype(f32)
+        return own
+
+    def sent(self):
+        for k in range(1, self.count):
+            for h in range(2):
+                self.copy(k, h).wait_send()
+
+
+class Loads:
+    def __init__(self, sources, targets, sem):
+        self.copies = [
+            pltpu.make_async_copy(source, target, sem.at[i])
+            for i, (source, target) in enumerate(zip(sources, targets))
+        ]
+        for copy in self.copies:
+            copy.start()
+
+    def take(self, *which):
+        for i in which:
+            self.copies[i].wait()
+
+
 def gate_and_up(block, expand_ref, gate_start, up_start, size):
     if size % 128:
         both = matmul(block, expand_ref[:, gate_start : up_start + size])
@@ -662,35 +867,22 @@
 
 
 def feed_kernel(
-    count, turns, low_ref, mid_ref, expand_ref, down_ref,
+    count, low_ref, mid_ref, expand_any, down_any,
     out_ref, blocks_ref, kept_gate_ref, kept_up_ref,
-    act_ref, part_ref, sent_ref, got_ref, send_sem, recv_sem, send_sem2, recv_sem2, turn_sem,
+    expand_ref, down_ref, act_ref, part_ref, sent_ref, got_ref,
+    send_sem, recv_sem, send_sem2, recv_sem2, load_sem,
 ):
     units = down_ref.shape[0]
-    if turns:
-        section, ctx, fsdp = place_of()
-        greet_all([peer_of(k) for k in range(1, count)] + [(1 - section, ctx, fsdp)])
-
-        @pl.when(section == 1)
-        def _():
-            pl.semaphore_wait(turn_sem, 1)
-    else:
-        greet(count)
-    for k in range(1, count):
-        remote(low_ref, blocks_ref.at[k], send_sem, recv_sem, k).start()
-    if turns:
-
-        @pl.when(section == 0)
-        def _():
-            for k in range(1, count):
-                remote(low_ref, blocks_ref.at[k], send_sem, recv_sem, k).wait_send()
-            pl.semaphore_signal(
-                turn_sem, inc=1, device_id=(1 - section, ctx, fsdp), device_id_type=MESH
-            )
+    loads = Loads((expand_any, down_any), (expand_ref, down_ref), load_sem)
+    rows = Rows(count, low_ref, blocks_ref, send_sem, recv_sem)
+    parts = Parts(count, sent_ref, got_ref, send_sem2, recv_sem2)
+    greet(count)
+    rows.begin()
     blocks_ref[0] = low_ref[...]
+    loads.take(0, 1)
     for k in range(count):
         if k:
-            remote(low_ref, blocks_ref.at[k], send_sem, recv_sem, k).wait_recv()
+            rows.take(k)
         block = blocks_ref[k]
         for gate_start, up_start, start, size in unit_chunks(units):
             gate, up = gate_and_up(block, expand_ref, gate_start, up_start, size)
@@ -699,36 +891,23 @@
             act_ref[:, start : start + size] = (gate / (1.0 + jnp.exp(-gate)) * up).astype(bf16)
         part = matmul(act_ref[...], down_ref[...])
         if k:
-            sent_ref[k] = part.astype(bf16)
-            remote(sent_ref.at[k], got_ref.at[k], send_sem2, recv_sem2, k).start()
+            parts.put(k, part)
         else:
-            part_ref[...] = part
-    total = mid_ref[...] + part_ref[...]
-    for k in range(1, count):
-        remote(sent_ref.at[k], got_ref.at[k], send_sem2, recv_sem2, k).wait_recv()
-        total = total + got_ref[k].astype(f32)
-    out_ref[...] = total.astype(bf16)
-    for k in range(1, count):
-        remote(sent_ref.at[k], got_ref.at[k], send_sem2, recv_sem2, k).wait_send()
-    if turns:
-
-        @pl.when(section == 1)
-        def _():
-            for k in range(1, count):
-                remote(low_ref, blocks_ref.at[k], send_sem, recv_sem, k).wait_send()
-    else:
-        for k in range(1, count):
-            remote(low_ref, blocks_ref.at[k], send_sem, recv_sem, k).wait_send()
-
-
-def feed(layer, second_normed, middle, turns):
+            part_ref[...] = part + mid_ref[...]
+            rows.relay()
+    parts.merge()
+    out_ref[...] = parts.total(part_ref[...]).astype(bf16)
+    rows.sent()
+    parts.sent()
+
+
+def feed(layer, second_normed, middle):
     expand_w, down_w = layer[4:]
     count = lax.axis_size(CTX)
     rows, width = second_normed.shape
     units = down_w.shape[0]
-    sems = [pltpu.SemaphoreType.DMA((count,))] * 4
     return call(
-        functools.partial(feed_kernel, count, turns),
+        functools.partial(feed_kernel, count),
         [
             ((rows, width), bf16),
             ((count, rows, width), bf16),
@@ -736,33 +915,43 @@
             ((count, rows, units), bf16),
         ],
         [
+            VMEM(expand_w.shape, bf16),
+            VMEM(down_w.shape, bf16),
             VMEM((rows, units), bf16),
             VMEM((rows, width), f32),
             VMEM((count, rows, width), bf16),
             VMEM((count, rows, width), bf16),
         ]
-        + sems
-        + [pltpu.SemaphoreType.REGULAR],
-        3 if turns else 9,
-        second_normed, middle, expand_w, down_w,
+        + [dma(count, 2)] * 4
+        + [dma(2)],
+        3,
+        second_normed, middle, expand_w, down_w, far=(2, 3),
     )
 
 
 def feed_back_kernel(
-    count, grad_ref, mid_ref, g2_ref, blocks_ref, kept_gate_ref, kept_up_ref, expand_ref, down_ref,
+    count, grad_ref, mid_ref, g2_ref, blocks_any, kept_gate_any, kept_up_any, expand_any, down_any,
     dmid_ref, gain_ref, dexpand_ref, ddown_ref,
+    blocks_ref, kept_gate_ref, kept_up_ref, expand_ref, down_ref,
     grads_ref, act_ref, dwide_ref, part_ref, sent_ref, got_ref,
-    send_sem, recv_sem, send_sem2, recv_sem2,
+    send_sem, recv_sem, send_sem2, recv_sem2, load_sem,
 ):
     rows, width = grad_ref.shape
     units = down_ref.shape[0]
+    loads = Loads(
+        (down_any, kept_gate_any, kept_up_any, expand_any, blocks_any),
+        (down_ref, kept_gate_ref, kept_up_ref, expand_ref, blocks_ref),
+        load_sem,
+    )
+    gather = Rows(count, grad_ref, grads_ref, send_sem, recv_sem)
+    parts = Parts(count, sent_ref, got_ref, send_sem2, recv_sem2)
     greet(count)
-    for k in range(1, count):
-        remote(grad_ref, grads_ref.at[k], send_sem, recv_sem, k).start()
+    gather.begin()
     grads_ref[0] = grad_ref[...]
+    loads.take(0, 1, 2)
     for k in range(count):
         if k:
-            remote(grad_ref, grads_ref.at[k], send_sem, recv_sem, k).wait_recv()
+            gather.take(k)
         block = grads_ref[k]
         for gate_start, up_start, start, size in unit_chunks(units):
             cut = slice(start, start + size)
@@ -779,25 +968,27 @@
             else:
                 dwide_ref[k, :, gate_start : gate_start + size] = dgate
                 dwide_ref[k, :, up_start : up_start + size] = dup
+        if not k:
+            loads.take(3)
         part = matmul_nt(dwide_ref[k], expand_ref[...])
         if k:
-            sent_ref[k] = part.astype(bf16)
-            remote(sent_ref.at[k], got_ref.at[k], send_sem2, recv_sem2, k).start()
+            parts.put(k, part)
         else:
             part_ref[...] = part
+            gather.relay()
+    loads.take(4)
     tall = count * rows
     grads = grads_ref[...].reshape(tall, width)
-    for start, size in tiles(units // 128 * 128, 384) + [(units // 128 * 128, units % 128)] * (units % 128 > 0):
+    main = units // 128 * 128
+    for start, size in tiles(main, 384) + [(main, units - main)] * (units > main):
         act = act_ref[:, :, start : start + size].reshape(tall, size)
         ddown_ref[start : start + size, :] = matmul_tn(act, grads).astype(bf16)
+    parts.merge()
     blocks = blocks_ref[...].reshape(tall, width)
     for start, size in tiles(2 * units, 512):
         dwide = dwide_ref[:, :, start : start + size].reshape(tall, size)
         dexpand_ref[:, start : start + size] = matmul_tn(blocks, dwide).astype(bf16)
-    total = part_ref[...]
-    for k in range(1, count):
-        remote(sent_ref.at[k], got_ref.at[k], send_sem2, recv_sem2, k).wait_recv()
-        total = total + got_ref[k].astype(f32)
+    total = parts.total(part_ref[...])
     middle = mid_ref[...]
     scale = row_scale(middle)
     gain_ref[...] = jnp.sum(total * middle * scale, axis=0, keepdims=True)
@@ -806,9 +997,8 @@
     dmid_ref[...] = (
         grad_ref[...].astype(f32) + scale * scaled - middle * (scale * scale * scale * mean)
     )
-    for k in range(1, count):
-        remote(grad_ref, grads_ref.at[k], send_sem, recv_sem, k).wait_send()
-        remote(sent_ref.at[k], got_ref.at[k], send_sem2, recv_sem2, k).wait_send()
+    gather.sent()
+    parts.sent()
 
 
 def feed_back(layer, middle, blocks, kept_gate, kept_up, grad_out):
@@ -817,7 +1007,7 @@
     count = lax.axis_size(CTX)
     rows, width = grad_out.shape
     units = down_w.shape[0]
-    sems = [pltpu.SemaphoreType.DMA((count,))] * 4
+    brought = (blocks, kept_gate, kept_up, expand_w, down_w)
     return call(
         functools.partial(feed_back_kernel, count),
         [
@@ -826,7 +1016,8 @@
             ((width, 2 * units), bf16),
             ((units, width), bf16),
         ],
-        [
+        [VMEM(array.shape, bf16) for array in brought]
+        + [
             VMEM((count, rows, width), bf16),
             VMEM((count, rows, units), bf16),
             VMEM((count, rows, 2 * units), bf16),
@@ -834,9 +1025,10 @@
             VMEM((count, rows, width), bf16),
             VMEM((count, rows, width), bf16),
         ]
-        + sems,
+        + [dma(count, 2)] * 4
+        + [dma(5)],
         4,
-        grad_out, middle, second_gain, blocks, kept_gate, kept_up, expand_w, down_w,
+        grad_out, middle, second_gain, *brought, far=(3, 4, 5, 6, 7),
     )
 
 
@@ -844,7 +1036,7 @@
     ctx_count, fsdp_count, wide, low_ref, high_ref, small_ref, expand_ref, down_ref,
     projections_ref, output_ref, total_ref, expand_all_ref, down_all_ref,
     c_out, c_in, d_out, whole_ref, s_out, s_in,
-    c_send, c_recv, d_send, d_recv, s_send, s_recv, e_send, e_recv, e_own, *square_refs,
+    c_send, c_recv, d_send, d_recv, s_send, s_recv, e_send, e_recv, e_onward, e_own, *square_refs,
 ):
     section, ctx, fsdp = place_of()
     sister = (1 - section, ctx, fsdp)
@@ -859,6 +1051,8 @@
         for i, (source, target) in enumerate(zip(sources, targets))
     ]
 
+    owners = Owners(ctx_count, 1, sources, targets, e_send, e_recv, e_onward)
+
     def ahead(d):
         return (section, ctx, lax.rem(fsdp + d, fsdp_count))
 
@@ -906,11 +1100,13 @@
     s_out[1] = s_out[0] + s_in[0]
     for k in places:
         s_copy(*hops[k]).start()
+    owners.begin()
     line_sum(1)
+    steps.merge()
     c_out[0] = steps.end()
     for d in shards:
         c_copy(0, d).start()
-    every_owner(ctx_count, 1, "start", sources, targets, e_send, e_recv)
+    owners.relay()
     part = s_out[1]
     for k in places:
         s_copy(*hops[k]).wait_recv()
@@ -936,7 +1132,7 @@
             if size < piece:
                 first = start + size - wide
                 output_ref[:, first : first + piece - size] = block[:, size:]
-    from_owners(ctx_count, 1, targets, e_send, e_recv)
+    owners.end()
     steps.sent()
     for layer in (1, 0):
         for d in shards:
@@ -944,7 +1140,6 @@
         every_owner(
             ctx_count, layer, "wait", [d_out.at[layer]], [whole_ref], d_send.at[layer], d_recv
         )
-    every_owner(ctx_count, 1, "wait", sources, targets, e_send, e_recv)
     for hop in hops:
         s_copy(*hop).wait_send()
 
@@ -979,8 +1174,9 @@
             dma(2, fsdp_count), dma(2, fsdp_count),
             dma(2, 1, ctx_count), dma(1, 2, ctx_count),
             dma(hops), dma(hops),
-            dma(2, ctx_count), dma(2, 2, ctx_count), dma(2),
         ]
+        + owner_sems(ctx_count)
+        + [dma(2)]
         + square_scratch(ctx_count, low),
         7,
         low, high, small, expand_part, down_part, far_outs=(3, 4),
@@ -989,12 +1185,13 @@
 
 def settle_kernel(
     ctx_count, expand_ref, down_ref, expand_all_ref, down_all_ref,
-    expand_out, down_out, send_sem, recv_sem, own_sem,
+    expand_out, down_out, send_sem, recv_sem, onward_sem, own_sem,
 ):
     section, ctx, _ = place_of()
     greet_all(chip_square(ctx_count))
     sources, targets = (expand_ref, down_ref), (expand_out, down_out)
-    every_owner(ctx_count, 0, "start", sources, targets, send_sem, recv_sem)
+    owners = Owners(ctx_count, 0, sources, targets, send_sem, recv_sem, onward_sem)
+    owners.begin()
     kept = [
         pltpu.make_async_copy(source, target.at[ctx, section], own_sem.at[i])
         for i, (source, target) in enumerate(zip(sources, targets))
@@ -1018,8 +1215,8 @@
         for copy in loads:
             copy.wait()
 
-    from_owners(ctx_count, 0, targets, send_sem, recv_sem)
-    every_owner(ctx_count, 0, "wait", sources, targets, send_sem, recv_sem)
+    owners.relay()
+    owners.end()
 
 
 def spread_kernel(chunk, shards, side_width, block_ref, out_ref):
@@ -1039,7 +1236,7 @@
     expand_all, down_all = call(
         functools.partial(settle_kernel, ctx_count),
         [(expand_all.shape, bf16), (down_all.shape, bf16)],
-        [dma(2, ctx_count), dma(2, 2, ctx_count), dma(4)],
+        owner_sems(ctx_count) + [dma(4)],
         8,
         expand_part, down_part, expand_all, down_all,
         far=(2, 3),
@@ -1181,7 +1378,7 @@
         if fetched:
             weights[1] = fetched[0]
         kept = (hidden, normed, queries, every_kv, lse, context)
-        hidden, blocks, kept_gate, kept_up = feed(layers[layer], second_normed, middle, False)
+        hidden, blocks, kept_gate, kept_up = feed(layers[layer], second_normed, middle)
         sent.append(hidden)
         stored.append((middle, kept, blocks, kept_gate, kept_up))
 
@@ -1199,14 +1396,15 @@
         middle_grad, second_grad, expand_grad, down_grad = feed_back(
             layers[layer], middle, blocks, kept_gate, kept_up, grad
         )
-        if scattered:
-            expand_grad, down_grad, *scattered = lax.optimization_barrier(
-                (expand_grad, down_grad, *scattered)
-            )
         hidden_grad, first_grad, offset_grad, attn_grads[layer], *summed = attend_back(
             layers[layer], kept, middle_grad, place, attn_grads[1]
         )
-        earlier, scattered = scattered, (scatter(expand_grad), scatter(down_grad))
+        earlier = scattered
+        if earlier:
+            down_grad, _ = lax.optimization_barrier((down_grad, earlier[1]))
+            expand_grad, _ = lax.optimization_barrier((expand_grad, (earlier[0], attn_grads[0])))
+        down_part = scatter(down_grad)
+        scattered = (scatter(expand_grad), down_part)
         small_grads[layer] = jnp.concatenate([first_grad, offset_grad, second_grad], axis=1)[0]
         hidden_grads[layer] = hidden_grad
         grad = hidden_grad.astype(bf16)

time: 581 us -> 524 us (0.902)
  Pallas kernels: 495 us -> 427 us
  waiting for transfers between devices: 19.9 us -> 30.1 us
    pallas_call x11, Pallas kernels: 487 us -> 418 us  [call(): pl.pallas_call(kernel, out_shape=[jax.ShapeDtypeStruct(shape, kind) for s...]
    all_gather x4, waiting for transfers between devices: 3.2 us -> 14.9 us  [gather(): return lax.all_gather(piece, both, axis=0, tiled=True)]
  transfers between devices with their start and end apart: 14 -> 14, of which waited for: 5 -> 5; matrix products, arithmetic and copies ran while one was open for 6% -> 7% of each run, Pallas kernels for 60% -> 59%
where the time goes in v4:
time: 524 us; the launch traced here: 518 us
  Pallas kernels  427 us (81%)
  waiting for transfers between devices  30.1 us (6%)
  other arithmetic  28.4 us (5%)
  local copies, waits for them, and re-layouts  15.7 us (3%)
  between operations  14.9 us (3%)
    pallas_call x11, Pallas kernels, call(): pl.pallas_call(kernel, out_shape=[jax.ShapeDtypeStruct(shape, kind) for s...  418 us
    all_gather x4, waiting for transfers between devices, gather(): return lax.all_gather(piece, both, axis=0, tiled=True)  14.9 us
  transfers between devices with their start and end apart: 14, of which 5 were waited for; matrix products, arithmetic and copies ran while one was open for 7% of the time, Pallas kernels for 59%

profile of v4, /device:TPU:0, one launch (start us, length us, event | category | flops | bytes accessed | tf_op | source)
XLA Modules:
  0.0 518.5 jit_solution(7439219619578234334)
XLA Ops:
  7.3 1.2 select_bitcast_fusion.4
  8.9 1.2 collective-permute-done.3
  10.1 2.0 bitcast_select_fusion
  12.2 3.2 select_bitcast_fusion.6
  15.5 3.1 select_bitcast_fusion.5
  19.8 1.1 concatenate.41
  21.5 1.6 collective-permute-done.2
  23.1 1.1 broadcast_select_fusion.2
  30.2 1.0 copy.35.refs_7_.refs_6_
  31.9 2.8 broadcast_select_fusion
  34.7 33.2 %shard_map.177 = (bf16[896,2048]{1,0:T(8,128)(2,1)}, bf16[4,32,384]{2,1,0:T(8,128)(2,1)}) custom-call(bf16[224,2048]{1,0:T(8,128)(2,1)} %get-tuple-element.63.shard_ref, bf16[32,384]{1,0:T(8,128)(2,1)} %pad_maximum_fusion.4.small_ref), custom_call_target="tpu_custom_call" | custom-call | tf_op jit(solution)/shard_map/pallas_call | solution.py:116
  73.0 40.3 %shard_map.178 = (bf16[256,896]{1,0:T(8,128)(2,1)}, bf16[256,896]{1,0:T(8,128)(2,1)}, bf16[4,256,256]{2,1,0:T(8,128)(2,1)}, f32[16,256]{1,0:T(8,128)}, bf16[896,...) custom-call(bf16[256,896]{1,0:T(8,128)(2,1)} %dynamic-slice_bitcast_fusion.1.refs_0_, ...), custom_call_target="tpu_custom_call" | custom-call | tf_op jit(solution)/shard_map/pallas_call | solution.py:116
  113.4 37.5 %shard_map.179 = (bf16[256,896]{1,0:T(8,128)(2,1)}, bf16[4,256,896]{2,1,0:T(8,128)(2,1)}, bf16[4,256,1216]{2,1,0:T(8,128)(2,1)}, bf16[4,256,1216]{2,1,0:T(8,128)(2,1)}) custom-call(bf16[256,896]{1,0:T(8,128)(2,1)} %get-tuple-element.67.low_ref, f32[256,896]{1,0:T(8,128)} %get-tuple-element.68.mid_ref, ...), custom_call_target="tpu_custom_call" | custom-call | tf_op jit(solution)/shard_map/pallas_call | solution.py:116
  150.9 21.7 %shard_map.180 = (bf16[256,896]{1,0:T(8,128)(2,1)}, bf16[256,896]{1,0:T(8,128)(2,1)}, bf16[4,256,256]{2,1,0:T(8,128)(2,1)}, f32[16,256]{1,0:T(8,128)}, bf16[896,...) custom-call(bf16[256,896]{1,0:T(8,128)(2,1)} %get-tuple-element.69.refs_0_.refs_1_, ...), custom_call_target="tpu_custom_call" | custom-call | tf_op jit(solution)/shard_map/pallas_call | solution.py:116
  172.7 14.8 %all-gather.9.cloned.1.call-done.expand_any = bf16[896,2432]{1,0:T(8,128)(2,1)} async-done(((bf16[112,2432]{1,0:T(8,128)(2,1)}), bf16[896,2432]{1,0:T(8,128)(2,1)}) %all-gather.9.cloned.1.call-update) | async-done | bytes 4358160 | tf_op jit(solution)/shard_map/all_gather | solution.py:1346
  187.5 39.9 %shard_map.181 = (bf16[256,896]{1,0:T(8,128)(2,1)}, bf16[4,256,896]{2,1,0:T(8,128)(2,1)}, bf16[4,256,1216]{2,1,0:T(8,128)(2,1)}, bf16[4,256,1216]{2,1,0:T(8,128)(2,1)}) custom-call(bf16[256,896]{1,0:T(8,128)(2,1)} %get-tuple-element.71.low_ref, f32[256,896]{1,0:T(8,128)} %get-tuple-element.72.mid_ref, ...), custom_call_target="tpu_custom_call" | custom-call | tf_op jit(solution)/shard_map/pallas_call | solution.py:116
  227.3 38.4 %shard_map.182 = (f32[256,896]{1,0:T(8,128)}, f32[1,896]{1,0:T(1,128)}, bf16[896,2432]{1,0:T(8,128)(2,1)}, bf16[1216,896]{1,0:T(8,128)(2,1)}) custom-call(bf16[256,896]{1,0:T(8,128)(2,1)} %dynamic-slice_bitcast_fusion.grad_ref, f32[256,896]{1,0:T(8,128)} %get-tuple-element.72.mid_ref, f32[1,896]{1,0:T(1,128)} %reshape_squeeze.23.refs_3_.g2_ref, ...), custom_call_target="tpu_custom_call" | custom-call | tf_op jit(solution)/shard_map/pallas_call | solution.py:116
  266.4 28.7 %shard_map.183 = (f32[256,896]{1,0:T(8,128)}, f32[1,896]{1,0:T(1,128)}, f32[1,1152]{1,0:T(1,128)}, bf16[896,2048]{1,0:T(8,128)(2,1)}) custom-call(f32[256,896]{1,0:T(8,128)} %get-tuple-element.77.refs_0_, bf16[256,896]{1,0:T(8,128)(2,1)} %get-tuple-element.69.refs_0_.refs_1_, f32[1,896]{1,0:T(1,128)} %reshape_squeeze.21.refs_1_.refs_2_, ...), custom_call_target="tpu_custom_call" | custom-call | tf_op jit(solution)/shard_map/pallas_call | solution.py:116
  295.1 2.0 convert_element_type.28.grad_ref
  297.1 37.3 %shard_map.184 = (f32[256,896]{1,0:T(8,128)}, f32[1,896]{1,0:T(1,128)}, bf16[896,2432]{1,0:T(8,128)(2,1)}, bf16[1216,896]{1,0:T(8,128)(2,1)}) custom-call(bf16[256,896]{1,0:T(8,128)(2,1)} %convert_element_type.28.grad_ref, f32[256,896]{1,0:T(8,128)} %get-tuple-element.68.mid_ref, f32[1,896]{1,0:T(1,128)} %reshape_squeeze.20.refs_3_.g2_ref, ...), custom_call_target="tpu_custom_call" | custom-call | tf_op jit(solution)/shard_map/pallas_call | solution.py:116
  334.4 34.9 %shard_map.185 = (f32[256,896]{1,0:T(8,128)}, f32[1,896]{1,0:T(1,128)}, f32[1,1152]{1,0:T(1,128)}, bf16[896,2048]{1,0:T(8,128)(2,1)}, bf16[896,256]{1,0:T(8,128)(2,1)}) custom-call(f32[256,896]{1,0:T(8,128)} %get-tuple-element.87.refs_0_, bf16[256,896]{1,0:T(8,128)(2,1)} %dynamic-slice_bitcast_fusion.1.refs_0_.refs_1_, ...), custom_call_target="tpu_custom_call" | custom-call | tf_op jit(solution)/shard_map/pallas_call | solution.py:116
  369.5 1.1 copy-done.2
  370.9 1.0 convert_select_fusion
  374.1 1.3 collective-permute-done.4
  375.5 1.0 maximum_bitcast_fusion.1
  376.5 1.4 select_bitcast_fusion.1
  377.9 1.3 maximum_bitcast_fusion
  379.2 71.5 %shard_map.186 = (f32[224,1152]{1,0:T(8,128)}, f32[224,896]{1,0:T(8,128)}, f32[8,896]{1,0:T(8,128)}, bf16[4,2,112,2432]{3,2,1,0:T(8,128)(2,1)}, bf16[4,2,152,896]{3,2,1,0:T(8,128)(2,1)}) custom-call(bf16[896,2048]{1,0:T(8,128)(2,1)} %get-tuple-element.95.low_ref, bf16[896,256]{1,0:T(8,128)(2,1)} %get-tuple-element.96.high_ref, ...), custom_call_target="tpu_custom_call" | custom-call | tf_op jit(solution)/shard_map/pallas_call | solution.py:116
  454.1 9.3 %reduce-scatter.11.cloned.1.call-done.expand_ref = bf16[112,2432]{1,0:T(8,128)(2,1)} async-done(((bf16[896,2432]{1,0:T(8,128)(2,1)}), bf16[112,2432]{1,0:T(8,128)(2,1)}) %reduce-scatter.11.cloned.1.call-update) | async-done | bytes 544784 | tf_op jit(solution)/shard_map/reduce_scatter | solution.py:1386
  463.5 35.0 %shard_map.187 = (bf16[4,2,112,2432]{3,2,1,0:T(8,128)(2,1)}, bf16[4,2,152,896]{3,2,1,0:T(8,128)(2,1)}) custom-call(bf16[112,2432]{1,0:T(8,128)(2,1)} %reduce-scatter.11.cloned.1.call-done.expand_ref, bf16[152,896]{1,0:T(8,128)(2,1)} %reduce-scatter.15.cloned.1.call-done.down_ref, bf16[4,2,112,2432]{3,2,1,0:T(8,128)(2,1)} %get-tuple-element.112.expand_all_ref, ...), custom_call_target="tpu_custom_call" | custom-call | tf_op jit(solution)/shard_map/pallas_call | solution.py:116
  498.4 8.2 %shard_map.188 = f32[224,9728]{1,0:T(8,128)} custom-call(bf16[4,224,2432]{2,1,0:T(8,128)(2,1)} %bitcast.61), custom_call_target="tpu_custom_call" | custom-call | tf_op jit(solution)/shard_map/pallas_call | solution.py:1246
  506.7 2.3 convert.1
  (127 shorter events, 23.1 us)
Async XLA Ops:
  7.2 21.4 %copy-start = (bf16[2,1,256,896]{3,2,1,0:T(8,128)(2,1)S(1)}, bf16[2,1,256,896]{3,2,1,0:T(8,128)(2,1)}, u32[]{:S(2)}) copy-start(bf16[2,1,256,896]{3,2,1,0:T(8,128)(2,1)} %param.10) | copy-start | bytes 2752516
  7.2 106.2 %all-gather.7.cloned.1.call-start = ((), (), s32[]{:S(2)}) async-start(), calls=%async_computation.5 | async-start | bytes 2451456 | tf_op jit(solution)/shard_map/all_gather | solution.py:1346
  8.4 1.7 collective-permute-start.3
  12.1 101.3 %all-gather.5.cloned.1.call-start = ((), (), s32[]{:S(2)}) async-start(), calls=%async_computation.4 | async-start | bytes 4902912 | tf_op jit(solution)/shard_map/all_gather | solution.py:1346
  21.0 5.1 copy-start.13
  21.0 5.1 copy-start.16
  21.0 5.1 copy-start.17
  21.0 5.5 %copy-start.6 = (bf16[1,224,1152]{2,1,0:T(8,128)(2,1)S(1)}, bf16[1,224,1152]{2,1,0:T(8,128)(2,1)}, u32[]{:S(2)}) copy-start(bf16[1,224,1152]{2,1,0:T(8,128)(2,1)} %param.12) | copy-start | bytes 1548292
  21.0 5.5 %copy-start.8 = (bf16[1,224,896]{2,1,0:T(8,128)(2,1)S(1)}, bf16[1,224,896]{2,1,0:T(8,128)(2,1)}, u32[]{:S(2)}) copy-start(bf16[1,224,896]{2,1,0:T(8,128)(2,1)} %param.14) | copy-start | bytes 1204228
  21.0 2.0 collective-permute-start.2
  24.2 2.7 copy-start.22
  24.2 148.5 %all-gather.11.cloned.1.call-start = ((), (), s32[]{:S(2)}) async-start(), calls=%async_computation.7 | async-start | bytes 2451456 | tf_op jit(solution)/shard_map/all_gather | solution.py:1346
  24.9 162.5 %all-gather.9.cloned.1.call-start = ((), (), s32[]{:S(2)}) async-start(), calls=%async_computation.6 | async-start | bytes 4902912 | tf_op jit(solution)/shard_map/all_gather | solution.py:1346
  25.5 308.9 %reduce-scatter.13.cloned.1.call-start = ((), (), s32[]{:S(2)}) async-start(), calls=%async_computation.10 | async-start | bytes 2451456
  26.2 5.0 collective-permute-start.1
  26.7 5.2 %collective-permute-start = (bf16[224,2048]{1,0:T(8,128)(2,1)S(1)}, bf16[224,2048]{1,0:T(8,128)(2,1)}, u32[]{:S(2)}, u32[]{:S(2)}) collective-permute-start(bf16[224,2048]{1,0:T(8,128)(2,1)S(1)} %pad_maximum_fusion), channel_id=1, source_target_pairs={{0,16},{16,0},{1,17},{17,1},{2,18},{18,2},{3,19},{19,3},{4,20},{20... | collective-permute-start | bytes 2752520 | tf_op jit(solution)/shard_map/ppermute | solution.py:22
  26.9 2.5 copy-start.11
  27.0 7.8 %copy-start.12 = (s32[1,1,256]{2,1,0:T(1,128)}, s32[1,1,256]{2,1,0:T(1,128)S(1)}, u32[]{:S(2)}) copy-start(s32[1,1,256]{2,1,0:T(1,128)S(1)} %get-tuple-element.183) | copy-start | bytes 3076
  265.7 103.7 %reduce-scatter.9.cloned.1.call-start = ((), (), s32[]{:S(2)}) async-start(), calls=%async_computation.8 | async-start | bytes 4902912 | tf_op jit(solution)/shard_map/reduce_scatter | solution.py:1386
  266.3 187.8 %reduce-scatter.15.cloned.1.call-start = ((), (), s32[]{:S(2)}) async-start(), calls=%async_computation.11 | async-start | bytes 2451456
  334.4 129.1 %reduce-scatter.11.cloned.1.call-start = ((), (), s32[]{:S(2)}) async-start(), calls=%async_computation.9 | async-start | bytes 4902912 | tf_op jit(solution)/shard_map/reduce_scatter | solution.py:1386
  369.5 2.5 copy-start.3
  369.5 3.8 copy-start.15
  369.5 3.8 copy-start.20
  369.5 3.8 copy-start.21
  369.5 3.8 copy-start.14
  369.5 3.8 copy-start.18
  369.5 3.8 copy-start.19
  371.9 4.6 collective-permute-start.5
  372.8 2.6 collective-permute-start.4
  498.4 8.2 %copy-start.5 = (bf16[4,2,152,896]{3,2,1,0:T(8,128)(2,1)S(1)}, bf16[4,2,152,896]{3,2,1,0:T(8,128)(2,1)}, u32[]{:S(2)}) copy-start(bf16[4,2,152,896]{3,2,1,0:T(8,128)(2,1)} %get-tuple-element.115) | copy-start | bytes 6537220
  506.7 4.8 copy-start.1
  (5 other events, 9.0 us)
Sparse Core Ops, SparseCore 0:
  12.3 32.3 all-gather.6
  46.9 60.0 all-gather.4
  108.6 28.4 all-gather.10
  139.2 48.2 all-gather.8
  265.8 37.1 reduce-scatter.12
  305.2 50.4 reduce-scatter.8
  358.0 41.2 reduce-scatter.14
  401.6 61.8 reduce-scatter.10

commit v5 on v4

--- a/solution.py
+++ b/solution.py
@@ -215,7 +215,8 @@
 
 
 def collect_kernel(
-    ctx_count, fsdp_count, shard_ref, small_ref, w_ref, smalls_ref, s_send, s_recv, *sems
+    ctx_count, fsdp_count, sizes, shard_ref, small_ref, w_ref, vectors_ref, smalls_ref, s_send, s_recv,
+    *sems
 ):
     steps = Collect(ctx_count, fsdp_count, shard_ref, w_ref, sems)
 
@@ -234,17 +235,26 @@
     for d in steps.shards:
         came = smalls_ref.at[steps.behind(d)]
         send(came, came, s_send.at[d], s_recv.at[d], steps.sister).wait_recv()
+    for shard in range(fsdp_count):
+        rows = smalls_ref[shard].astype(f32)
+        for layer in range(2):
+            for i, size in enumerate(sizes):
+                row = 4 * layer + i
+                vectors_ref[row : row + 1, shard * size : (shard + 1) * size] = rows[
+                    16 * layer + i : 16 * layer + i + 1, :size
+                ]
     for d in steps.shards:
         small(d).wait_send()
 
 
-def collect(shard, small):
+def collect(shard, small, sizes):
     ctx_count, fsdp_count = lax.axis_size(CTX), lax.axis_size(FSDP)
     rows, width = shard.shape
     return call(
-        functools.partial(collect_kernel, ctx_count, fsdp_count),
-        [((fsdp_count * rows, width), bf16), ((fsdp_count,) + small.shape, bf16)],
-        [dma(fsdp_count), dma(fsdp_count)] + collect_sems(ctx_count, fsdp_count),
+        functools.partial(collect_kernel, ctx_count, fsdp_count, sizes),
+        [((fsdp_count * rows, width), bf16), ((8, fsdp_count * max(sizes)), f32)],
+        [VMEM((fsdp_count,) + small.shape, bf16), dma(fsdp_count), dma(fsdp_count)]
+        + collect_sems(ctx_count, fsdp_count),
         5,
         shard, small, far_outs=(0,),
     )
@@ -338,26 +348,24 @@
 
 
 class Owners:
-    def __init__(self, ctx_count, layer, sources, targets, send_sem, recv_sem, onward_sem):
+    def __init__(self, ctx_count, layer, sources, targets, cuts, sems):
         self.layer, self.targets = layer, targets
-        self.send_sem, self.recv_sem, self.onward_sem = send_sem, recv_sem, onward_sem
+        self.send_sem, self.recv_sem, self.onward_sem = sems
         self.section, self.ctx, self.fsdp = place_of()
         self.count, self.square = ctx_count, ctx_count == 4
-        rows = sources[0].shape[0]
-        cut = rows * 5 // 7 // 16 * 16
-        self.square = self.square and 0 < cut < rows and rows % 16 == 0
-        if self.square:
-            low, high = pl.ds(0, cut), pl.ds(cut, rows - cut)
-            self.pieces = [(sources[0].at[low], 0, low), (sources[0].at[high], 0, high)]
-            self.pieces.append((sources[1], 1, None))
-        else:
-            self.pieces = [(source, i, None) for i, source in enumerate(sources)]
+        self.pieces = []
+        for i, source in enumerate(sources):
+            for h in range(2) if self.square else (0,):
+                cut = cuts[i][h] if self.square else None
+                self.pieces.append((source.at[cut] if self.square else source, i, cut, h))
+        self.all = range(len(self.pieces))
+        self.early = [(i, 2 - self.pieces[i][3]) for i in self.all if self.square]
         self.keeper = self.section == layer
 
     def spot(self, i, k, core):
-        _, which, rows = self.pieces[i]
+        _, which, cut, _ = self.pieces[i]
         spot = self.targets[which].at[flip(self.ctx, k), core]
-        return spot if rows is None else spot.at[rows]
+        return spot if cut is None else spot.at[cut]
 
     def peer(self, k):
         return (self.layer, flip(self.ctx, k), self.fsdp)
@@ -372,7 +380,7 @@
         )
 
     def onward(self, i, core):
-        came = 2 if i == 0 else 1
+        came = 2 - self.pieces[i][3]
         spot = self.spot(i, came, core)
         return send(
             spot, spot, self.onward_sem.at[i, core], self.recv_sem.at[i, core, 3], self.peer(3 - came)
@@ -380,8 +388,9 @@
 
     def outgoing(self):
         if self.square:
-            return [(1, 1), (2, 1), (0, 2), (0, 1), (1, 2), (2, 2)]
-        return [(i, k) for k in range(1, self.count) for i in range(len(self.pieces))]
+            late = [(i, 3 - k) for i, k in self.early]
+            return self.early + late
+        return [(i, k) for k in range(1, self.count) for i in self.all]
 
     def begin(self):
         for i, k in self.outgoing():
@@ -389,50 +398,227 @@
 
         @pl.when(jnp.logical_not(self.keeper))
         def _():
-            for i in range(len(self.pieces)):
+            for i in self.all:
                 self.own(i, 0).start()
 
     def arrival(self, i, core, k):
         spot = self.spot(i, k, core)
         recv = self.recv_sem.at[i, core, k]
-        send(spot, spot, self.send_sem.at[i, k], recv, (1 - self.section, self.ctx, self.fsdp)).wait_recv()
+        sister = (1 - self.section, self.ctx, self.fsdp)
+        send(spot, spot, self.send_sem.at[i, k], recv, sister).wait_recv()
 
     def relay(self):
         if self.square:
 
             @pl.when(self.keeper)
             def _():
-                for i, k in ((1, 1), (2, 1), (0, 2)):
+                for i, k in self.early:
                     for core in range(2):
                         self.arrival(i, core, k)
                         self.onward(i, core).start()
 
     def end(self):
-        early = ((1, 1), (2, 1), (0, 2)) if self.square else ()
-
         @pl.when(self.keeper)
         def _():
             for k in range(self.count):
                 for core in range(2):
-                    for i in range(len(self.pieces)):
-                        if (i, k) not in early and (k or core != self.layer):
+                    for i in self.all:
+                        if (i, k) not in self.early and (k or core != self.layer):
                             self.arrival(i, core, k)
             if self.square:
-                for i in range(3):
+                for i in self.all:
                     for core in range(2):
                         self.onward(i, core).wait_send()
 
         @pl.when(jnp.logical_not(self.keeper))
         def _():
-            for i in range(len(self.pieces)):
+            for i in self.all:
                 self.own(i, 0).wait_send()
 
         for i, k in self.outgoing():
             self.own(i, k).wait_send()
 
 
+def row_halves(rows):
+    cut = rows // 2 // 16 * 16
+    return (pl.ds(0, cut), pl.ds(cut, rows - cut))
+
+
+def column_halves(width):
+    cut = -(-width // 256) * 128
+    return ((slice(None), pl.ds(0, cut)), (slice(None), pl.ds(cut, width - cut)))
+
+
 def owner_sems(ctx_count):
-    return [dma(3, ctx_count), dma(3, 2, ctx_count), dma(3, 2)]
+    return [dma(4, ctx_count), dma(4, 2, ctx_count), dma(4, 2)]
+
+
+class LineSum:
+    def __init__(self, fsdp_count, grad_ref, done_ref, refs):
+        self.own_ref, self.a_ref, self.sum_ref, self.in_ref, self.a_sem, self.z_send, self.z_recv = refs
+        self.grad_ref, self.done_ref = grad_ref, done_ref
+        self.section, self.ctx, self.fsdp = place_of()
+        self.fsdp_count = fsdp_count
+        self.group = fsdp_count // 2
+        self.units = grad_ref.shape[0] // fsdp_count
+        self.sister = (1 - self.section, self.ctx, self.fsdp)
+        self.holds = self.fsdp // self.group == self.section
+
+    def part(self, core):
+        size = self.group * self.units
+        return self.grad_ref.at[pl.ds(pl.multiple_of(core * size, size), size)]
+
+    def load(self):
+        return pltpu.make_async_copy(self.part(self.section), self.own_ref, self.a_sem.at[2])
+
+    def chip(self):
+        source = self.part(1 - self.section)
+        return send(source, self.a_ref, self.a_sem.at[0], self.a_sem.at[1], self.sister)
+
+    def line(self, j):
+        device = (self.section, self.ctx, self.section * self.group + j)
+        source = self.sum_ref.at[pl.ds(j * self.units, self.units)]
+        return send(source, self.in_ref.at[self.fsdp], self.z_send.at[j], self.z_recv.at[self.fsdp], device)
+
+    def elsewhere(self, j):
+        return pl.when(self.section * self.group + j != self.fsdp)
+
+    def begin(self):
+        self.chip().start()
+        self.load().start()
+
+    def middle(self):
+        self.load().wait()
+        self.chip().wait_recv()
+        self.sum_ref[...] = (self.own_ref[...].astype(f32) + self.a_ref[...].astype(f32)).astype(bf16)
+        for j in range(self.group):
+
+            @self.elsewhere(j)
+            def _():
+                self.line(j).start()
+
+    def end(self):
+        @pl.when(self.holds)
+        def _():
+            start = lax.rem(self.fsdp, self.group) * self.units
+            total = self.sum_ref[pl.ds(pl.multiple_of(start, self.units), self.units)].astype(f32)
+            for d in range(1, self.fsdp_count):
+                came = lax.rem(self.fsdp + d, self.fsdp_count)
+                spot = self.in_ref.at[came]
+                send(spot, spot, self.z_send.at[0], self.z_recv.at[came], self.sister).wait_recv()
+                total = total + self.in_ref[came].astype(f32)
+            self.done_ref[...] = total.astype(bf16)
+
+    def sent(self):
+        self.chip().wait_send()
+        for j in range(self.group):
+
+            @self.elsewhere(j)
+            def _():
+                self.line(j).wait_send()
+
+
+def line_scratch(fsdp_count, grad):
+    units, width = grad.shape
+    half = VMEM((units // 2, width), bf16)
+    shards = VMEM((fsdp_count, units // fsdp_count, width), bf16)
+    return [half, half, half, shards, dma(3), dma(fsdp_count), dma(fsdp_count)]
+
+
+class Handout:
+    def __init__(self, ctx_count, fsdp_count, layer, done_ref, all_ref, refs):
+        self.own_sem, self.o_send, self.o_recv, self.n_send = refs
+        self.layer, self.done_ref, self.all_ref = layer, done_ref, all_ref
+        self.section, self.ctx, self.fsdp = place_of()
+        self.count, self.square = ctx_count, ctx_count == 4
+        self.halves = column_halves(done_ref.shape[1])
+        self.holder = self.fsdp // (fsdp_count // 2)
+        self.holds = self.section == self.holder
+        self.keeps = self.section == layer
+        self.away = jnp.logical_and(self.holds, jnp.logical_not(self.keeps))
+        self.at_home = jnp.logical_and(self.holds, self.keeps)
+        self.early = ((1, 1), (2, 0)) if self.square else ()
+        late = ((1, 0), (2, 1)) if self.square else ()
+        pairs = [(k, h) for k in range(1, ctx_count) for h in range(2)]
+        self.sends = (*self.early, *late) if self.square else pairs
+
+    def spot(self, k, h):
+        return self.all_ref.at[flip(self.ctx, k)].at[self.halves[h]]
+
+    def peer(self, k):
+        return (self.layer, flip(self.ctx, k), self.fsdp)
+
+    def out(self, k, h):
+        source = self.done_ref.at[self.halves[h]]
+        return send(source, self.spot(0, h), self.o_send.at[k, h], self.o_recv.at[k, h], self.peer(k))
+
+    def onward(self, h):
+        came = 1 if h else 2
+        spot = self.spot(came, h)
+        return send(spot, spot, self.n_send.at[h], self.o_recv.at[3, h], self.peer(3 - came))
+
+    def arrival(self, k, h):
+        spot = self.spot(k, h)
+        sister = (1 - self.section, self.ctx, self.fsdp)
+        send(spot, spot, self.o_send.at[k, h], self.o_recv.at[k, h], sister).wait_recv()
+
+    def kept(self):
+        return pltpu.make_async_copy(self.done_ref, self.all_ref.at[self.ctx], self.own_sem.at[0])
+
+    def begin(self):
+        @pl.when(self.holds)
+        def _():
+            for k, h in self.sends:
+                self.out(k, h).start()
+
+        @pl.when(self.away)
+        def _():
+            for h in range(2):
+                self.out(0, h).start()
+
+        @pl.when(self.at_home)
+        def _():
+            self.kept().start()
+
+    def relay(self):
+        @pl.when(self.keeps)
+        def _():
+            for k, h in self.early:
+                self.arrival(k, h)
+                self.onward(h).start()
+
+    def end(self):
+        @pl.when(self.keeps)
+        def _():
+            for k in range(1, self.count):
+                for h in range(2):
+                    if (k, h) not in self.early:
+                        self.arrival(k, h)
+            for _, h in self.early:
+                self.onward(h).wait_send()
+
+        @pl.when(jnp.logical_and(self.keeps, jnp.logical_not(self.holds)))
+        def _():
+            for h in range(2):
+                self.arrival(0, h)
+
+        @pl.when(self.holds)
+        def _():
+            for k, h in self.sends:
+                self.out(k, h).wait_send()
+
+        @pl.when(self.away)
+        def _():
+            for h in range(2):
+                self.out(0, h).wait_send()
+
+        @pl.when(self.at_home)
+        def _():
+            self.kept().wait()
+
+
+def handout_sems(ctx_count):
+    return [dma(1), dma(ctx_count, 2), dma(ctx_count, 2), dma(2)]
 
 
 def chip_square(ctx_count):
@@ -461,9 +647,9 @@
     return jnp.where(lane // HEAD_DIM == group, moved, 0.0).astype(bf16)
 
 
-def attend_kernel(count, fsdp_count, fetch, *refs):
-    x_ref, g1_ref, bias_ref, g2_ref, w_ref, cos_ref, sin_ref, kpos_ref, qpos_ref = refs[:9]
-    refs = refs[9:]
+def attend_kernel(count, fsdp_count, layer, fetch, *refs):
+    x_ref, vectors_ref, w_ref, cos_ref, sin_ref, kpos_ref, qpos_ref = refs[:7]
+    refs = refs[7:]
     shard_ref, refs = (refs[0], refs[1:]) if fetch else (None, refs)
     normed_ref, q_ref, kv_ref, lse_ref, ctx_ref, mid_ref, low2_ref = refs[:7]
     refs = refs[7:]
@@ -481,16 +667,17 @@
     else:
         greet(count)
     x = x_ref[...].astype(f32)
-    normed = (x * row_scale(x) * g1_ref[...]).astype(bf16)
+    gain1, bias, gain2 = (vectors_ref[4 * layer + i : 4 * layer + i + 1, :] for i in range(3))
+    normed = (x * row_scale(x) * gain1[:, :width]).astype(bf16)
     normed_ref[...] = normed
     cos, sin = cos_ref[...], sin_ref[...]
-    kv = matmul(normed, w_ref[:, width:wide]) + bias_ref[:, width:wide]
+    kv = matmul(normed, w_ref[:, width:wide]) + bias[:, width:wide]
     keys = kv[:, :pair]
     kv_ref[0, :, :pair] = (keys * cos + turn_tile(keys) * sin).astype(bf16)
     kv_ref[0, :, pair:] = kv[:, pair:].astype(bf16)
     for k in range(1, count):
         remote(kv_ref.at[0], kv_ref.at[k], send_sem, recv_sem, k).start()
-    merged = matmul(normed, w_ref[:, :width]) + bias_ref[:, :width]
+    merged = matmul(normed, w_ref[:, :width]) + bias[:, :width]
     for start, size in tiles(width, 2 * HEAD_DIM):
         part = merged[:, start : start + size]
         turned_part = (part * cos + turn_tile(part) * sin) * HEAD_DIM ** (-0.5)
@@ -531,7 +718,7 @@
     ctx_ref[...] = context.astype(bf16)
     middle = x + matmul(context.T.astype(bf16), w_ref[:, wide:])
     mid_ref[...] = middle
-    low2_ref[...] = (middle * row_scale(middle) * g2_ref[...]).astype(bf16)
+    low2_ref[...] = (middle * row_scale(middle) * gain2[:, :width]).astype(bf16)
     for k in range(1, count):
         remote(kv_ref.at[0], kv_ref.at[k], send_sem, recv_sem, k).wait_send()
     if fetch:
@@ -539,21 +726,19 @@
 
 
 def attend(layer, hidden, place, shard=None):
-    first_gain, bias, second_gain, weights = layer[:4]
+    index, vectors, weights = layer[:3]
     cosine, sine, key_positions, query_positions = place
     rows, width = hidden.shape
     count = lax.axis_size(CTX)
-    wide = bias.shape[1]
+    wide = weights.shape[1] - width
     pair = (wide - width) // 2
     keys = count * rows
     heads = width // HEAD_DIM
     fetch = shard is not None
     fsdp_count = lax.axis_size(FSDP)
-    args = (
-        hidden, first_gain, bias, second_gain, weights, cosine, sine, key_positions, query_positions,
-    )
+    args = (hidden, vectors, weights, cosine, sine, key_positions, query_positions)
     return call(
-        functools.partial(attend_kernel, count, fsdp_count, fetch),
+        functools.partial(attend_kernel, count, fsdp_count, index, fetch),
         [
             ((rows, width), bf16),
             ((rows, width), bf16),
@@ -580,16 +765,16 @@
     )
 
 
-def attend_back_kernel(count, carried, *refs):
+def attend_back_kernel(count, layer, carried, *refs):
     (
-        dmid_ref, x_ref, g1_ref, w_ref, cos_ref, sin_ref, kpos_ref, qpos_ref,
+        dmid_ref, x_ref, vectors_ref, w_ref, cos_ref, sin_ref, kpos_ref, qpos_ref,
         normed_ref, q_ref, kv_ref, lse_ref, ctx_ref,
     ) = refs[:13]
     refs = refs[13:]
-    load_ref, refs = (refs[0], refs[1:]) if carried else (None, refs)
+    (load_ref, expand_ref), refs = (refs[:2], refs[2:]) if carried else ((None, None), refs)
     dh_ref, gain_ref, bias_ref, grad_ref = refs[:4]
     refs = refs[4:]
-    summed_ref, refs = (refs[0], refs[1:]) if carried else (None, refs)
+    (summed_ref, expand_all_ref), refs = (refs[:2], refs[2:]) if carried else ((None, None), refs)
     (
         mask_ref, p_ref, dp_ref, ds_ref, kt_ref, dctx_ref, dq_ref, dkv_ref, out_ref, in_ref,
         merged_ref, low_ref, send_sem, recv_sem, *scratch,
@@ -600,9 +785,19 @@
     heads = width // HEAD_DIM
     group_size = heads // (pair // HEAD_DIM)
     if carried:
-        steps = SquareSum(count, load_ref, *scratch[:3], scratch[3:])
-        greet_all([peer_of(k) for k in range(1, count)] + [steps.sister])
+        section, ctx, _ = place_of()
+        steps = SquareSum(count, load_ref, *scratch[:3], scratch[3:7])
+        halves = [row_halves(expand_ref.shape[0])]
+        owners = Owners(count, 1, [expand_ref], [expand_all_ref], halves, scratch[7:10])
+        kept = pltpu.make_async_copy(expand_ref, expand_all_ref.at[ctx, section], scratch[10].at[0])
+        greet_all(chip_square(count))
         steps.begin()
+        owners.begin()
+
+        @pl.when(owners.keeper)
+        def _():
+            kept.start()
+
     else:
         greet(count)
     low = dmid_ref[...].astype(bf16)
@@ -639,9 +834,11 @@
         dq_ref[head * HEAD_DIM : (head + 1) * HEAD_DIM, :] = (
             matmul(key_rows, ds_ref[...]) * HEAD_DIM ** (-0.5)
         )
-        if carried and head == 1:
+        if carried and head == heads // 5:
             steps.middle()
-        if carried and head == heads // 2:
+        if carried and head == heads // 3:
+            owners.relay()
+        if carried and head == heads * 2 // 3:
             steps.merge()
     for k in range(1, count):
         out_ref[k] = dkv_ref[k].astype(bf16)
@@ -676,39 +873,49 @@
     x = x_ref[...].astype(f32)
     scale = row_scale(x)
     gain_ref[...] = jnp.sum(normed_grad * x * scale, axis=0, keepdims=True)
-    scaled = normed_grad * g1_ref[...]
+    scaled = normed_grad * vectors_ref[4 * layer : 4 * layer + 1, :width]
     mean = jnp.mean(scaled * x, axis=-1, keepdims=True)
-    dh_ref[...] = dmid_ref[...] + scale * scaled - x * (scale * scale * scale * mean)
+    hidden_grad = dmid_ref[...] + scale * scaled - x * (scale * scale * scale * mean)
+    dh_ref[...] = hidden_grad.astype(dh_ref.dtype)
     for k in range(1, count):
         remote(out_ref.at[k], in_ref.at[k], send_sem, recv_sem, k).wait_send()
     if carried:
         summed_ref[...] = steps.end()
         steps.sent()
-
-
-def attend_back(layer, kept, middle_grad, place, load=None):
-    first_gain, bias, second_gain, weights = layer[:4]
+        owners.end()
+
+        @pl.when(owners.keeper)
+        def _():
+            kept.wait()
+
+
+def attend_back(layer, kept, middle_grad, place, load=()):
+    index, vectors, weights = layer[:3]
     cosine, sine, key_positions, query_positions = place
     hidden, normed, queries, every_kv, lse, context = kept
     rows, width = hidden.shape
     count = lax.axis_size(CTX)
-    wide = bias.shape[1]
+    wide = weights.shape[1] - width
     pair = (wide - width) // 2
     keys = count * rows
-    carried = load is not None
+    carried = bool(load)
     args = (
-        middle_grad, hidden, first_gain, weights, cosine, sine, key_positions, query_positions,
+        middle_grad, hidden, vectors, weights, cosine, sine, key_positions, query_positions,
         normed, queries, every_kv, lse, context,
     )
     return call(
-        functools.partial(attend_back_kernel, count, carried),
+        functools.partial(attend_back_kernel, count, index, carried),
         [
-            ((rows, width), f32),
+            ((rows, width), bf16 if index else f32),
             ((1, width), f32),
             ((1, wide), f32),
             ((width, wide + width), bf16),
         ]
-        + [((width, (wide + width) // (2 * count)), bf16)] * carried,
+        + (
+            [((width, (wide + width) // (2 * count)), bf16), ((count, 2) + load[1].shape, bf16)]
+            if carried
+            else []
+        ),
         [
             VMEM((count, rows, rows), f32),
             VMEM((count, rows, rows), f32),
@@ -725,9 +932,10 @@
             dma(count),
             dma(count),
         ]
-        + (square_scratch(count, load) if carried else []),
+        + (square_scratch(count, load[0]) + owner_sems(count) + [dma(1)] if carried else []),
         6 if carried else 2,
-        *args, *([load] if carried else []),
+        *args, *load,
+        far_outs=(5,) if carried else (),
     )
 
 
@@ -747,6 +955,8 @@
 def unpack_units(packed):
     units = packed.shape[-1] // 2
     main = units // 128 * 128
+    if units == main:
+        return packed[..., :main], packed[..., main:]
     gate = jnp.concatenate([packed[..., :main], packed[..., 2 * main : main + units]], axis=-1)
     up = jnp.concatenate([packed[..., main : 2 * main], packed[..., main + units :]], axis=-1)
     return gate, up
@@ -902,7 +1112,7 @@
 
 
 def feed(layer, second_normed, middle):
-    expand_w, down_w = layer[4:]
+    expand_w, down_w = layer[3:]
     count = lax.axis_size(CTX)
     rows, width = second_normed.shape
     units = down_w.shape[0]
@@ -929,13 +1139,21 @@
     )
 
 
-def feed_back_kernel(
-    count, grad_ref, mid_ref, g2_ref, blocks_any, kept_gate_any, kept_up_any, expand_any, down_any,
-    dmid_ref, gain_ref, dexpand_ref, ddown_ref,
-    blocks_ref, kept_gate_ref, kept_up_ref, expand_ref, down_ref,
-    grads_ref, act_ref, dwide_ref, part_ref, sent_ref, got_ref,
-    send_sem, recv_sem, send_sem2, recv_sem2, load_sem,
-):
+def feed_back_kernel(count, fsdp_count, layer, carried, *refs):
+    (
+        grad_ref, mid_ref, vectors_ref,
+        blocks_any, kept_gate_any, kept_up_any, expand_any, down_any,
+    ) = refs[:8]
+    refs = refs[8:]
+    line_ref, refs = (refs[0], refs[1:]) if carried else (None, refs)
+    dmid_ref, gain_ref, dexpand_ref, ddown_ref = refs[:4]
+    refs = refs[4:]
+    done_ref, refs = (refs[0], refs[1:]) if carried else (None, refs)
+    (
+        blocks_ref, kept_gate_ref, kept_up_ref, expand_ref, down_ref,
+        grads_ref, act_ref, dwide_ref, part_ref, sent_ref, got_ref,
+        send_sem, recv_sem, send_sem2, recv_sem2, load_sem, *scratch,
+    ) = refs
     rows, width = grad_ref.shape
     units = down_ref.shape[0]
     loads = Loads(
@@ -945,7 +1163,17 @@
     )
     gather = Rows(count, grad_ref, grads_ref, send_sem, recv_sem)
     parts = Parts(count, sent_ref, got_ref, send_sem2, recv_sem2)
-    greet(count)
+    if carried:
+        line = LineSum(fsdp_count, line_ref, done_ref, scratch)
+        section, ctx, fsdp = place_of()
+        greet_all(
+            [peer_of(k) for k in range(1, count)]
+            + [line.sister]
+            + [(section, ctx, lax.rem(fsdp + d, fsdp_count)) for d in range(1, fsdp_count)]
+        )
+        line.begin()
+    else:
+        greet(count)
     gather.begin()
     grads_ref[0] = grad_ref[...]
     loads.take(0, 1, 2)
@@ -976,6 +1204,8 @@
         else:
             part_ref[...] = part
             gather.relay()
+            if carried:
+                line.middle()
     loads.take(4)
     tall = count * rows
     grads = grads_ref[...].reshape(tall, width)
@@ -988,34 +1218,40 @@
     for start, size in tiles(2 * units, 512):
         dwide = dwide_ref[:, :, start : start + size].reshape(tall, size)
         dexpand_ref[:, start : start + size] = matmul_tn(blocks, dwide).astype(bf16)
+    if carried:
+        line.end()
     total = parts.total(part_ref[...])
     middle = mid_ref[...]
     scale = row_scale(middle)
     gain_ref[...] = jnp.sum(total * middle * scale, axis=0, keepdims=True)
-    scaled = total * g2_ref[...]
+    scaled = total * vectors_ref[4 * layer + 2 : 4 * layer + 3, :width]
     mean = jnp.mean(scaled * middle, axis=-1, keepdims=True)
     dmid_ref[...] = (
         grad_ref[...].astype(f32) + scale * scaled - middle * (scale * scale * scale * mean)
     )
     gather.sent()
     parts.sent()
-
-
-def feed_back(layer, middle, blocks, kept_gate, kept_up, grad_out):
-    second_gain = layer[2]
-    expand_w, down_w = layer[4:]
+    if carried:
+        line.sent()
+
+
+def feed_back(layer, middle, blocks, kept_gate, kept_up, grad_out, load=()):
+    index, vectors = layer[:2]
+    expand_w, down_w = layer[3:]
     count = lax.axis_size(CTX)
     rows, width = grad_out.shape
     units = down_w.shape[0]
+    fsdp_count = lax.axis_size(FSDP)
     brought = (blocks, kept_gate, kept_up, expand_w, down_w)
     return call(
-        functools.partial(feed_back_kernel, count),
+        functools.partial(feed_back_kernel, count, fsdp_count, index, bool(load)),
         [
             ((rows, width), f32),
             ((1, width), f32),
             ((width, 2 * units), bf16),
             ((units, width), bf16),
-        ],
+        ]
+        + [((units // fsdp_count, width), bf16)] * len(load),
         [VMEM(array.shape, bf16) for array in brought]
         + [
             VMEM((count, rows, width), bf16),
@@ -1026,17 +1262,20 @@
             VMEM((count, rows, width), bf16),
         ]
         + [dma(count, 2)] * 4
-        + [dma(5)],
-        4,
-        grad_out, middle, second_gain, *brought, far=(3, 4, 5, 6, 7),
+        + [dma(5)]
+        + (line_scratch(fsdp_count, load[0]) if load else []),
+        4 + 7 * index,
+        grad_out, middle, vectors, *brought, *load, far=(3, 4, 5, 6, 7, 8),
     )
 
 
 def attn_sum_kernel(
-    ctx_count, fsdp_count, wide, low_ref, high_ref, small_ref, expand_ref, down_ref,
-    projections_ref, output_ref, total_ref, expand_all_ref, down_all_ref,
+    ctx_count, fsdp_count, wide, low_ref, high_ref, small_ref, down_ref,
+    act_zero_ref, act_one_ref, grad_zero_ref, grad_one_ref, down_grad_ref, expand_ref, expand_all_ref,
+    projections_ref, output_ref, total_ref, down_all_ref, act_ref, grad_ref, expand_out,
+    wide_ref, done_ref,
     c_out, c_in, d_out, whole_ref, s_out, s_in,
-    c_send, c_recv, d_send, d_recv, s_send, s_recv, e_send, e_recv, e_onward, e_own, *square_refs,
+    c_send, c_recv, d_send, d_recv, s_send, s_recv, *more,
 ):
     section, ctx, fsdp = place_of()
     sister = (1 - section, ctx, fsdp)
@@ -1044,14 +1283,22 @@
     rows = width // fsdp_count
     places = range(1, ctx_count)
     shards = range(1, fsdp_count)
-    steps = SquareSum(ctx_count, low_ref, *square_refs[:3], square_refs[3:])
-    sources, targets = (expand_ref, down_ref), (expand_all_ref, down_all_ref)
-    kept = [
-        pltpu.make_async_copy(source, target.at[ctx, section], e_own.at[i])
-        for i, (source, target) in enumerate(zip(sources, targets))
+    steps = SquareSum(ctx_count, low_ref, *more[:3], more[3:7])
+    halves = [row_halves(expand_ref.shape[0])]
+    owners = Owners(ctx_count, 0, [expand_ref], [expand_out], halves, more[7:10])
+    own_sem, swap_send, swap_recv = more[10:13]
+    kept = pltpu.make_async_copy(expand_ref, expand_out.at[ctx, section], own_sem.at[0])
+    load = pltpu.make_async_copy(expand_all_ref, expand_out, own_sem.at[1])
+    down = LineSum(fsdp_count, down_grad_ref, done_ref, more[13:20])
+    handouts = [
+        Handout(ctx_count, fsdp_count, 1, down_ref, down_all_ref, more[20:24]),
+        Handout(ctx_count, fsdp_count, 0, done_ref, down_all_ref, more[24:28]),
     ]
-
-    owners = Owners(ctx_count, 1, sources, targets, e_send, e_recv, e_onward)
+    layers = ((act_zero_ref, grad_zero_ref), (act_one_ref, wide_ref))
+
+    def swap(i, layer):
+        target = (act_ref, grad_ref)[i].at[section]
+        return send(layers[layer][i], target, swap_send.at[i], swap_recv.at[i], sister)
 
     def ahead(d):
         return (section, ctx, lax.rem(fsdp + d, fsdp_count))
@@ -1084,29 +1331,52 @@
 
     greet_all(chip_square(ctx_count) + [ahead(d) for d in shards])
     steps.begin()
+    down.begin()
+    owners.begin()
+
+    @pl.when(section == 0)
+    def _():
+        kept.start()
+
+    @pl.when(section == 1)
+    def _():
+        load.start()
+
+    wide_ref[...] = grad_one_ref[...].astype(f32)
+    for layer in range(2):
+
+        @pl.when(section != layer)
+        def _():
+            for i in range(2):
+                swap(i, layer).start()
+
+        @pl.when(section == layer)
+        def _():
+            for i, target in enumerate((act_ref, grad_ref)):
+                target[section] = layers[layer][i][...]
+
     s_out[0] = small_ref[...]
     s_copy(*hops[0]).start()
     c_out[1] = high_ref[...]
     for d in shards:
         c_copy(1, d).start()
 
-    @pl.when(section == 1)
-    def _():
-        for copy in kept:
-            copy.start()
-
     steps.middle()
+    down.middle()
+    handouts[0].begin()
+    owners.relay()
     s_copy(*hops[0]).wait_recv()
     s_out[1] = s_out[0] + s_in[0]
     for k in places:
         s_copy(*hops[k]).start()
-    owners.begin()
     line_sum(1)
     steps.merge()
     c_out[0] = steps.end()
     for d in shards:
         c_copy(0, d).start()
-    owners.relay()
+    handouts[0].relay()
+    down.end()
+    handouts[1].begin()
     part = s_out[1]
     for k in places:
         s_copy(*hops[k]).wait_recv()
@@ -1133,6 +1403,21 @@
                 first = start + size - wide
                 output_ref[:, first : first + piece - size] = block[:, size:]
     owners.end()
+    handouts[1].relay()
+    for handout in handouts:
+        handout.end()
+    down.sent()
+
+    @pl.when(section == 0)
+    def _():
+        kept.wait()
+
+    @pl.when(section == 1)
+    def _():
+        load.wait()
+
+    for i in range(2):
+        swap(i, 0).wait()
     steps.sent()
     for layer in (1, 0):
         for d in shards:
@@ -1143,13 +1428,8 @@
     for hop in hops:
         s_copy(*hop).wait_send()
 
-    @pl.when(section == 1)
-    def _():
-        for copy in kept:
-            copy.wait()
-
-
-def attn_sum(low, high, small, expand_part, down_part, wide):
+
+def attn_sum(low, high, small, down_one, acts, grads, down_grad, expand_part, expand_all, wide):
     ctx_count, fsdp_count = lax.axis_size(CTX), lax.axis_size(FSDP)
     width, both = low.shape
     rows = width // fsdp_count
@@ -1161,10 +1441,14 @@
             ((rows, wide), f32),
             ((rows, both - wide), f32),
             (small.shape, f32),
-            ((ctx_count, 2) + expand_part.shape, bf16),
-            ((ctx_count, 2) + down_part.shape, bf16),
+            ((ctx_count,) + down_one.shape, bf16),
+            ((2,) + acts[0].shape, bf16),
+            ((2,) + grads[0].shape, f32),
+            (expand_all.shape, bf16),
         ],
         [
+            VMEM(grads[0].shape, f32),
+            VMEM(down_one.shape, bf16),
             VMEM((2, width, piece), bf16),
             VMEM((2, fsdp_count, rows, piece), bf16),
             VMEM((2, rows, piece), bf16),
@@ -1175,84 +1459,41 @@
             dma(2, 1, ctx_count), dma(1, 2, ctx_count),
             dma(hops), dma(hops),
         ]
+        + square_scratch(ctx_count, low)
         + owner_sems(ctx_count)
-        + [dma(2)]
-        + square_scratch(ctx_count, low),
+        + [dma(2), dma(2), dma(2)]
+        + line_scratch(fsdp_count, down_grad)
+        + handout_sems(ctx_count) * 2,
         7,
-        low, high, small, expand_part, down_part, far_outs=(3, 4),
+        low, high, small, down_one, *acts, *grads, down_grad, expand_part, expand_all,
+        far=(8, 10), far_outs=(3,),
     )
 
 
-def settle_kernel(
-    ctx_count, expand_ref, down_ref, expand_all_ref, down_all_ref,
-    expand_out, down_out, send_sem, recv_sem, onward_sem, own_sem,
-):
-    section, ctx, _ = place_of()
-    greet_all(chip_square(ctx_count))
-    sources, targets = (expand_ref, down_ref), (expand_out, down_out)
-    owners = Owners(ctx_count, 0, sources, targets, send_sem, recv_sem, onward_sem)
-    owners.begin()
-    kept = [
-        pltpu.make_async_copy(source, target.at[ctx, section], own_sem.at[i])
-        for i, (source, target) in enumerate(zip(sources, targets))
-    ]
-    loads = [
-        pltpu.make_async_copy(source, target, own_sem.at[2 + i])
-        for i, (source, target) in enumerate(zip((expand_all_ref, down_all_ref), targets))
-    ]
-
-    @pl.when(section == 0)
-    def _():
-        for copy in kept:
-            copy.start()
-        for copy in kept:
-            copy.wait()
-
-    @pl.when(section == 1)
-    def _():
-        for copy in loads:
-            copy.start()
-        for copy in loads:
-            copy.wait()
-
-    owners.relay()
-    owners.end()
-
-
-def spread_kernel(chunk, shards, side_width, block_ref, out_ref):
+def spread_kernel(chunk, stride, shards, side_width, block_ref, out_ref):
     count = block_ref.shape[0]
     for where in range(count):
         sides = unpack_units(block_ref[where].astype(f32))
         for side, values in enumerate(sides):
             for shard in range(shards):
                 start = side * side_width + (shard * count + where) * chunk
-                out_ref[:, start : start + chunk] = values[:, shard * chunk : (shard + 1) * chunk]
-
-
-def finish(expand_part, down_part, expand_all, down_all, ff_width):
+                out_ref[:, start : start + chunk] = values[:, shard * stride : shard * stride + chunk]
+
+
+def finish(expand_all, ff_width, units):
     ctx_count, fsdp_count = lax.axis_size(CTX), lax.axis_size(FSDP)
-    half, packed = expand_part.shape
-    half_units, width = down_part.shape
-    expand_all, down_all = call(
-        functools.partial(settle_kernel, ctx_count),
-        [(expand_all.shape, bf16), (down_all.shape, bf16)],
-        owner_sems(ctx_count) + [dma(4)],
-        8,
-        expand_part, down_part, expand_all, down_all,
-        far=(2, 3),
-    )
+    half, packed = expand_all.shape[2:]
     rows = 2 * half
     step = 32 if rows % 32 == 0 else 16
-    grad_expand = pl.pallas_call(
-        functools.partial(spread_kernel, packed // 2 // fsdp_count, fsdp_count, ff_width),
+    stride = packed // 2 // fsdp_count
+    return pl.pallas_call(
+        functools.partial(spread_kernel, units, stride, fsdp_count, ff_width),
         grid=(rows // step,),
         out_shape=jax.ShapeDtypeStruct((rows, 2 * ff_width), f32),
         in_specs=[pl.BlockSpec((ctx_count, step, packed), lambda i: (0, i, 0))],
         out_specs=pl.BlockSpec((step, 2 * ff_width), lambda i: (i, 0)),
         compiler_params=pltpu.CompilerParams(vmem_limit_bytes=LIMIT),
     )(expand_all.reshape(ctx_count, rows, packed))
-    grad_down = down_all.astype(f32).reshape(2 * ctx_count * half_units, width)
-    return grad_expand, grad_down
 
 
 def per_device(
@@ -1279,6 +1520,7 @@
     ff_width = expand_weight.shape[2] // 2
     shard_units = down_weight.shape[1]
     units = shard_units // ctx_count
+    spare_units = -units % 16
     both = (FSDP, SECTION)
 
     def mine(array):
@@ -1325,10 +1567,13 @@
                     ],
                 )
             )
+            if spare_units:
+                pieces.append(jnp.zeros((shard_rows, spare_units), bf16))
         return jnp.concatenate(pieces, axis=1)
 
     expand_shard = pack_units(unit_columns(0), unit_columns(1))
     down_shard = lax.dynamic_slice_in_dim(down_weight[0], ctx * units, units)
+    down_shard = jnp.pad(down_shard, ((0, spare_units), (0, 0)))
 
     def halves(array):
         size = array.shape[0] // 2
@@ -1350,21 +1595,12 @@
     first_shard, small_pair = lax.optimization_barrier(
         (first_shard, small_pair, expand_pair[0], down_pair[0])
     )[:2]
-    weights, smalls = collect(first_shard, small_pair)
-    smalls = smalls.astype(f32)
+    weights, vectors = collect(first_shard, small_pair, (shard_rows, bias_part, shard_rows))
     weights = [weights, None]
     expands[1], downs[1] = gather(expand_pair[1]), gather(down_pair[1])
 
     def layer_of(layer):
-        first = 16 * layer
-        return (
-            smalls[:, first, :shard_rows].reshape(1, -1),
-            smalls[:, first + 1, :bias_part].reshape(1, -1),
-            smalls[:, first + 2, :shard_rows].reshape(1, -1),
-            weights[layer],
-            expands[layer],
-            downs[layer],
-        )
+        return (layer, vectors, weights[layer], expands[layer], downs[layer])
 
     layers = []
     hidden = source
@@ -1389,35 +1625,41 @@
     hidden_grads = [None, None]
     small_grads = [None, None]
     attn_grads = [None, None]
-    scattered = ()
-    summed = ()
     for layer in (1, 0):
         middle, kept, blocks, kept_gate, kept_up = stored[layer]
-        middle_grad, second_grad, expand_grad, down_grad = feed_back(
-            layers[layer], middle, blocks, kept_gate, kept_up, grad
+        load = () if layer else (down_grad,)
+        middle_grad, second_grad, expand_grad, down_grad, *summed = feed_back(
+            layers[layer], middle, blocks, kept_gate, kept_up, grad, load
         )
+        if layer:
+            expand_one = scatter(expand_grad)
+            load = ()
+        else:
+            expand_grad, expand_one = lax.optimization_barrier((expand_grad, expand_one))
+            expand_zero = scatter(expand_grad)
+            (down_one,) = summed
+            load = (attn_grads[1], expand_one)
         hidden_grad, first_grad, offset_grad, attn_grads[layer], *summed = attend_back(
-            layers[layer], kept, middle_grad, place, attn_grads[1]
+            layers[layer], kept, middle_grad, place, load
         )
-        earlier = scattered
-        if earlier:
-            down_grad, _ = lax.optimization_barrier((down_grad, earlier[1]))
-            expand_grad, _ = lax.optimization_barrier((expand_grad, (earlier[0], attn_grads[0])))
-        down_part = scatter(down_grad)
-        scattered = (scatter(expand_grad), down_part)
         small_grads[layer] = jnp.concatenate([first_grad, offset_grad, second_grad], axis=1)[0]
         hidden_grads[layer] = hidden_grad
-        grad = hidden_grad.astype(bf16)
+        grad = hidden_grad
 
     spare = -small_grads[0].shape[0] % model_width
     small_rows = [jnp.pad(vector, (0, spare)).reshape(-1, model_width) for vector in small_grads]
     small_count = small_rows[0].shape[0]
     rows_left = -2 * small_count % 8
     small_stack = jnp.pad(jnp.concatenate(small_rows), ((0, rows_left), (0, 0)))
-    grad_projections, grad_output, small_all, *gathered = attn_sum(
-        attn_grads[0], *summed, small_stack, *earlier, wide
+    attn_one, expand_one = summed
+    (
+        grad_projections, grad_output, small_all, down_all, activations, input_grads, expand_all,
+    ) = attn_sum(
+        attn_grads[0], attn_one, small_stack, down_one, sent, hidden_grads,
+        down_grad, expand_zero, expand_one, wide,
     )
-    grad_expand, grad_down = finish(*scattered, *gathered, ff_width)
+    grad_expand = finish(expand_all, ff_width, units)
+    grad_down = down_all[:, :units].astype(f32).reshape(shard_units, model_width)
     small_own = jnp.where(
         is_first, small_all[:small_count], small_all[small_count : 2 * small_count]
     ).reshape(-1)
@@ -1432,18 +1674,9 @@
         size = vector.shape[0] // fsdp_count
         return lax.dynamic_slice_in_dim(vector, fsdp * size, size)[None]
 
-    def from_both(pair):
-        own = jnp.where(is_first, pair[0], pair[1])
-        other = swap_sections(jnp.where(is_first, pair[1], pair[0]))
-        return jnp.stack(
-            [jnp.where(is_first, own, other), jnp.where(is_first, other, own)]
-        )[None, :, None]
-
-    activations = from_both(sent)
-    input_grads = from_both([hidden_grads[0], hidden_grads[1].astype(bf16).astype(f32)])
     return (
-        activations,
-        input_grads,
+        activations[None, :, None],
+        input_grads[None, :, None],
         part(first_all),
         grad_projections[None],
         part(offset_all[: model_width + pair_width]),

time: 524 us -> 505 us (0.964)
  Pallas kernels: 427 us -> 417 us
  other arithmetic: 28.4 us -> 20.4 us
    pallas_call x11 -> x10, Pallas kernels: 418 us -> 409 us  [call(): pl.pallas_call(kernel, out_shape=[jax.ShapeDtypeStruct(shape, kind) for s...]
  transfers between devices with their start and end apart: 14 -> 10, of which waited for: 5 -> 4; matrix products, arithmetic and copies ran while one was open for 7% -> 4% of each run, Pallas kernels for 59% -> 50%
where the time goes in v5:
time: 505 us; the launch traced here: 499 us
  Pallas kernels  417 us (83%)
  waiting for transfers between devices  31.6 us (6%)
  other arithmetic  20.4 us (4%)
  between operations  14.8 us (3%)
  local copies, waits for them, and re-layouts  13.1 us (3%)
    pallas_call x10, Pallas kernels, call(): pl.pallas_call(kernel, out_shape=[jax.ShapeDtypeStruct(shape, kind) for s...  409 us
    all_gather x4, waiting for transfers between devices, gather(): return lax.all_gather(piece, both, axis=0, tiled=True)  18.6 us
  transfers between devices with their start and end apart: 10, of which 4 were waited for; matrix products, arithmetic and copies ran while one was open for 4% of the time, Pallas kernels for 50%

profile of v5, /device:TPU:0, one launch (start us, length us, event | category | flops | bytes accessed | tf_op | source)
XLA Modules:
  0.0 499.3 jit_solution(12027150096996418490)
XLA Ops:
  7.3 1.2 select_bitcast_fusion
  8.9 1.2 collective-permute-done.3
  10.1 2.0 bitcast_select_fusion
  12.2 3.2 select_bitcast_fusion.2
  15.4 3.1 select_bitcast_fusion.1
  19.8 1.1 concatenate.41
  21.5 1.6 collective-permute-done.2
  23.0 1.1 broadcast_select_fusion.2
  27.5 1.0 pad_maximum_fusion.1
  28.5 0.8 dynamic-slice_bitcast_fusion.refs_0_.refs_1_
  29.3 0.8 dynamic-slice_bitcast_fusion.1.refs_0_
  30.1 1.0 copy.29.refs_5_.refs_6_
  31.8 2.8 broadcast_select_fusion
  34.7 33.3 %shard_map.177 = (bf16[896,2048]{1,0:T(8,128)(2,1)}, f32[8,1152]{1,0:T(8,128)}) custom-call(bf16[224,2048]{1,0:T(8,128)(2,1)} %get-tuple-element.65.shard_ref, bf16[32,384]{1,0:T(8,128)(2,1)} %pad_maximum_fusion.4.small_ref), custom_call_target="tpu_custom_call" | custom-call | tf_op jit(solution)/shard_map/pallas_call | solution.py:116
  68.0 40.5 %shard_map.178 = (bf16[256,896]{1,0:T(8,128)(2,1)}, bf16[256,896]{1,0:T(8,128)(2,1)}, bf16[4,256,256]{2,1,0:T(8,128)(2,1)}, f32[16,256]{1,0:T(8,128)}, bf16[896,...) custom-call(bf16[256,896]{1,0:T(8,128)(2,1)} %dynamic-slice_bitcast_fusion.refs_0_.r, ...), custom_call_target="tpu_custom_call" | custom-call | tf_op jit(solution)/shard_map/pallas_call | solution.py:116
  108.5 38.8 %shard_map.179 = (bf16[256,896]{1,0:T(8,128)(2,1)}, bf16[4,256,896]{2,1,0:T(8,128)(2,1)}, bf16[4,256,1216]{2,1,0:T(8,128)(2,1)}, bf16[4,256,1216]{2,1,0:T(8,128)(2,1)}) custom-call(bf16[256,896]{1,0:T(8,128)(2,1)} %get-tuple-element.69.low_ref, f32[256,896]{1,0:T(8,128)} %get-tuple-element.70.mid_ref.refs_1_, ...), custom_call_target="tpu_custom_call" | custom-call | tf_op jit(solution)/shard_map/pallas_call | solution.py:116
  147.3 21.5 %shard_map.180 = (bf16[256,896]{1,0:T(8,128)(2,1)}, bf16[256,896]{1,0:T(8,128)(2,1)}, bf16[4,256,256]{2,1,0:T(8,128)(2,1)}, f32[16,256]{1,0:T(8,128)}, bf16[896,...) custom-call(bf16[256,896]{1,0:T(8,128)(2,1)} %get-tuple-element.71.refs_0_.refs_1_.act_zero_ref, ...), custom_call_target="tpu_custom_call" | custom-call | tf_op jit(solution)/shard_map/pallas_call | solution.py:116
  168.9 18.5 %all-gather.9.cloned.1.call-done.expand_any.refs_6_ = bf16[896,2432]{1,0:T(8,128)(2,1)} async-done(((bf16[112,2432]{1,0:T(8,128)(2,1)}), bf16[896,2432]{1,0:T(8,128)(2,1)}) %all-gather.9.cloned.1.call-update) | async-done | bytes 4358160 | tf_op jit(solution)/shard_map/all_gather | solution.py:1591
  187.4 39.9 %shard_map.181 = (bf16[256,896]{1,0:T(8,128)(2,1)}, bf16[4,256,896]{2,1,0:T(8,128)(2,1)}, bf16[4,256,1216]{2,1,0:T(8,128)(2,1)}, bf16[4,256,1216]{2,1,0:T(8,128)(2,1)}) custom-call(bf16[256,896]{1,0:T(8,128)(2,1)} %get-tuple-element.74.low_ref, f32[256,896]{1,0:T(8,128)} %get-tuple-element.73.mid_ref.refs_1_, ...), custom_call_target="tpu_custom_call" | custom-call | tf_op jit(solution)/shard_map/pallas_call | solution.py:116
  227.4 37.8 %shard_map.182 = (f32[256,896]{1,0:T(8,128)}, f32[1,896]{1,0:T(1,128)}, bf16[896,2432]{1,0:T(8,128)(2,1)}, bf16[1216,896]{1,0:T(8,128)(2,1)}) custom-call(bf16[256,896]{1,0:T(8,128)(2,1)} %dynamic-slice_bitcast_fusion.1.refs_0_, f32[256,896]{1,0:T(8,128)} %get-tuple-element.73.mid_ref.refs_1_, f32[8,1152]{1,0:T(8,128)} %get-tuple-element.67.refs_1_.refs_2_, ...), custom_call_target="tpu_custom_call" | custom-call | tf_op jit(solution)/shard_map/pallas_call | solution.py:116
  265.2 28.5 %shard_map.183 = (bf16[256,896]{1,0:T(8,128)(2,1)}, f32[1,896]{1,0:T(1,128)}, f32[1,1152]{1,0:T(1,128)}, bf16[896,2048]{1,0:T(8,128)(2,1)}) custom-call(f32[256,896]{1,0:T(8,128)} %get-tuple-element.78.refs_0_, bf16[256,896]{1,0:T(8,128)(2,1)} %get-tuple-element.71.refs_0_.refs_1_.act_zero_ref, f32[8,1152]{1,0:T(8,128)} %get-tuple-element.67.refs_1_.refs_2_, ...), custom_call_target="tpu_custom_call" | custom-call | tf_op jit(solution)/shard_map/pallas_call | solution.py:116
  293.7 41.2 %shard_map.184 = (f32[256,896]{1,0:T(8,128)}, f32[1,896]{1,0:T(1,128)}, bf16[896,2432]{1,0:T(8,128)(2,1)}, bf16[1216,896]{1,0:T(8,128)(2,1)}, bf16[304,896]{1,0:T(8,128)(2,1)}) custom-call(bf16[256,896]{1,0:T(8,128)(2,1)} %get-tuple-element.84.refs_0_.grad_one_ref, f32[256,896]{1,0:T(8,128)} %get-tuple-element.70.mid_ref.refs_1_, ...), custom_call_target="tpu_custom_call" | custom-call | tf_op jit(solution)/shard_map/pallas_call | solution.py:116
  335.8 45.8 %shard_map.185 = (f32[256,896]{1,0:T(8,128)}, f32[1,896]{1,0:T(1,128)}, f32[1,1152]{1,0:T(1,128)}, bf16[896,2048]{1,0:T(8,128)(2,1)}, bf16[896,256]{1,0:T(8,128)(2,1)}, /*index=5*/bf16[4,2,112,2432]{3,2,1,0:T(8,128)(2,1)}) custom-call(f32[256,896]{1,0:T(8,128)} %get-tuple-element.89.refs_0_, bf16[256,896]{1,0:T(8,128)(2,1)} %dynamic-slice_bitcast_fusion.refs_0_.refs_1_, ...), custom_call_target="tpu_custom_call" | custom-call | tf_op jit(solution)/shard_map/pallas_call | solution.py:116
  382.9 9.0 %reduce-scatter.5.cloned.1.call-done.expand_ref = bf16[112,2432]{1,0:T(8,128)(2,1)} async-done(((bf16[896,2432]{1,0:T(8,128)(2,1)}), bf16[112,2432]{1,0:T(8,128)(2,1)}) %reduce-scatter.5.cloned.1.call-update) | async-done | bytes 544784 | tf_op jit(solution)/shard_map/reduce_scatter | solution.py:1622
  391.9 81.6 %shard_map.186 = (f32[224,1152]{1,0:T(8,128)}, f32[224,896]{1,0:T(8,128)}, f32[8,896]{1,0:T(8,128)}, bf16[4,304,896]{2,1,0:T(8,128)(2,1)}, bf16[2,256,896]{2,1,0...) custom-call(bf16[896,2048]{1,0:T(8,128)(2,1)} %get-tuple-element.99.low_ref, ...), custom_call_target="tpu_custom_call" | custom-call | tf_op jit(solution)/shard_map/pallas_call | solution.py:116
  473.5 0.8 slice_select_fusion
  474.4 8.2 %shard_map.187 = f32[224,9728]{1,0:T(8,128)} custom-call(bf16[4,224,2432]{2,1,0:T(8,128)(2,1)} %bitcast.52), custom_call_target="tpu_custom_call" | custom-call | tf_op jit(solution)/shard_map/pallas_call | solution.py:1489
  482.7 2.3 bitcast_convert_fusion
  487.5 0.9 copy.39
  488.5 1.2 copy.40
  490.3 1.0 copy.41
  491.3 0.9 copy.42
  (100 shorter events, 11.8 us)
Async XLA Ops:
  7.2 21.3 %copy-start = (bf16[2,1,256,896]{3,2,1,0:T(8,128)(2,1)S(1)}, bf16[2,1,256,896]{3,2,1,0:T(8,128)(2,1)}, u32[]{:S(2)}) copy-start(bf16[2,1,256,896]{3,2,1,0:T(8,128)(2,1)} %param.10) | copy-start | bytes 2752516
  7.2 101.3 %all-gather.7.cloned.1.call-start = ((), (), s32[]{:S(2)}) async-start(), calls=%async_computation.3 | async-start | bytes 2451456 | tf_op jit(solution)/shard_map/all_gather | solution.py:1591
  8.4 1.7 collective-permute-start.3
  12.1 96.4 %all-gather.5.cloned.1.call-start = ((), (), s32[]{:S(2)}) async-start(), calls=%async_computation.2 | async-start | bytes 4902912 | tf_op jit(solution)/shard_map/all_gather | solution.py:1591
  21.0 5.1 %copy-start.13 = (bf16[1,288]{1,0:T(2,128)(2,1)S(1)}, bf16[1,288]{1,0:T(2,128)(2,1)}, u32[]{:S(2)}) copy-start(bf16[1,288]{1,0:T(2,128)(2,1)} %param.13) | copy-start | bytes 1732
  21.0 5.1 %copy-start.15 = (bf16[1,224]{1,0:T(2,128)(2,1)S(1)}, bf16[1,224]{1,0:T(2,128)(2,1)}, u32[]{:S(2)}) copy-start(bf16[1,224]{1,0:T(2,128)(2,1)} %param.15) | copy-start | bytes 1348
  21.0 5.1 %copy-start.16 = (bf16[1,224]{1,0:T(2,128)(2,1)S(1)}, bf16[1,224]{1,0:T(2,128)(2,1)}, u32[]{:S(2)}) copy-start(bf16[1,224]{1,0:T(2,128)(2,1)} %param.11) | copy-start | bytes 1348
  21.0 5.5 %copy-start.3 = (bf16[1,224,1152]{2,1,0:T(8,128)(2,1)S(1)}, bf16[1,224,1152]{2,1,0:T(8,128)(2,1)}, u32[]{:S(2)}) copy-start(bf16[1,224,1152]{2,1,0:T(8,128)(2,1)} %param.12) | copy-start | bytes 1548292
  21.0 5.5 %copy-start.5 = (bf16[1,224,896]{2,1,0:T(8,128)(2,1)S(1)}, bf16[1,224,896]{2,1,0:T(8,128)(2,1)}, u32[]{:S(2)}) copy-start(bf16[1,224,896]{2,1,0:T(8,128)(2,1)} %param.14) | copy-start | bytes 1204228
  21.0 2.0 collective-permute-start.2
  24.1 2.7 copy-start.20
  24.2 144.8 %all-gather.11.cloned.1.call-start = ((), (), s32[]{:S(2)}) async-start(), calls=%async_computation.5 | async-start | bytes 2451456 | tf_op jit(solution)/shard_map/all_gather | solution.py:1591
  24.9 162.5 %all-gather.9.cloned.1.call-start = ((), (), s32[]{:S(2)}) async-start(), calls=%async_computation.4 | async-start | bytes 4902912 | tf_op jit(solution)/shard_map/all_gather | solution.py:1591
  25.5 309.5 %reduce-scatter.3.cloned.1.call-start = ((), (), s32[]{:S(2)}) async-start(), calls=%async_computation.6 | async-start | bytes 4902912 | tf_op jit(solution)/shard_map/reduce_scatter | solution.py:1622
  26.1 5.0 %collective-permute-start.1 = (bf16[16,384]{1,0:T(8,128)(2,1)S(1)}, bf16[16,384]{1,0:T(8,128)(2,1)S(1)}, u32[]{:S(2)}, u32[]{:S(2)}) collective-permute-start(bf16[16,384]{1,0:T(8,128)(2,1)S(1)} %fusion.7), channel_id=1, source_target_pairs={{0,16},{16,0},{1,17},{17,1},{2,18},{18,2},{3,19},{19,3},{4,20},{20... | collective-permute-start | bytes 36872 | tf_op jit(solution)/shard_map/ppermute | solution.py:22
  26.6 5.2 %collective-permute-start = (bf16[224,2048]{1,0:T(8,128)(2,1)S(1)}, bf16[224,2048]{1,0:T(8,128)(2,1)}, u32[]{:S(2)}, u32[]{:S(2)}) collective-permute-start(bf16[224,2048]{1,0:T(8,128)(2,1)S(1)} %pad_maximum_fusion), channel_id=1, source_target_pairs={{0,16},{16,0},{1,17},{17,1},{2,18},{18,2},{3,19},{19,3},{4,20},{20... | collective-permute-start | bytes 2752520 | tf_op jit(solution)/shard_map/ppermute | solution.py:22
  26.9 2.5 copy-start.9
  26.9 7.7 %copy-start.11 = (s32[1,1,256]{2,1,0:T(1,128)}, s32[1,1,256]{2,1,0:T(1,128)S(1)}, u32[]{:S(2)}) copy-start(s32[1,1,256]{2,1,0:T(1,128)S(1)} %get-tuple-element.167) | copy-start | bytes 3076
  265.2 126.8 %reduce-scatter.5.cloned.1.call-start = ((), (), s32[]{:S(2)}) async-start(), calls=%async_computation.7 | async-start | bytes 4902912 | tf_op jit(solution)/shard_map/reduce_scatter | solution.py:1622
  335.0 0.7 copy-start.14
  335.0 0.7 copy-start.17
  335.8 45.8 %copy-start.18 = (f32[1,896]{1,0:T(1,128)S(1)}, f32[1,896]{1,0:T(1,128)}, u32[]{:S(2)}) copy-start(f32[1,896]{1,0:T(1,128)} %get-tuple-element.103) | copy-start | bytes 10756
  474.4 8.3 %copy-start.10 = (f32[4,896]{1,0:T(4,128)}, f32[4,896]{1,0:T(4,128)S(1)}, u32[]{:S(2)}) copy-start(f32[4,896]{1,0:T(4,128)S(1)} %slice_select_fusion) | copy-start | bytes 43012
  474.4 8.3 %copy-start.12 = (f32[3584]{0:T(1024)}, f32[3584]{0:T(1024)S(1)}, u32[]{:S(2)}) copy-start(f32[3584]{0:T(1024)S(1)} %reshape.112) | copy-start | bytes 43012
  474.4 8.2 %copy-start.2 = (bf16[4,304,896]{2,1,0:T(8,128)(2,1)S(1)}, bf16[4,304,896]{2,1,0:T(8,128)(2,1)}, u32[]{:S(2)}) copy-start(bf16[4,304,896]{2,1,0:T(8,128)(2,1)} %get-tuple-element.119) | copy-start | bytes 6537220
  482.6 2.4 slice-start.1
  482.7 3.0 slice-start
  482.7 4.9 copy-start.7
  485.0 3.4 copy-start.4
  488.5 1.9 copy-start.6
  488.5 2.8 copy-start.8
  488.5 3.7 copy-start.1
  (1 other events, 0.7 us)
Sparse Core Ops, SparseCore 0:
  12.2 32.3 all-gather.6
  46.9 59.9 all-gather.4
  108.5 28.5 all-gather.10
  139.2 48.1 all-gather.8
  265.3 58.7 reduce-scatter.2
  335.2 56.7 reduce-scatter.4

commit v6 on v5

--- a/solution.py
+++ b/solution.py
@@ -129,11 +129,68 @@
     return pltpu.SemaphoreType.DMA(shape)
 
 
+class Relay:
+    def __init__(self, fsdp_count, source, spot, z_send, z_recv):
+        self.count, self.source, self.spot = fsdp_count, source, spot
+        self.z_send, self.z_recv = z_send, z_recv
+        self.section, self.ctx, self.fsdp = place_of()
+        self.hops = [(side, e) for e in range(1, fsdp_count) for side in (1, 0)]
+
+    def device(self, side):
+        step = 1 if side else self.count - 1
+        return (self.section, self.ctx, lax.rem(self.fsdp + step, self.count))
+
+    def goes_on(self, side):
+        return self.fsdp < self.count - 1 if side else self.fsdp > 0
+
+    def came(self, side, e):
+        return self.fsdp >= e if side else self.fsdp < self.count - e
+
+    def origin(self, side, e):
+        return lax.rem(self.fsdp + (self.count - e if side else e), self.count)
+
+    def copy(self, side, e):
+        spot = self.spot(self.origin(side, e))
+        source = spot if e else self.source
+        return send(source, spot, self.z_send.at[side, e], self.z_recv.at[side, e + 1], self.device(side))
+
+    def begin(self):
+        for side in range(2):
+
+            @pl.when(self.goes_on(side))
+            def _():
+                self.copy(side, 0).start()
+
+    def each(self, step):
+        for side, e in self.hops:
+            pl.when(self.came(side, e))(functools.partial(step, side, e))
+
+    def steps(self):
+        return range(1, self.count)
+
+    def take(self, side, e):
+        spot = self.spot(self.origin(side, e))
+        sems = self.z_send.at[side, e], self.z_recv.at[side, e]
+        send(spot, spot, *sems, self.device(side)).wait_recv()
+        if e < self.count - 1:
+
+            @pl.when(self.goes_on(side))
+            def _():
+                self.copy(side, e).start()
+
+    def sent(self):
+        for side, e in [(0, 0), (1, 0)] + self.hops:
+            if e < self.count - 1:
+
+                @pl.when(jnp.logical_and(self.came(side, e), self.goes_on(side)))
+                def _():
+                    self.copy(side, e).wait_send()
+
+
 class Collect:
     def __init__(self, ctx_count, fsdp_count, shard_ref, w_ref, sems):
         self.shard_ref, self.w_ref = shard_ref, w_ref
-        self.z_send, self.z_recv, self.y_send, self.y_recv, self.v_send, self.v_recv, self.own_sem = sems
-        self.shards = range(1, fsdp_count)
+        z_send, z_recv, self.y_send, self.y_recv, self.v_send, self.v_recv, self.own_sem = sems
         self.places = range(1, ctx_count)
         self.fsdp_count = fsdp_count
         self.section, self.ctx, self.fsdp = place_of()
@@ -141,99 +198,191 @@
         self.rows, width = shard_ref.shape
         self.piece = width // (2 * ctx_count)
         self.mine = pl.ds(pl.multiple_of(self.fsdp * self.rows, self.rows), self.rows)
-        self.friends = (
-            [self.ahead(d) for d in self.shards] + [peer_of(k) for k in self.places] + [self.sister]
+        own = shard_ref.at[:, self.columns(self.ctx, self.section)]
+        self.line = Relay(
+            fsdp_count, own, lambda shard: self.spot(shard, self.ctx, self.section), z_send, z_recv
         )
-
-    def ahead(self, d):
-        return (self.section, self.ctx, lax.rem(self.fsdp + d, self.fsdp_count))
-
-    def behind(self, d):
-        return lax.rem(self.fsdp + self.fsdp_count - d, self.fsdp_count)
+        self.ahead = [
+            (self.section, self.ctx, lax.rem(self.fsdp + d, fsdp_count)) for d in range(1, fsdp_count)
+        ]
+        self.friends = self.ahead + [peer_of(k) for k in self.places] + [self.sister]
 
     def columns(self, where, core):
         return pl.ds(pl.multiple_of((where * 2 + core) * self.piece, self.piece), self.piece)
 
-    def block(self, d, where, core):
-        start = pl.multiple_of(self.behind(d) * self.rows, self.rows)
-        return self.w_ref.at[pl.ds(start, self.rows), self.columns(where, core)]
-
-    def own(self, d):
-        cols = self.columns(self.ctx, self.section)
-        source, target = self.shard_ref.at[:, cols], self.w_ref.at[self.mine, cols]
-        return send(source, target, self.z_send.at[d], self.z_recv.at[d], self.ahead(d))
+    def spot(self, shard, where, core):
+        rows = pl.ds(pl.multiple_of(shard * self.rows, self.rows), self.rows)
+        return self.w_ref.at[rows, self.columns(where, core)]
+
+    def block(self, side, e, where, core):
+        return self.spot(self.line.origin(side, e), where, core)
 
     def kept(self):
         return pltpu.make_async_copy(self.shard_ref, self.w_ref.at[self.mine], self.own_sem.at[0])
 
-    def spread(self, d, k):
-        source = self.block(d, self.ctx, self.section)
+    def spread(self, side, e, k):
+        source = self.block(side, e, self.ctx, self.section)
         device = peer_of(k) if k else self.sister
-        return send(source, source, self.y_send.at[d, k], self.y_recv.at[d, k], device)
-
-    def passed(self, d, k):
-        source = self.block(d, flip(self.ctx, k), self.section)
-        return send(source, source, self.v_send.at[d, k], self.v_recv.at[d, k], self.sister)
+        i = side * self.fsdp_count + e
+        return send(source, source, self.y_send.at[i, k], self.y_recv.at[i, k], device)
+
+    def passed(self, side, e, k):
+        source = self.block(side, e, flip(self.ctx, k), self.section)
+        i = side * self.fsdp_count + e
+        return send(source, source, self.v_send.at[i, k], self.v_recv.at[i, k], self.sister)
 
     def begin(self):
-        for d in self.shards:
-            self.own(d).start()
+        self.line.begin()
         self.kept().start()
 
-    def relay(self):
-        for d in self.shards:
-            came = self.block(d, self.ctx, self.section)
-            send(came, came, self.z_send.at[d], self.z_recv.at[d], self.sister).wait_recv()
-            for k in (*self.places, 0):
-                self.spread(d, k).start()
+    def relay(self, which):
+        def step(side, e):
+            if e == which:
+                self.line.take(side, e)
+                for k in (*self.places, 0):
+                    self.spread(side, e, k).start()
+
+        self.line.each(step)
 
     def hand(self):
-        for d in self.shards:
+        def step(side, e):
+            i = side * self.fsdp_count + e
             for k in self.places:
-                came = self.block(d, flip(self.ctx, k), self.section)
-                send(came, came, self.y_send.at[d, k], self.y_recv.at[d, k], self.sister).wait_recv()
-                self.passed(d, k).start()
+                came = self.block(side, e, flip(self.ctx, k), self.section)
+                send(came, came, self.y_send.at[i, k], self.y_recv.at[i, k], self.sister).wait_recv()
+                self.passed(side, e, k).start()
+
+        self.line.each(step)
 
     def finish(self):
-        for d in self.shards:
+        def arrivals(side, e):
+            i = side * self.fsdp_count + e
             for k in (0, *self.places):
-                came = self.block(d, flip(self.ctx, k), 1 - self.section)
-                recv = (self.v_recv if k else self.y_recv).at[d, k]
-                send(came, came, self.v_send.at[d, k], recv, self.sister).wait_recv()
-        for d in self.shards:
-            self.own(d).wait_send()
-            self.spread(d, 0).wait_send()
+                came = self.block(side, e, flip(self.ctx, k), 1 - self.section)
+                recv = (self.v_recv if k else self.y_recv).at[i, k]
+                send(came, came, self.v_send.at[i, k], recv, self.sister).wait_recv()
+
+        def sent(side, e):
+            self.spread(side, e, 0).wait_send()
             for k in self.places:
-                self.spread(d, k).wait_send()
-                self.passed(d, k).wait_send()
+                self.spread(side, e, k).wait_send()
+                self.passed(side, e, k).wait_send()
+
+        self.line.each(arrivals)
+        self.line.each(sent)
+        self.line.sent()
         self.kept().wait()
 
 
 def collect_sems(ctx_count, fsdp_count):
-    table = dma(fsdp_count, ctx_count)
-    return [dma(fsdp_count), dma(fsdp_count), table, table, table, table, dma(1)]
+    line = dma(2, fsdp_count)
+    table = dma(2 * fsdp_count, ctx_count)
+    return [line, line, table, table, table, table, dma(1)]
+
+
+class Line:
+    def __init__(self, fsdp_count, piece_ref, out_ref, sems):
+        self.piece_ref, self.out_ref = piece_ref, out_ref
+        z_send, z_recv, self.v_send, self.v_recv, self.own_sem = sems
+        self.section, self.ctx, self.fsdp = place_of()
+        self.count = fsdp_count
+        self.rows = piece_ref.shape[0]
+        cut = -(-self.rows // 32) * 16
+        self.parts = ((0, cut), (cut, self.rows - cut))
+        self.sister = (1 - self.section, self.ctx, self.fsdp)
+        self.lines = [
+            Relay(
+                fsdp_count,
+                piece_ref.at[pl.ds(start, size)],
+                functools.partial(self.spot, core),
+                z_send,
+                z_recv,
+            )
+            for core, (start, size) in enumerate(self.parts)
+        ]
+        self.ahead = [
+            (self.section, self.ctx, lax.rem(self.fsdp + d, fsdp_count)) for d in range(1, fsdp_count)
+        ]
+
+    def spot(self, core, shard):
+        start, size = self.parts[core]
+        return self.out_ref.at[pl.ds(pl.multiple_of(shard * self.rows + start, 16), size)]
+
+    def passed(self, core, side, e):
+        spot = self.spot(core, self.lines[core].origin(side, e))
+        i = side * self.count + e
+        return send(spot, spot, self.v_send.at[i], self.v_recv.at[i], self.sister)
+
+    def kept(self):
+        start = pl.multiple_of(self.fsdp * self.rows, 16)
+        return pltpu.make_async_copy(
+            self.piece_ref, self.out_ref.at[pl.ds(start, self.rows)], self.own_sem.at[0]
+        )
+
+    def each_core(self, step):
+        for core in range(2):
+            pl.when(self.section == core)(functools.partial(step, core))
+
+    def begin(self):
+        self.each_core(lambda core: self.lines[core].begin())
+        self.kept().start()
+
+    def relay(self, which):
+        def step(core):
+            def take(side, e):
+                if e == which:
+                    self.lines[core].take(side, e)
+                    self.passed(core, side, e).start()
+
+            self.lines[core].each(take)
+
+        self.each_core(step)
+
+    def end(self):
+        def step(core):
+            line = self.lines[core]
+            line.each(lambda side, e: self.passed(1 - core, side, e).wait_recv())
+            line.each(lambda side, e: self.passed(core, side, e).wait_send())
+            line.sent()
+
+        self.each_core(step)
+        self.kept().wait()
+
+
+def line_sems(fsdp_count):
+    hops = dma(2 * fsdp_count)
+    return [dma(2, fsdp_count), dma(2, fsdp_count), hops, hops, dma(1)]
 
 
 def collect_kernel(
-    ctx_count, fsdp_count, sizes, shard_ref, small_ref, w_ref, vectors_ref, smalls_ref, s_send, s_recv,
-    *sems
+    ctx_count, fsdp_count, sizes, low_ref, high_ref, small_ref, low_w_ref, high_w_ref, vectors_ref,
+    smalls_ref, s_send, s_recv, *sems
 ):
-    steps = Collect(ctx_count, fsdp_count, shard_ref, w_ref, sems)
+    half = len(sems) // 2
+    steps = Collect(ctx_count, fsdp_count, low_ref, low_w_ref, sems[:half])
+    later = Collect(ctx_count, fsdp_count, high_ref, high_w_ref, sems[half:])
+
+    shards = range(1, fsdp_count)
 
     def small(d):
         target = smalls_ref.at[steps.fsdp]
-        return send(small_ref, target, s_send.at[d], s_recv.at[d], steps.ahead(d))
+        return send(small_ref, target, s_send.at[d], s_recv.at[d], steps.ahead[d - 1])
 
     greet_all(steps.friends)
     steps.begin()
-    for d in steps.shards:
+    later.begin()
+    for d in shards:
         small(d).start()
     smalls_ref[steps.fsdp] = small_ref[...]
-    steps.relay()
+    for e in steps.line.steps():
+        steps.relay(e)
+        later.relay(e)
     steps.hand()
+    later.hand()
     steps.finish()
-    for d in steps.shards:
-        came = smalls_ref.at[steps.behind(d)]
+    later.finish()
+    for d in shards:
+        came = smalls_ref.at[lax.rem(steps.fsdp + fsdp_count - d, fsdp_count)]
         send(came, came, s_send.at[d], s_recv.at[d], steps.sister).wait_recv()
     for shard in range(fsdp_count):
         rows = smalls_ref[shard].astype(f32)
@@ -243,20 +392,21 @@
                 vectors_ref[row : row + 1, shard * size : (shard + 1) * size] = rows[
                     16 * layer + i : 16 * layer + i + 1, :size
                 ]
-    for d in steps.shards:
+    for d in shards:
         small(d).wait_send()
 
 
-def collect(shard, small, sizes):
+def collect(low, high, small, sizes):
     ctx_count, fsdp_count = lax.axis_size(CTX), lax.axis_size(FSDP)
-    rows, width = shard.shape
+    rows, width = low.shape
+    whole = ((fsdp_count * rows, width), bf16)
     return call(
         functools.partial(collect_kernel, ctx_count, fsdp_count, sizes),
-        [((fsdp_count * rows, width), bf16), ((8, fsdp_count * max(sizes)), f32)],
+        [whole, whole, ((8, fsdp_count * max(sizes)), f32)],
         [VMEM((fsdp_count,) + small.shape, bf16), dma(fsdp_count), dma(fsdp_count)]
-        + collect_sems(ctx_count, fsdp_count),
+        + collect_sems(ctx_count, fsdp_count) * 2,
         5,
-        shard, small, far_outs=(0,),
+        low, high, small, far_outs=(0, 1),
     )
 
 
@@ -647,23 +797,25 @@
     return jnp.where(lane // HEAD_DIM == group, moved, 0.0).astype(bf16)
 
 
-def attend_kernel(count, fsdp_count, layer, fetch, *refs):
+def attend_kernel(count, fsdp_count, layer, *refs):
     x_ref, vectors_ref, w_ref, cos_ref, sin_ref, kpos_ref, qpos_ref = refs[:7]
     refs = refs[7:]
-    shard_ref, refs = (refs[0], refs[1:]) if fetch else (None, refs)
+    if layer:
+        shard_ref, *refs = refs
     normed_ref, q_ref, kv_ref, lse_ref, ctx_ref, mid_ref, low2_ref = refs[:7]
     refs = refs[7:]
-    next_ref, refs = (refs[0], refs[1:]) if fetch else (None, refs)
+    if layer:
+        next_ref, *refs = refs
     mask_ref, s_ref, p_ref, vt_ref, ctxf_ref, send_sem, recv_sem, *sems = refs
     rows, width = x_ref.shape
     pair = kv_ref.shape[2] // 2
     wide = width + 2 * pair
     heads = width // HEAD_DIM
     group_size = heads // (pair // HEAD_DIM)
-    if fetch:
-        steps = Collect(count, fsdp_count, shard_ref, next_ref, sems)
-        greet_all(steps.friends)
-        steps.begin()
+    if layer:
+        line = Line(fsdp_count, shard_ref, next_ref, sems)
+        greet_all([peer_of(k) for k in range(1, count)] + [line.sister] + line.ahead)
+        line.begin()
     else:
         greet(count)
     x = x_ref[...].astype(f32)
@@ -685,8 +837,6 @@
     for k in range(count):
         allowed = kpos_ref[k * rows : (k + 1) * rows, :] <= qpos_ref[...]
         mask_ref[k] = jnp.where(allowed, 0.0, masked_value)
-    if fetch:
-        steps.relay()
     for k in range(count):
         if k:
             remote(kv_ref.at[0], kv_ref.at[k], send_sem, recv_sem, k).wait_recv()
@@ -712,8 +862,9 @@
         context = matmul(value_rows, p_ref[...]) * (1.0 / total)
         ctxf_ref[head * HEAD_DIM : (head + 1) * HEAD_DIM, :] = context
         lse_ref[head : head + 1, :] = top + jnp.log(total)
-        if fetch and head == heads // 2:
-            steps.hand()
+        for e in range(1, fsdp_count - 1) if layer else ():
+            if head == e * heads // fsdp_count + 1:
+                line.relay(e)
     context = ctxf_ref[...]
     ctx_ref[...] = context.astype(bf16)
     middle = x + matmul(context.T.astype(bf16), w_ref[:, wide:])
@@ -721,11 +872,12 @@
     low2_ref[...] = (middle * row_scale(middle) * gain2[:, :width]).astype(bf16)
     for k in range(1, count):
         remote(kv_ref.at[0], kv_ref.at[k], send_sem, recv_sem, k).wait_send()
-    if fetch:
-        steps.finish()
-
-
-def attend(layer, hidden, place, shard=None):
+    if layer:
+        line.relay(fsdp_count - 1)
+        line.end()
+
+
+def attend(layer, hidden, place, piece=()):
     index, vectors, weights = layer[:3]
     cosine, sine, key_positions, query_positions = place
     rows, width = hidden.shape
@@ -734,11 +886,10 @@
     pair = (wide - width) // 2
     keys = count * rows
     heads = width // HEAD_DIM
-    fetch = shard is not None
     fsdp_count = lax.axis_size(FSDP)
     args = (hidden, vectors, weights, cosine, sine, key_positions, query_positions)
     return call(
-        functools.partial(attend_kernel, count, fsdp_count, index, fetch),
+        functools.partial(attend_kernel, count, fsdp_count, index),
         [
             ((rows, width), bf16),
             ((rows, width), bf16),
@@ -748,7 +899,7 @@
             ((rows, width), f32),
             ((rows, width), bf16),
         ]
-        + [(weights.shape, bf16)] * fetch,
+        + [((fsdp_count * array.shape[0], width), bf16) for array in piece],
         [
             VMEM((count, rows, rows), f32),
             VMEM((count, rows, rows), f32),
@@ -758,10 +909,10 @@
             dma(count),
             dma(count),
         ]
-        + (collect_sems(count, fsdp_count) if fetch else []),
-        10 if fetch else 1,
-        *args, *([shard] if fetch else []),
-        far_outs=(7,) if fetch else (),
+        + line_sems(fsdp_count) * len(piece),
+        1 if index else 10,
+        *args, *piece,
+        far_outs=(7,) * len(piece),
     )
 
 
@@ -1583,38 +1734,38 @@
         return jnp.where(is_first, own, other), jnp.where(is_first, other, own)
 
     expand_pair = halves(expand_shard)
-    down_pair = halves(down_shard)
+    down_first, down_next = in_order(down_shard)
+    half_units = down_shard.shape[0] // 2
+    down_halves = jnp.where(is_first, down_first[:half_units], down_first[half_units:])
     first_shard, second_shard = in_order(attn_shard)
     small_pair = jnp.concatenate(in_order(small_shard))
 
     def gather(piece):
         return lax.all_gather(piece, both, axis=0, tiled=True)
 
-    expands, downs = [None, None], [None, None]
-    expands[0], downs[0] = gather(expand_pair[0]), gather(down_pair[0])
-    first_shard, small_pair = lax.optimization_barrier(
-        (first_shard, small_pair, expand_pair[0], down_pair[0])
-    )[:2]
-    weights, vectors = collect(first_shard, small_pair, (shard_rows, bias_part, shard_rows))
-    weights = [weights, None]
-    expands[1], downs[1] = gather(expand_pair[1]), gather(down_pair[1])
-
-    def layer_of(layer):
-        return (layer, vectors, weights[layer], expands[layer], downs[layer])
+    down_w = gather(down_halves)
+    expands = [gather(piece) for piece in expand_pair]
+    first_shard, second_shard, small_pair = lax.optimization_barrier(
+        (first_shard, second_shard, small_pair, expand_pair[0], down_halves)
+    )[:3]
+    sizes = (shard_rows, bias_part, shard_rows)
+    *weights, vectors = collect(first_shard, second_shard, small_pair, sizes)
 
     layers = []
     hidden = source
     stored = []
     sent = []
     for layer in range(2):
-        layers.append(layer_of(layer))
+        now = (layer, vectors, weights[layer])
         normed, queries, every_kv, lse, context, middle, second_normed, *fetched = attend(
-            layers[layer], hidden, place, None if layer else second_shard
+            now, hidden, place, (down_next,) if layer else ()
         )
-        if fetched:
-            weights[1] = fetched[0]
+        if layer:
+            (down_w,) = fetched
+        now = now + (expands[layer], down_w)
+        layers.append(now)
         kept = (hidden, normed, queries, every_kv, lse, context)
-        hidden, blocks, kept_gate, kept_up = feed(layers[layer], second_normed, middle)
+        hidden, blocks, kept_gate, kept_up = feed(now, second_normed, middle)
         sent.append(hidden)
         stored.append((middle, kept, blocks, kept_gate, kept_up))
 

time: 505 us -> 494 us (0.978)
  waiting for transfers between devices: 31.6 us -> 13 us
  Pallas kernels: 417 us -> 425 us
    all_gather x4 -> x3, waiting for transfers between devices: 18.6 us -> 0.06 us  [gather(): return lax.all_gather(piece, both, axis=0, tiled=True)]
    pallas_call x10, Pallas kernels: 409 us -> 417 us  [call(): pl.pallas_call(kernel, out_shape=[jax.ShapeDtypeStruct(shape, kind) for s...]
  transfers between devices with their start and end apart: 10 -> 9, of which waited for: 4 -> 3; matrix products, arithmetic and copies ran while one was open for 4% -> 4% of each run, Pallas kernels for 50% -> 53%
where the time goes in v6:
time: 494 us; the launch traced here: 488 us
  Pallas kernels  425 us (86%)
  other arithmetic  18.9 us (4%)
  local copies, waits for them, and re-layouts  14.7 us (3%)
  between operations  14.4 us (3%)
  waiting for transfers between devices  13 us (3%)
    pallas_call x10, Pallas kernels, call(): pl.pallas_call(kernel, out_shape=[jax.ShapeDtypeStruct(shape, kind) for s...  417 us
  transfers between devices with their start and end apart: 9, of which 3 were waited for; matrix products, arithmetic and copies ran while one was open for 4% of the time, Pallas kernels for 53%

profile of v6, /device:TPU:0, one launch (start us, length us, event | category | flops | bytes accessed | tf_op | source)
XLA Modules:
  0.0 488.1 jit_solution(16893797632272096879)
XLA Ops:
  7.2 1.1 dynamic-slice_bitcast_fusion
  8.8 1.6 collective-permute-done.3
  10.4 2.0 broadcast_select_fusion.2
  12.4 0.7 slice_select_fusion
  13.3 3.2 select_bitcast_fusion.1
  16.5 3.1 select_bitcast_fusion
  20.9 1.1 concatenate.41
  22.6 1.6 collective-permute-done.2
  24.1 1.1 broadcast_select_fusion.4
  27.6 1.0 pad_maximum_fusion.1
  28.6 2.2 dynamic-slice_bitcast_fusion.1
  30.8 1.0 copy.29.refs_5_.refs_6_
  32.5 1.6 broadcast_select_fusion
  34.1 50.1 %shard_map.177 = (bf16[896,2048]{1,0:T(8,128)(2,1)}, bf16[896,2048]{1,0:T(8,128)(2,1)}, f32[8,1152]{1,0:T(8,128)}) custom-call(bf16[224,2048]{1,0:T(8,128)(2,1)} %get-tuple-element.67.low_ref, bf16[224,2048]{1,0:T(8,128)(2,1)} %get-tuple-element.68.high_ref, bf16[32,384]{1,0:T(8,128)(2,1)} %pad_maximum_fusion.4.small_ref), custom_call_target="tpu_custom_call" | custom-call | tf_op jit(solution)/shard_map/pallas_call | solution.py:116
  84.2 22.7 %shard_map.178 = (bf16[256,896]{1,0:T(8,128)(2,1)}, bf16[256,896]{1,0:T(8,128)(2,1)}, bf16[4,256,256]{2,1,0:T(8,128)(2,1)}, f32[16,256]{1,0:T(8,128)}, bf16[896,...) custom-call(bf16[256,896]{1,0:T(8,128)(2,1)} %get-tuple-element.177.refs_0_.refs_1_, ...), custom_call_target="tpu_custom_call" | custom-call | tf_op jit(solution)/shard_map/pallas_call | solution.py:116
  107.0 37.8 %shard_map.179 = (bf16[256,896]{1,0:T(8,128)(2,1)}, bf16[4,256,896]{2,1,0:T(8,128)(2,1)}, bf16[4,256,1216]{2,1,0:T(8,128)(2,1)}, bf16[4,256,1216]{2,1,0:T(8,128)(2,1)}) custom-call(bf16[256,896]{1,0:T(8,128)(2,1)} %get-tuple-element.72.low_ref, f32[256,896]{1,0:T(8,128)} %get-tuple-element.73.mid_ref.refs_1_, ...), custom_call_target="tpu_custom_call" | custom-call | tf_op jit(solution)/shard_map/pallas_call | solution.py:116
  144.8 30.4 %shard_map.180 = (bf16[256,896]{1,0:T(8,128)(2,1)}, bf16[256,896]{1,0:T(8,128)(2,1)}, bf16[4,256,256]{2,1,0:T(8,128)(2,1)}, f32[16,256]{1,0:T(8,128)}, bf16[896,...) custom-call(bf16[256,896]{1,0:T(8,128)(2,1)} %get-tuple-element.74.refs_0_.refs_1_.a, ...), custom_call_target="tpu_custom_call" | custom-call | tf_op jit(solution)/shard_map/pallas_call | solution.py:116
  175.2 40.4 %shard_map.181 = (bf16[256,896]{1,0:T(8,128)(2,1)}, bf16[4,256,896]{2,1,0:T(8,128)(2,1)}, bf16[4,256,1216]{2,1,0:T(8,128)(2,1)}, bf16[4,256,1216]{2,1,0:T(8,128)(2,1)}) custom-call(bf16[256,896]{1,0:T(8,128)(2,1)} %get-tuple-element.77.low_ref, f32[256,896]{1,0:T(8,128)} %get-tuple-element.76.mid_ref.refs_1_, ...), custom_call_target="tpu_custom_call" | custom-call | tf_op jit(solution)/shard_map/pallas_call | solution.py:116
  215.6 38.1 %shard_map.182 = (f32[256,896]{1,0:T(8,128)}, f32[1,896]{1,0:T(1,128)}, bf16[896,2432]{1,0:T(8,128)(2,1)}, bf16[1216,896]{1,0:T(8,128)(2,1)}) custom-call(bf16[256,896]{1,0:T(8,128)(2,1)} %get-tuple-element.178.refs_0_, f32[256,896]{1,0:T(8,128)} %get-tuple-element.76.mid_ref.refs_1_, f32[8,1152]{1,0:T(8,128)} %get-tuple-element.70.refs_1_.refs_2_, ...), custom_call_target="tpu_custom_call" | custom-call | tf_op jit(solution)/shard_map/pallas_call | solution.py:116
  253.8 28.5 %shard_map.183 = (bf16[256,896]{1,0:T(8,128)(2,1)}, f32[1,896]{1,0:T(1,128)}, f32[1,1152]{1,0:T(1,128)}, bf16[896,2048]{1,0:T(8,128)(2,1)}) custom-call(f32[256,896]{1,0:T(8,128)} %get-tuple-element.82.refs_0_, bf16[256,896]{1,0:T(8,128)(2,1)} %get-tuple-element.74.refs_0_.refs_1_.act_zero_ref, f32[8,1152]{1,0:T(8,128)} %get-tuple-element.70.refs_1_.refs_2_, ...), custom_call_target="tpu_custom_call" | custom-call | tf_op jit(solution)/shard_map/pallas_call | solution.py:116
  282.3 41.7 %shard_map.184 = (f32[256,896]{1,0:T(8,128)}, f32[1,896]{1,0:T(1,128)}, bf16[896,2432]{1,0:T(8,128)(2,1)}, bf16[1216,896]{1,0:T(8,128)(2,1)}, bf16[304,896]{1,0:T(8,128)(2,1)}) custom-call(bf16[256,896]{1,0:T(8,128)(2,1)} %get-tuple-element.88.refs_0_.grad_one_ref, f32[256,896]{1,0:T(8,128)} %get-tuple-element.73.mid_ref.refs_1_, ...), custom_call_target="tpu_custom_call" | custom-call | tf_op jit(solution)/shard_map/pallas_call | solution.py:116
  324.8 45.7 %shard_map.185 = (f32[256,896]{1,0:T(8,128)}, f32[1,896]{1,0:T(1,128)}, f32[1,1152]{1,0:T(1,128)}, bf16[896,2048]{1,0:T(8,128)(2,1)}, bf16[896,256]{1,0:T(8,128)(2,1)}, /*index=5*/bf16[4,2,112,2432]{3,2,1,0:T(8,128)(2,1)}) custom-call(f32[256,896]{1,0:T(8,128)} %get-tuple-element.93.refs_0_, bf16[256,896]{1,0:T(8,128)(2,1)} %get-tuple-element.177.refs_0_.refs_1_, ...), custom_call_target="tpu_custom_call" | custom-call | tf_op jit(solution)/shard_map/pallas_call | solution.py:116
  370.6 0.7 maximum_reduce_fusion
  372.0 9.0 %reduce-scatter.5.cloned.1.call-done.expand_ref = bf16[112,2432]{1,0:T(8,128)(2,1)} async-done(((bf16[896,2432]{1,0:T(8,128)(2,1)}), bf16[112,2432]{1,0:T(8,128)(2,1)}) %reduce-scatter.5.cloned.1.call-update) | async-done | bytes 544784 | tf_op jit(solution)/shard_map/reduce_scatter | solution.py:1773
  381.0 81.7 %shard_map.186 = (f32[224,1152]{1,0:T(8,128)}, f32[224,896]{1,0:T(8,128)}, f32[8,896]{1,0:T(8,128)}, bf16[4,304,896]{2,1,0:T(8,128)(2,1)}, bf16[2,256,896]{2,1,0...) custom-call(bf16[896,2048]{1,0:T(8,128)(2,1)} %get-tuple-element.103.low_ref, ...), custom_call_target="tpu_custom_call" | custom-call | tf_op jit(solution)/shard_map/pallas_call | solution.py:116
  462.7 0.8 slice_select_fusion.1
  463.6 8.2 %shard_map.187 = f32[224,9728]{1,0:T(8,128)} custom-call(bf16[4,224,2432]{2,1,0:T(8,128)(2,1)} %bitcast.51), custom_call_target="tpu_custom_call" | custom-call | tf_op jit(solution)/shard_map/pallas_call | solution.py:1640
  471.9 2.3 bitcast_convert_fusion
  476.7 0.9 copy.39
  477.6 1.2 copy.40
  479.5 1.0 copy.41
  480.5 0.9 copy.42
  (91 shorter events, 10.0 us)
Async XLA Ops:
  7.2 99.8 %all-gather.6.cloned.1.call-start = ((), (), s32[]{:S(2)}) async-start(), calls=%async_computation.3 | async-start | bytes 2451456 | tf_op jit(solution)/shard_map/all_gather | solution.py:1744
  8.3 2.1 collective-permute-start.3
  13.2 93.8 %all-gather.4.cloned.1.call-start = ((), (), s32[]{:S(2)}) async-start(), calls=%async_computation.2 | async-start | bytes 4902912 | tf_op jit(solution)/shard_map/all_gather | solution.py:1744
  22.1 4.1 copy-start.10
  22.1 4.1 copy-start.12
  22.1 4.1 copy-start.13
  22.1 4.5 copy-start.1
  22.1 4.5 copy-start.3
  22.1 2.0 collective-permute-start.2
  25.3 1.7 copy-start.17
  25.3 149.9 %all-gather.8.cloned.1.call-start = ((), (), s32[]{:S(2)}) async-start(), calls=%async_computation.4 | async-start | bytes 4902912 | tf_op jit(solution)/shard_map/all_gather | solution.py:1744
  26.0 298.0 %reduce-scatter.3.cloned.1.call-start = ((), (), s32[]{:S(2)}) async-start(), calls=%async_computation.5 | async-start | bytes 4902912 | tf_op jit(solution)/shard_map/reduce_scatter | solution.py:1773
  26.2 5.6 %collective-permute-start.1 = (bf16[16,384]{1,0:T(8,128)(2,1)S(1)}, bf16[16,384]{1,0:T(8,128)(2,1)S(1)}, u32[]{:S(2)}, u32[]{:S(2)}) collective-permute-start(bf16[16,384]{1,0:T(8,128)(2,1)S(1)} %fusion.7), channel_id=1, source_target_pairs={{0,16},{16,0},{1,17},{17,1},{2,18},{18,2},{3,19},{19,3},{4,20},{20... | collective-permute-start | bytes 36872 | tf_op jit(solution)/shard_map/ppermute | solution.py:22
  26.7 5.7 %collective-permute-start = (bf16[224,2048]{1,0:T(8,128)(2,1)S(1)}, bf16[224,2048]{1,0:T(8,128)(2,1)S(1)}, u32[]{:S(2)}, u32[]{:S(2)}) collective-permute-start(bf16[224,2048]{1,0:T(8,128)(2,1)S(1)} %pad_maximum_fusion), channel_id=1, source_target_pairs={{0,16},{16,0},{1,17},{17,1},{2,18},{18,2},{3,19},{19,3},{4,20},{20... | collective-permute-start | bytes 2752520 | tf_op jit(solution)/shard_map/ppermute | solution.py:22
  27.0 7.1 %copy-start.8 = (s32[1,1,256]{2,1,0:T(1,128)}, s32[1,1,256]{2,1,0:T(1,128)S(1)}, u32[]{:S(2)}) copy-start(s32[1,1,256]{2,1,0:T(1,128)S(1)} %get-tuple-element.171) | copy-start | bytes 3076
  253.8 127.2 %reduce-scatter.5.cloned.1.call-start = ((), (), s32[]{:S(2)}) async-start(), calls=%async_computation.6 | async-start | bytes 4902912 | tf_op jit(solution)/shard_map/reduce_scatter | solution.py:1773
  324.1 0.7 copy-start.11
  324.1 0.7 copy-start.14
  324.1 0.7 copy-start.16
  324.8 45.8 %copy-start.15 = (f32[1,896]{1,0:T(1,128)S(1)}, f32[1,896]{1,0:T(1,128)}, u32[]{:S(2)}) copy-start(f32[1,896]{1,0:T(1,128)} %get-tuple-element.107) | copy-start | bytes 10756
  463.5 8.3 %copy-start.7 = (f32[4,896]{1,0:T(4,128)}, f32[4,896]{1,0:T(4,128)S(1)}, u32[]{:S(2)}) copy-start(f32[4,896]{1,0:T(4,128)S(1)} %slice_select_fusion.1) | copy-start | bytes 43012
  463.6 8.3 %copy-start.9 = (f32[3584]{0:T(1024)}, f32[3584]{0:T(1024)S(1)}, u32[]{:S(2)}) copy-start(f32[3584]{0:T(1024)S(1)} %reshape.106) | copy-start | bytes 43012
  463.6 8.2 %copy-start = (bf16[4,304,896]{2,1,0:T(8,128)(2,1)S(1)}, bf16[4,304,896]{2,1,0:T(8,128)(2,1)}, u32[]{:S(2)}) copy-start(bf16[4,304,896]{2,1,0:T(8,128)(2,1)} %get-tuple-element.123) | copy-start | bytes 6537220
  471.8 2.4 slice-start.1
  471.8 3.0 slice-start
  471.8 4.9 copy-start.5
  474.2 3.4 copy-start.2
  477.6 1.9 copy-start.4
  477.6 2.8 copy-start.6
Sparse Core Ops, SparseCore 0:
  13.3 33.6 all-gather.5
  49.3 50.4 all-gather.3
  101.9 47.5 all-gather.7
  253.9 59.5 reduce-scatter.2
  324.2 56.7 reduce-scatter.4

commit v7 on v6

--- a/solution.py
+++ b/solution.py
@@ -192,6 +192,8 @@
         self.shard_ref, self.w_ref = shard_ref, w_ref
         z_send, z_recv, self.y_send, self.y_recv, self.v_send, self.v_recv, self.own_sem = sems
         self.places = range(1, ctx_count)
+        self.square = ctx_count == 4
+        self.early = ((1, 1), (2, 0)) if self.square else ()
         self.fsdp_count = fsdp_count
         self.section, self.ctx, self.fsdp = place_of()
         self.sister = (1 - self.section, self.ctx, self.fsdp)
@@ -220,11 +222,27 @@
     def kept(self):
         return pltpu.make_async_copy(self.shard_ref, self.w_ref.at[self.mine], self.own_sem.at[0])
 
-    def spread(self, side, e, k):
-        source = self.block(side, e, self.ctx, self.section)
+    def half(self, side, e, where, core, h):
+        size = self.rows // 2
+        start = self.line.origin(side, e) * self.rows + h * size
+        rows = pl.ds(pl.multiple_of(start, size), size)
+        return self.w_ref.at[rows, self.columns(where, core)]
+
+    def spread(self, side, e, k, h, came=0):
+        source = self.half(side, e, flip(self.ctx, came), self.section, h)
         device = peer_of(k) if k else self.sister
-        i = side * self.fsdp_count + e
-        return send(source, source, self.y_send.at[i, k], self.y_recv.at[i, k], device)
+        i, j = side * self.fsdp_count + e, 2 * (k ^ came) + h
+        return send(source, source, self.y_send.at[i, j], self.y_recv.at[i, j], device)
+
+    def arrival(self, side, e, k, h, core):
+        came = self.half(side, e, flip(self.ctx, k), core, h)
+        i, j = side * self.fsdp_count + e, 2 * k + h
+        return send(came, came, self.y_send.at[i, j], self.y_recv.at[i, j], self.sister)
+
+    def outgoing(self):
+        if self.square:
+            return [(1, 1), (2, 0), (0, 0), (0, 1), (1, 0), (2, 1)]
+        return [(k, h) for k in (*self.places, 0) for h in range(2)]
 
     def passed(self, side, e, k):
         source = self.block(side, e, flip(self.ctx, k), self.section)
@@ -239,17 +257,26 @@
         def step(side, e):
             if e == which:
                 self.line.take(side, e)
-                for k in (*self.places, 0):
-                    self.spread(side, e, k).start()
+                for k, h in self.outgoing():
+                    self.spread(side, e, k, h).start()
 
         self.line.each(step)
+
+    def corner(self):
+        def step(side, e):
+            for k, h in self.early:
+                self.arrival(side, e, k, h, self.section).wait_recv()
+                self.spread(side, e, 3 - k, h, k).start()
+
+        if self.square:
+            self.line.each(step)
 
     def hand(self):
         def step(side, e):
-            i = side * self.fsdp_count + e
             for k in self.places:
-                came = self.block(side, e, flip(self.ctx, k), self.section)
-                send(came, came, self.y_send.at[i, k], self.y_recv.at[i, k], self.sister).wait_recv()
+                for h in range(2):
+                    if (k, h) not in self.early:
+                        self.arrival(side, e, k, h, self.section).wait_recv()
                 self.passed(side, e, k).start()
 
         self.line.each(step)
@@ -257,15 +284,18 @@
     def finish(self):
         def arrivals(side, e):
             i = side * self.fsdp_count + e
-            for k in (0, *self.places):
+            for h in range(2):
+                self.arrival(side, e, 0, h, 1 - self.section).wait_recv()
+            for k in self.places:
                 came = self.block(side, e, flip(self.ctx, k), 1 - self.section)
-                recv = (self.v_recv if k else self.y_recv).at[i, k]
-                send(came, came, self.v_send.at[i, k], recv, self.sister).wait_recv()
+                send(came, came, self.v_send.at[i, k], self.v_recv.at[i, k], self.sister).wait_recv()
 
         def sent(side, e):
-            self.spread(side, e, 0).wait_send()
+            for k, h in self.outgoing():
+                self.spread(side, e, k, h).wait_send()
+            for k, h in self.early:
+                self.spread(side, e, 3 - k, h, k).wait_send()
             for k in self.places:
-                self.spread(side, e, k).wait_send()
                 self.passed(side, e, k).wait_send()
 
         self.line.each(arrivals)
@@ -277,7 +307,8 @@
 def collect_sems(ctx_count, fsdp_count):
     line = dma(2, fsdp_count)
     table = dma(2 * fsdp_count, ctx_count)
-    return [line, line, table, table, table, table, dma(1)]
+    halves = dma(2 * fsdp_count, 2 * ctx_count)
+    return [line, line, halves, halves, table, table, dma(1)]
 
 
 class Line:
@@ -377,6 +408,8 @@
     for e in steps.line.steps():
         steps.relay(e)
         later.relay(e)
+    steps.corner()
+    later.corner()
     steps.hand()
     later.hand()
     steps.finish()

time: 494 us -> 489 us (0.990)
  Pallas kernels: 425 us -> 420 us
    pallas_call x10, Pallas kernels: 417 us -> 412 us  [call(): pl.pallas_call(kernel, out_shape=[jax.ShapeDtypeStruct(shape, kind) for s...]
  transfers between devices with their start and end apart: 9 -> 9, of which waited for: 3 -> 3; matrix products, arithmetic and copies ran while one was open for 4% -> 4% of each run, Pallas kernels for 53% -> 52%
where the time goes in v7:
time: 489 us; the launch traced here: 483 us
  Pallas kernels  420 us (86%)
  other arithmetic  18.9 us (4%)
  local copies, waits for them, and re-layouts  14.7 us (3%)
  between operations  14.6 us (3%)
  waiting for transfers between devices  13 us (3%)
    pallas_call x10, Pallas kernels, call(): pl.pallas_call(kernel, out_shape=[jax.ShapeDtypeStruct(shape, kind) for s...  412 us
  transfers between devices with their start and end apart: 9, of which 3 were waited for; matrix products, arithmetic and copies ran while one was open for 4% of the time, Pallas kernels for 52%

profile of v7, /device:TPU:0, one launch (start us, length us, event | category | flops | bytes accessed | tf_op | source)
XLA Modules:
  0.0 482.8 jit_solution(6708348449829081910)
XLA Ops:
  7.2 1.1 dynamic-slice_bitcast_fusion
  8.8 1.6 collective-permute-done.3
  10.4 2.0 broadcast_select_fusion.2
  12.4 0.7 slice_select_fusion
  13.3 3.2 select_bitcast_fusion.1
  16.5 3.1 select_bitcast_fusion
  20.9 1.1 concatenate.41
  22.6 1.6 collective-permute-done.2
  24.1 1.1 broadcast_select_fusion.4
  27.6 1.0 pad_maximum_fusion.1
  28.6 2.2 dynamic-slice_bitcast_fusion.1
  30.8 1.0 copy.29.refs_5_.refs_6_
  32.5 1.6 broadcast_select_fusion
  34.1 44.6 %shard_map.177 = (bf16[896,2048]{1,0:T(8,128)(2,1)}, bf16[896,2048]{1,0:T(8,128)(2,1)}, f32[8,1152]{1,0:T(8,128)}) custom-call(bf16[224,2048]{1,0:T(8,128)(2,1)} %get-tuple-element.67.low_ref, bf16[224,2048]{1,0:T(8,128)(2,1)} %get-tuple-element.68.high_ref, bf16[32,384]{1,0:T(8,128)(2,1)} %pad_maximum_fusion.4.small_ref), custom_call_target="tpu_custom_call" | custom-call | tf_op jit(solution)/shard_map/pallas_call | solution.py:116
  78.7 22.7 %shard_map.178 = (bf16[256,896]{1,0:T(8,128)(2,1)}, bf16[256,896]{1,0:T(8,128)(2,1)}, bf16[4,256,256]{2,1,0:T(8,128)(2,1)}, f32[16,256]{1,0:T(8,128)}, bf16[896,...) custom-call(bf16[256,896]{1,0:T(8,128)(2,1)} %get-tuple-element.177.refs_0_.refs_1_, ...), custom_call_target="tpu_custom_call" | custom-call | tf_op jit(solution)/shard_map/pallas_call | solution.py:116
  101.5 38.3 %shard_map.179 = (bf16[256,896]{1,0:T(8,128)(2,1)}, bf16[4,256,896]{2,1,0:T(8,128)(2,1)}, bf16[4,256,1216]{2,1,0:T(8,128)(2,1)}, bf16[4,256,1216]{2,1,0:T(8,128)(2,1)}) custom-call(bf16[256,896]{1,0:T(8,128)(2,1)} %get-tuple-element.72.low_ref, f32[256,896]{1,0:T(8,128)} %get-tuple-element.73.mid_ref.refs_1_, ...), custom_call_target="tpu_custom_call" | custom-call | tf_op jit(solution)/shard_map/pallas_call | solution.py:116
  139.8 30.7 %shard_map.180 = (bf16[256,896]{1,0:T(8,128)(2,1)}, bf16[256,896]{1,0:T(8,128)(2,1)}, bf16[4,256,256]{2,1,0:T(8,128)(2,1)}, f32[16,256]{1,0:T(8,128)}, bf16[896,...) custom-call(bf16[256,896]{1,0:T(8,128)(2,1)} %get-tuple-element.74.refs_0_.refs_1_.a, ...), custom_call_target="tpu_custom_call" | custom-call | tf_op jit(solution)/shard_map/pallas_call | solution.py:116
  170.6 40.5 %shard_map.181 = (bf16[256,896]{1,0:T(8,128)(2,1)}, bf16[4,256,896]{2,1,0:T(8,128)(2,1)}, bf16[4,256,1216]{2,1,0:T(8,128)(2,1)}, bf16[4,256,1216]{2,1,0:T(8,128)(2,1)}) custom-call(bf16[256,896]{1,0:T(8,128)(2,1)} %get-tuple-element.77.low_ref, f32[256,896]{1,0:T(8,128)} %get-tuple-element.76.mid_ref.refs_1_, ...), custom_call_target="tpu_custom_call" | custom-call | tf_op jit(solution)/shard_map/pallas_call | solution.py:116
  211.1 38.0 %shard_map.182 = (f32[256,896]{1,0:T(8,128)}, f32[1,896]{1,0:T(1,128)}, bf16[896,2432]{1,0:T(8,128)(2,1)}, bf16[1216,896]{1,0:T(8,128)(2,1)}) custom-call(bf16[256,896]{1,0:T(8,128)(2,1)} %get-tuple-element.178.refs_0_, f32[256,896]{1,0:T(8,128)} %get-tuple-element.76.mid_ref.refs_1_, f32[8,1152]{1,0:T(8,128)} %get-tuple-element.70.refs_1_.refs_2_, ...), custom_call_target="tpu_custom_call" | custom-call | tf_op jit(solution)/shard_map/pallas_call | solution.py:116
  249.2 28.5 %shard_map.183 = (bf16[256,896]{1,0:T(8,128)(2,1)}, f32[1,896]{1,0:T(1,128)}, f32[1,1152]{1,0:T(1,128)}, bf16[896,2048]{1,0:T(8,128)(2,1)}) custom-call(f32[256,896]{1,0:T(8,128)} %get-tuple-element.82.refs_0_, bf16[256,896]{1,0:T(8,128)(2,1)} %get-tuple-element.74.refs_0_.refs_1_.act_zero_ref, f32[8,1152]{1,0:T(8,128)} %get-tuple-element.70.refs_1_.refs_2_, ...), custom_call_target="tpu_custom_call" | custom-call | tf_op jit(solution)/shard_map/pallas_call | solution.py:116
  277.7 40.8 %shard_map.184 = (f32[256,896]{1,0:T(8,128)}, f32[1,896]{1,0:T(1,128)}, bf16[896,2432]{1,0:T(8,128)(2,1)}, bf16[1216,896]{1,0:T(8,128)(2,1)}, bf16[304,896]{1,0:T(8,128)(2,1)}) custom-call(bf16[256,896]{1,0:T(8,128)(2,1)} %get-tuple-element.88.refs_0_.grad_one_ref, f32[256,896]{1,0:T(8,128)} %get-tuple-element.73.mid_ref.refs_1_, ...), custom_call_target="tpu_custom_call" | custom-call | tf_op jit(solution)/shard_map/pallas_call | solution.py:116
  319.3 45.7 %shard_map.185 = (f32[256,896]{1,0:T(8,128)}, f32[1,896]{1,0:T(1,128)}, f32[1,1152]{1,0:T(1,128)}, bf16[896,2048]{1,0:T(8,128)(2,1)}, bf16[896,256]{1,0:T(8,128)(2,1)}, /*index=5*/bf16[4,2,112,2432]{3,2,1,0:T(8,128)(2,1)}) custom-call(f32[256,896]{1,0:T(8,128)} %get-tuple-element.93.refs_0_, bf16[256,896]{1,0:T(8,128)(2,1)} %get-tuple-element.177.refs_0_.refs_1_, ...), custom_call_target="tpu_custom_call" | custom-call | tf_op jit(solution)/shard_map/pallas_call | solution.py:116
  365.1 0.7 maximum_reduce_fusion
  366.5 9.0 %reduce-scatter.5.cloned.1.call-done.expand_ref = bf16[112,2432]{1,0:T(8,128)(2,1)} async-done(((bf16[896,2432]{1,0:T(8,128)(2,1)}), bf16[112,2432]{1,0:T(8,128)(2,1)}) %reduce-scatter.5.cloned.1.call-update) | async-done | bytes 544784 | tf_op jit(solution)/shard_map/reduce_scatter | solution.py:1806
  375.5 81.7 %shard_map.186 = (f32[224,1152]{1,0:T(8,128)}, f32[224,896]{1,0:T(8,128)}, f32[8,896]{1,0:T(8,128)}, bf16[4,304,896]{2,1,0:T(8,128)(2,1)}, bf16[2,256,896]{2,1,0...) custom-call(bf16[896,2048]{1,0:T(8,128)(2,1)} %get-tuple-element.103.low_ref, ...), custom_call_target="tpu_custom_call" | custom-call | tf_op jit(solution)/shard_map/pallas_call | solution.py:116
  457.2 0.8 slice_select_fusion.1
  458.1 8.2 %shard_map.187 = f32[224,9728]{1,0:T(8,128)} custom-call(bf16[4,224,2432]{2,1,0:T(8,128)(2,1)} %bitcast.51), custom_call_target="tpu_custom_call" | custom-call | tf_op jit(solution)/shard_map/pallas_call | solution.py:1673
  466.4 2.3 bitcast_convert_fusion
  471.2 0.9 copy.39
  472.1 1.2 copy.40
  474.0 1.0 copy.41
  475.0 0.9 copy.42
  (91 shorter events, 10.0 us)
Async XLA Ops:
  7.2 94.3 %all-gather.6.cloned.1.call-start = ((), (), s32[]{:S(2)}) async-start(), calls=%async_computation.3 | async-start | bytes 2451456 | tf_op jit(solution)/shard_map/all_gather | solution.py:1777
  8.3 2.1 collective-permute-start.3
  13.2 88.3 %all-gather.4.cloned.1.call-start = ((), (), s32[]{:S(2)}) async-start(), calls=%async_computation.2 | async-start | bytes 4902912 | tf_op jit(solution)/shard_map/all_gather | solution.py:1777
  22.1 4.1 copy-start.10
  22.1 4.1 copy-start.12
  22.1 4.1 copy-start.13
  22.1 4.5 copy-start.1
  22.1 4.5 copy-start.3
  22.1 2.0 collective-permute-start.2
  25.3 1.7 copy-start.17
  25.3 145.3 %all-gather.8.cloned.1.call-start = ((), (), s32[]{:S(2)}) async-start(), calls=%async_computation.4 | async-start | bytes 4902912 | tf_op jit(solution)/shard_map/all_gather | solution.py:1777
  26.0 292.5 %reduce-scatter.3.cloned.1.call-start = ((), (), s32[]{:S(2)}) async-start(), calls=%async_computation.5 | async-start | bytes 4902912 | tf_op jit(solution)/shard_map/reduce_scatter | solution.py:1806
  26.2 5.6 %collective-permute-start.1 = (bf16[16,384]{1,0:T(8,128)(2,1)S(1)}, bf16[16,384]{1,0:T(8,128)(2,1)S(1)}, u32[]{:S(2)}, u32[]{:S(2)}) collective-permute-start(bf16[16,384]{1,0:T(8,128)(2,1)S(1)} %fusion.7), channel_id=1, source_target_pairs={{0,16},{16,0},{1,17},{17,1},{2,18},{18,2},{3,19},{19,3},{4,20},{20... | collective-permute-start | bytes 36872 | tf_op jit(solution)/shard_map/ppermute | solution.py:22
  26.7 5.7 %collective-permute-start = (bf16[224,2048]{1,0:T(8,128)(2,1)S(1)}, bf16[224,2048]{1,0:T(8,128)(2,1)S(1)}, u32[]{:S(2)}, u32[]{:S(2)}) collective-permute-start(bf16[224,2048]{1,0:T(8,128)(2,1)S(1)} %pad_maximum_fusion), channel_id=1, source_target_pairs={{0,16},{16,0},{1,17},{17,1},{2,18},{18,2},{3,19},{19,3},{4,20},{20... | collective-permute-start | bytes 2752520 | tf_op jit(solution)/shard_map/ppermute | solution.py:22
  27.0 7.1 %copy-start.8 = (s32[1,1,256]{2,1,0:T(1,128)}, s32[1,1,256]{2,1,0:T(1,128)S(1)}, u32[]{:S(2)}) copy-start(s32[1,1,256]{2,1,0:T(1,128)S(1)} %get-tuple-element.171) | copy-start | bytes 3076
  249.1 126.3 %reduce-scatter.5.cloned.1.call-start = ((), (), s32[]{:S(2)}) async-start(), calls=%async_computation.6 | async-start | bytes 4902912 | tf_op jit(solution)/shard_map/reduce_scatter | solution.py:1806
  318.6 0.7 copy-start.11
  318.6 0.7 copy-start.14
  318.6 0.7 copy-start.16
  319.3 45.8 %copy-start.15 = (f32[1,896]{1,0:T(1,128)S(1)}, f32[1,896]{1,0:T(1,128)}, u32[]{:S(2)}) copy-start(f32[1,896]{1,0:T(1,128)} %get-tuple-element.107) | copy-start | bytes 10756
  458.0 8.3 %copy-start.7 = (f32[4,896]{1,0:T(4,128)}, f32[4,896]{1,0:T(4,128)S(1)}, u32[]{:S(2)}) copy-start(f32[4,896]{1,0:T(4,128)S(1)} %slice_select_fusion.1) | copy-start | bytes 43012
  458.1 8.3 %copy-start.9 = (f32[3584]{0:T(1024)}, f32[3584]{0:T(1024)S(1)}, u32[]{:S(2)}) copy-start(f32[3584]{0:T(1024)S(1)} %reshape.106) | copy-start | bytes 43012
  458.1 8.2 %copy-start = (bf16[4,304,896]{2,1,0:T(8,128)(2,1)S(1)}, bf16[4,304,896]{2,1,0:T(8,128)(2,1)}, u32[]{:S(2)}) copy-start(bf16[4,304,896]{2,1,0:T(8,128)(2,1)} %get-tuple-element.123) | copy-start | bytes 6537220
  466.3 2.4 slice-start.1
  466.3 3.0 slice-start
  466.3 4.9 %copy-start.5 = (bf16[2,256,896]{2,1,0:T(8,128)(2,1)S(1)}, bf16[2,256,896]{2,1,0:T(8,128)(2,1)}, u32[]{:S(2)}) copy-start(bf16[2,256,896]{2,1,0:T(8,128)(2,1)} %get-tuple-element.117) | copy-start | bytes 2752516
  468.7 3.4 copy-start.2
  472.1 1.9 copy-start.4
  472.1 2.8 copy-start.6
Sparse Core Ops, SparseCore 0:
  13.3 33.6 all-gather.5
  49.3 50.4 all-gather.3
  102.0 49.1 all-gather.7
  249.3 58.0 reduce-scatter.2
  318.7 56.7 reduce-scatter.4

commit v8 on v7

--- a/solution.py
+++ b/solution.py
@@ -1250,6 +1250,30 @@
     def take(self, *which):
         for i in which:
             self.copies[i].wait()
+
+
+def units_kernel(ctx_count, fsdp_count, units, stride, expand_ref, out_ref):
+    ff_width = expand_ref.shape[1] // 2
+    rows = expand_ref.shape[0]
+    main = fsdp_count * stride // 128 * 128
+    size = fsdp_count * stride
+    for where in range(ctx_count):
+
+        @pl.when(lax.axis_index(CTX) == where)
+        def _():
+            sides = []
+            for side in range(2):
+                pieces = []
+                for shard in range(fsdp_count):
+                    start = side * ff_width + (shard * ctx_count + where) * units
+                    pieces.append(expand_ref[:, start : start + units])
+                    if stride > units:
+                        pieces.append(jnp.zeros((rows, stride - units), bf16))
+                sides.append(jnp.concatenate(pieces, axis=1))
+            out_ref[:, :main] = sides[0][:, :main]
+            out_ref[:, main : 2 * main] = sides[1][:, :main]
+            if size > main:
+                out_ref[:, 2 * main :] = jnp.concatenate([side[:, main:] for side in sides], axis=1)
 
 
 def gate_and_up(block, expand_ref, gate_start, up_start, size):
@@ -1738,24 +1762,14 @@
         other = swap_sections(array)
         return jnp.where(is_first, array, other), jnp.where(is_first, other, array)
 
-    def unit_columns(side):
-        pieces = []
-        for shard in range(fsdp_count):
-            start = side * ff_width + shard * shard_units
-            pieces.append(
-                pick(
-                    ctx,
-                    [
-                        expand_weight[0, :, start + k * units : start + (k + 1) * units]
-                        for k in range(ctx_count)
-                    ],
-                )
-            )
-            if spare_units:
-                pieces.append(jnp.zeros((shard_rows, spare_units), bf16))
-        return jnp.concatenate(pieces, axis=1)
-
-    expand_shard = pack_units(unit_columns(0), unit_columns(1))
+    stride = units + spare_units
+    expand_shard = pl.pallas_call(
+        functools.partial(units_kernel, ctx_count, fsdp_count, units, stride),
+        out_shape=jax.ShapeDtypeStruct((shard_rows, 2 * fsdp_count * stride), bf16),
+        in_specs=[pl.BlockSpec(memory_space=VMEM)],
+        out_specs=pl.BlockSpec(memory_space=VMEM),
+        compiler_params=pltpu.CompilerParams(vmem_limit_bytes=LIMIT),
+    )(expand_weight[0])
     down_shard = lax.dynamic_slice_in_dim(down_weight[0], ctx * units, units)
     down_shard = jnp.pad(down_shard, ((0, spare_units), (0, 0)))
 

time: 489 us -> 491 us (level)
  Pallas kernels: 420 us -> 429 us
  other arithmetic: 18.9 us -> 13.8 us
    select_n x2 -> x0, other arithmetic: 6.31 us -> none  [pick(): chosen = jnp.where(index == position, options[position], chosen)]
    pallas_call x10, Pallas kernels: 412 us -> 417 us  [call(): pl.pallas_call(kernel, out_shape=[jax.ShapeDtypeStruct(shape, kind) for s...]
  transfers between devices with their start and end apart: 9 -> 9, of which waited for: 3 -> 4; matrix products, arithmetic and copies ran while one was open for 4% -> 2% of each run, Pallas kernels for 52% -> 54%
where the time goes in v8:
time: 491 us; the launch traced here: 485 us
  Pallas kernels  429 us (87%)
  between operations  14.4 us (3%)
  waiting for transfers between devices  14 us (3%)
  other arithmetic  13.8 us (3%)
  local copies, waits for them, and re-layouts  12.4 us (3%)
    pallas_call x10, Pallas kernels, call(): pl.pallas_call(kernel, out_shape=[jax.ShapeDtypeStruct(shape, kind) for s...  417 us
  transfers between devices with their start and end apart: 9, of which 4 were waited for; matrix products, arithmetic and copies ran while one was open for 2% of the time, Pallas kernels for 54%

profile of v8, /device:TPU:0, one launch (start us, length us, event | category | flops | bytes accessed | tf_op | source)
XLA Modules:
  0.0 485.2 jit_solution(15607250998869499117)
XLA Ops:
  7.2 1.1 dynamic-slice_bitcast_fusion
  8.8 1.6 collective-permute-done.3
  10.4 2.0 broadcast_select_fusion.2
  12.4 0.7 slice_select_fusion
  13.3 3.6 shard_map.177
  16.8 1.4 broadcast_select_fusion.6
  18.7 1.6 collective-permute-done.2
  20.3 1.1 broadcast_select_fusion.4
  23.8 1.0 pad_maximum_fusion.1
  24.7 2.2 dynamic-slice_bitcast_fusion.1
  26.9 1.0 copy.29.refs_5_.refs_6_
  28.6 1.6 broadcast_select_fusion
  30.2 48.6 %shard_map.178 = (bf16[896,2048]{1,0:T(8,128)(2,1)}, bf16[896,2048]{1,0:T(8,128)(2,1)}, f32[8,1152]{1,0:T(8,128)}) custom-call(bf16[224,2048]{1,0:T(8,128)(2,1)} %get-tuple-element.67.low_ref, bf16[224,2048]{1,0:T(8,128)(2,1)} %get-tuple-element.68.high_ref, bf16[32,384]{1,0:T(8,128)(2,1)} %pad_maximum_fusion.4.small_ref), custom_call_target="tpu_custom_call" | custom-call | tf_op jit(solution)/shard_map/pallas_call | solution.py:116
  78.9 22.7 %shard_map.179 = (bf16[256,896]{1,0:T(8,128)(2,1)}, bf16[256,896]{1,0:T(8,128)(2,1)}, bf16[4,256,256]{2,1,0:T(8,128)(2,1)}, f32[16,256]{1,0:T(8,128)}, bf16[896,...) custom-call(bf16[256,896]{1,0:T(8,128)(2,1)} %get-tuple-element.169.refs_0_.refs_1_, ...), custom_call_target="tpu_custom_call" | custom-call | tf_op jit(solution)/shard_map/pallas_call | solution.py:116
  101.7 1.0 all-gather.4.cloned.1.call-done.expand_any.refs_6_
  102.7 40.2 %shard_map.180 = (bf16[256,896]{1,0:T(8,128)(2,1)}, bf16[4,256,896]{2,1,0:T(8,128)(2,1)}, bf16[4,256,1216]{2,1,0:T(8,128)(2,1)}, bf16[4,256,1216]{2,1,0:T(8,128)(2,1)}) custom-call(bf16[256,896]{1,0:T(8,128)(2,1)} %get-tuple-element.72.low_ref, f32[256,896]{1,0:T(8,128)} %get-tuple-element.73.mid_ref.refs_1_, ...), custom_call_target="tpu_custom_call" | custom-call | tf_op jit(solution)/shard_map/pallas_call | solution.py:116
  142.9 30.2 %shard_map.181 = (bf16[256,896]{1,0:T(8,128)(2,1)}, bf16[256,896]{1,0:T(8,128)(2,1)}, bf16[4,256,256]{2,1,0:T(8,128)(2,1)}, f32[16,256]{1,0:T(8,128)}, bf16[896,...) custom-call(bf16[256,896]{1,0:T(8,128)(2,1)} %get-tuple-element.74.refs_0_.refs_1_.a, ...), custom_call_target="tpu_custom_call" | custom-call | tf_op jit(solution)/shard_map/pallas_call | solution.py:116
  173.1 40.6 %shard_map.182 = (bf16[256,896]{1,0:T(8,128)(2,1)}, bf16[4,256,896]{2,1,0:T(8,128)(2,1)}, bf16[4,256,1216]{2,1,0:T(8,128)(2,1)}, bf16[4,256,1216]{2,1,0:T(8,128)(2,1)}) custom-call(bf16[256,896]{1,0:T(8,128)(2,1)} %get-tuple-element.77.low_ref, f32[256,896]{1,0:T(8,128)} %get-tuple-element.76.mid_ref.refs_1_, ...), custom_call_target="tpu_custom_call" | custom-call | tf_op jit(solution)/shard_map/pallas_call | solution.py:116
  213.7 38.0 %shard_map.183 = (f32[256,896]{1,0:T(8,128)}, f32[1,896]{1,0:T(1,128)}, bf16[896,2432]{1,0:T(8,128)(2,1)}, bf16[1216,896]{1,0:T(8,128)(2,1)}) custom-call(bf16[256,896]{1,0:T(8,128)(2,1)} %get-tuple-element.170.refs_0_, f32[256,896]{1,0:T(8,128)} %get-tuple-element.76.mid_ref.refs_1_, f32[8,1152]{1,0:T(8,128)} %get-tuple-element.70.refs_1_.refs_2_, ...), custom_call_target="tpu_custom_call" | custom-call | tf_op jit(solution)/shard_map/pallas_call | solution.py:116
  251.8 28.5 %shard_map.184 = (bf16[256,896]{1,0:T(8,128)(2,1)}, f32[1,896]{1,0:T(1,128)}, f32[1,1152]{1,0:T(1,128)}, bf16[896,2048]{1,0:T(8,128)(2,1)}) custom-call(f32[256,896]{1,0:T(8,128)} %get-tuple-element.82.refs_0_, bf16[256,896]{1,0:T(8,128)(2,1)} %get-tuple-element.74.refs_0_.refs_1_.act_zero_ref, f32[8,1152]{1,0:T(8,128)} %get-tuple-element.70.refs_1_.refs_2_, ...), custom_call_target="tpu_custom_call" | custom-call | tf_op jit(solution)/shard_map/pallas_call | solution.py:116
  280.3 40.8 %shard_map.185 = (f32[256,896]{1,0:T(8,128)}, f32[1,896]{1,0:T(1,128)}, bf16[896,2432]{1,0:T(8,128)(2,1)}, bf16[1216,896]{1,0:T(8,128)(2,1)}, bf16[304,896]{1,0:T(8,128)(2,1)}) custom-call(bf16[256,896]{1,0:T(8,128)(2,1)} %get-tuple-element.88.refs_0_.grad_one_ref, f32[256,896]{1,0:T(8,128)} %get-tuple-element.73.mid_ref.refs_1_, ...), custom_call_target="tpu_custom_call" | custom-call | tf_op jit(solution)/shard_map/pallas_call | solution.py:116
  321.9 45.7 %shard_map.186 = (f32[256,896]{1,0:T(8,128)}, f32[1,896]{1,0:T(1,128)}, f32[1,1152]{1,0:T(1,128)}, bf16[896,2048]{1,0:T(8,128)(2,1)}, bf16[896,256]{1,0:T(8,128)(2,1)}, /*index=5*/bf16[4,2,112,2432]{3,2,1,0:T(8,128)(2,1)}) custom-call(f32[256,896]{1,0:T(8,128)} %get-tuple-element.93.refs_0_, bf16[256,896]{1,0:T(8,128)(2,1)} %get-tuple-element.169.refs_0_.refs_1_, ...), custom_call_target="tpu_custom_call" | custom-call | tf_op jit(solution)/shard_map/pallas_call | solution.py:116
  367.7 0.7 maximum_reduce_fusion
  369.1 9.0 %reduce-scatter.5.cloned.1.call-done.expand_ref = bf16[112,2432]{1,0:T(8,128)(2,1)} async-done(((bf16[896,2432]{1,0:T(8,128)(2,1)}), bf16[112,2432]{1,0:T(8,128)(2,1)}) %reduce-scatter.5.cloned.1.call-update) | async-done | bytes 544784 | tf_op jit(solution)/shard_map/reduce_scatter | solution.py:1820
  378.1 81.7 %shard_map.187 = (f32[224,1152]{1,0:T(8,128)}, f32[224,896]{1,0:T(8,128)}, f32[8,896]{1,0:T(8,128)}, bf16[4,304,896]{2,1,0:T(8,128)(2,1)}, bf16[2,256,896]{2,1,0...) custom-call(bf16[896,2048]{1,0:T(8,128)(2,1)} %get-tuple-element.103.low_ref, ...), custom_call_target="tpu_custom_call" | custom-call | tf_op jit(solution)/shard_map/pallas_call | solution.py:116
  459.8 0.8 slice_select_fusion.1
  460.7 8.2 %shard_map.188 = f32[224,9728]{1,0:T(8,128)} custom-call(bf16[4,224,2432]{2,1,0:T(8,128)(2,1)} %bitcast.36), custom_call_target="tpu_custom_call" | custom-call | tf_op jit(solution)/shard_map/pallas_call | solution.py:1697
  469.0 2.3 bitcast_convert_fusion
  473.8 0.9 copy.39
  474.8 1.2 copy.40
  476.6 1.0 copy.41
  477.6 0.9 copy.42
  (85 shorter events, 8.7 us)
Async XLA Ops:
  7.2 94.5 %all-gather.6.cloned.1.call-start = ((), (), s32[]{:S(2)}) async-start(), calls=%async_computation.3 | async-start | bytes 2451456 | tf_op jit(solution)/shard_map/all_gather | solution.py:1791
  8.3 2.1 collective-permute-start.3
  13.2 89.5 %all-gather.4.cloned.1.call-start = ((), (), s32[]{:S(2)}) async-start(), calls=%async_computation.2 | async-start | bytes 4902912 | tf_op jit(solution)/shard_map/all_gather | solution.py:1791
  16.8 3.4 copy-start
  18.2 4.1 copy-start.11
  18.2 4.1 copy-start.13
  18.2 4.1 copy-start.14
  18.2 4.5 copy-start.2
  18.3 4.5 copy-start.4
  18.3 2.0 collective-permute-start.2
  21.4 1.7 copy-start.18
  21.4 151.7 %all-gather.8.cloned.1.call-start = ((), (), s32[]{:S(2)}) async-start(), calls=%async_computation.4 | async-start | bytes 4902912 | tf_op jit(solution)/shard_map/all_gather | solution.py:1791
  22.2 299.0 %reduce-scatter.3.cloned.1.call-start = ((), (), s32[]{:S(2)}) async-start(), calls=%async_computation.5 | async-start | bytes 4902912 | tf_op jit(solution)/shard_map/reduce_scatter | solution.py:1820
  22.4 5.6 %collective-permute-start.1 = (bf16[16,384]{1,0:T(8,128)(2,1)S(1)}, bf16[16,384]{1,0:T(8,128)(2,1)S(1)}, u32[]{:S(2)}, u32[]{:S(2)}) collective-permute-start(bf16[16,384]{1,0:T(8,128)(2,1)S(1)} %fusion.7), channel_id=1, source_target_pairs={{0,16},{16,0},{1,17},{17,1},{2,18},{18,2},{3,19},{19,3},{4,20},{20... | collective-permute-start | bytes 36872 | tf_op jit(solution)/shard_map/ppermute | solution.py:22
  22.9 5.7 %collective-permute-start = (bf16[224,2048]{1,0:T(8,128)(2,1)S(1)}, bf16[224,2048]{1,0:T(8,128)(2,1)S(1)}, u32[]{:S(2)}, u32[]{:S(2)}) collective-permute-start(bf16[224,2048]{1,0:T(8,128)(2,1)S(1)} %pad_maximum_fusion), channel_id=1, source_target_pairs={{0,16},{16,0},{1,17},{17,1},{2,18},{18,2},{3,19},{19,3},{4,20},{20... | collective-permute-start | bytes 2752520 | tf_op jit(solution)/shard_map/ppermute | solution.py:22
  23.2 7.1 %copy-start.9 = (s32[1,1,256]{2,1,0:T(1,128)}, s32[1,1,256]{2,1,0:T(1,128)S(1)}, u32[]{:S(2)}) copy-start(s32[1,1,256]{2,1,0:T(1,128)S(1)} %get-tuple-element.163) | copy-start | bytes 3076
  251.8 126.3 %reduce-scatter.5.cloned.1.call-start = ((), (), s32[]{:S(2)}) async-start(), calls=%async_computation.6 | async-start | bytes 4902912 | tf_op jit(solution)/shard_map/reduce_scatter | solution.py:1820
  321.2 0.7 copy-start.12
  321.2 0.7 copy-start.15
  321.2 0.7 copy-start.17
  321.9 45.8 %copy-start.16 = (f32[1,896]{1,0:T(1,128)S(1)}, f32[1,896]{1,0:T(1,128)}, u32[]{:S(2)}) copy-start(f32[1,896]{1,0:T(1,128)} %get-tuple-element.107) | copy-start | bytes 10756
  460.7 8.3 %copy-start.8 = (f32[4,896]{1,0:T(4,128)}, f32[4,896]{1,0:T(4,128)S(1)}, u32[]{:S(2)}) copy-start(f32[4,896]{1,0:T(4,128)S(1)} %slice_select_fusion.1) | copy-start | bytes 43012
  460.7 8.3 %copy-start.10 = (f32[3584]{0:T(1024)}, f32[3584]{0:T(1024)S(1)}, u32[]{:S(2)}) copy-start(f32[3584]{0:T(1024)S(1)} %reshape.58) | copy-start | bytes 43012
  460.7 8.2 %copy-start.1 = (bf16[4,304,896]{2,1,0:T(8,128)(2,1)S(1)}, bf16[4,304,896]{2,1,0:T(8,128)(2,1)}, u32[]{:S(2)}) copy-start(bf16[4,304,896]{2,1,0:T(8,128)(2,1)} %get-tuple-element.123) | copy-start | bytes 6537220
  468.9 2.4 slice-start.1
  469.0 3.0 slice-start
  469.0 4.9 %copy-start.6 = (bf16[2,256,896]{2,1,0:T(8,128)(2,1)S(1)}, bf16[2,256,896]{2,1,0:T(8,128)(2,1)}, u32[]{:S(2)}) copy-start(bf16[2,256,896]{2,1,0:T(8,128)(2,1)} %get-tuple-element.117) | copy-start | bytes 2752516
  471.3 3.4 copy-start.3
  474.8 1.9 copy-start.5
  474.8 2.8 copy-start.7
Sparse Core Ops, SparseCore 0:
  13.3 35.0 all-gather.5
  50.7 51.9 all-gather.3
  104.9 48.9 all-gather.7
  251.9 58.0 reduce-scatter.2
  321.3 56.7 reduce-scatter.4
